TPU v7x, 32 devices: a whole 2x2x4 slice. The times are simulated.
32 devices in a mesh: groups: 2 (over x), dp: 16 (over z, y, core).
Axes of the slice: x: 2, y: 2, z: 4, core: 2. Of those that a mesh axis runs over, the one named last changes fastest.
Arguments:
- images: bfloat16 [16, 128, 128, 320], P('groups', 'dp'), parts along dimension 0, may hold values from -6 to 6
- kernel_weights: bfloat16 [16, 2, 3, 3, 320, 320], P('dp'), may hold values from -0.109375 to 0.109375
- kernel_momentum: float32 [16, 2, 3, 3, 320, 320], P('dp'), may hold values from -0.12 to 0.12
- kernel_grads: bfloat16 [16, 2, 3, 3, 320, 320], P('dp'), may hold values from -0.119628906 to 0.119628906
- owners: int32 [2], replicated, may hold values from 0 to 15
Outputs:
- blocks_out: bfloat16 [16, 128, 128, 320], P('groups', 'dp'), parts along dimension 0
There are 2 independent parts, one for each index of `groups`. A program takes and returns all parts, laid end to end along the dimension named above; an argument that names none is the same for every part. Nothing has to cross between parts.
Inputs may be any that keep to these rules, and one draw needn't show every extreme that they name: `owners`: each entry is a slot index along the first dimension of the kernel state.
All inputs are finite; a program needn't handle non-finite values.
Results may differ from a plain program's by a relative error of at most 0.0095.
Values may be sent and summed in bfloat16 or wider, within the bound.
No kernel may reach another device: no remote copies, remote signals or barrier semaphores. Data moves between devices by JAX's collectives and lax.ppermute only.
A program may use at most 128 MiB of HBM per device.

v0:
```python
import jax
import jax.numpy as jnp
from jax import lax
from jax.sharding import PartitionSpec as P

momentum_decay = 0.9
learn_rate = 0.5


def from_root(x, axis, root):
    mine = lax.axis_index(axis) == root
    return lax.psum(jnp.where(mine, x, jnp.zeros_like(x)), axis)


def padded(cells, sides, width):
    for axis, dim in sides:
        count = lax.axis_size(axis)
        ends = count - 1
        head = lax.slice_in_dim(cells, 0, width, axis=dim)
        tail = lax.slice_in_dim(cells, cells.shape[dim] - width, cells.shape[dim], axis=dim)
        cells = jnp.concatenate(
            [
                lax.ppermute(tail, axis, [(i, (i + 1) % count) for i in range(ends)]),
                cells,
                lax.ppermute(head, axis, [((i + 1) % count, i) for i in range(ends)]),
            ],
            axis=dim,
        )
    return cells


def conv_rows(activated, kernel):
    return lax.conv_general_dilated(
        activated,
        kernel,
        (1, 1),
        ((0, 0), (1, 1)),
        dimension_numbers=("NHWC", "HWIO", "NHWC"),
        preferred_element_type=jnp.float32,
    )


def renew(kernel_weights, kernel_momentum, kernel_grads, owners, kernel_index):
    velocity = momentum_decay * kernel_momentum[0, kernel_index] + kernel_grads[
        0, kernel_index
    ].astype(jnp.float32)
    updated = (kernel_weights[0, kernel_index].astype(jnp.float32) - learn_rate * velocity).astype(
        jnp.bfloat16
    )
    return from_root(updated, "dp", owners[kernel_index])


def residual_conv(strip_field, kernel):
    activated = jax.nn.silu(strip_field.astype(jnp.float32)).astype(jnp.bfloat16)
    with_rims = padded(activated, (("dp", 1),), 1)
    branch = conv_rows(with_rims, kernel)
    return strip_field.astype(jnp.float32) + branch


def local(images, kernel_weights, kernel_momentum, kernel_grads, owners):
    first_kernel = renew(kernel_weights, kernel_momentum, kernel_grads, owners, 0)
    hidden = residual_conv(images, first_kernel).astype(jnp.bfloat16)
    second_kernel = renew(kernel_weights, kernel_momentum, kernel_grads, owners, 1)
    return residual_conv(hidden, second_kernel).astype(jnp.bfloat16)


def solution(mesh):
    placed = (
        P("groups", "dp", None, None),
        P("dp", None, None, None, None, None),
        P("dp", None, None, None, None, None),
        P("dp", None, None, None, None, None),
        P(),
    )
    return jax.shard_map(
        local, mesh=mesh, in_specs=placed, out_specs=P("groups", "dp", None, None), check_vma=False
    )
```

profile of v0, /device:TPU:1, one launch (start us, length us, event | category | flops | bytes accessed | tf_op | source)
XLA Modules:
  0.0 239.8 jit_solution(6173910143435806145)
XLA Ops:
  6.5 0.0 all-reduce.3.cloned.1.call-start
  6.5 1.3 fusion.34
  9.1 9.4 %fusion.29 = (bf16[3,3,320,320]{3,2,1,0:T(8,128)(2,1)}, bf16[3,3,320,320]{3,2,1,0:T(8,128)(2,1)}) fusion(f32[1,2,3,3,320,320]{5,4,3,2,1,0:T(8,128)} %param.7, bf16[1,2,3,3,320,320]{5,4,3,2,1,0:T(8,128)(2,1)} %param.8, bf16[1,2,3,3,320,320]{5,4,3,2,1,0:T(8,128)(2,1)} %param.6, pred[]{:T(512)S(6)} %eq.7, pred[]{:T(512)S(6)} %eq.6), kind=kLoop, calls=%fused_computation.33 | loop fusion | flops 14745600 | bytes 18432002 | tf_op jit(solution)/shard_map/jit(_where)/select_n | solution.py:12
  18.5 0.0 all-reduce.3.cloned.1.call-update
  18.5 8.6 %copy.8 = bf16[8,8,128,320]{3,0,2,1:T(8,128)(2,1)} copy(bf16[8,8,128,320]{2,3,1,0:T(8,128)(2,1)} %param.5) | data formatting | bytes 10485760 | tf_op args[0]
  27.1 5.5 %fusion.3 = bf16[8,8,128,320]{3,0,2,1:T(8,128)(2,1)S(1)} fusion(bf16[8,8,128,320]{3,0,2,1:T(8,128)(2,1)} %copy.8), kind=kLoop, calls=%fused_computation.9 | loop fusion | flops 15728640 | bytes 10485760 | tf_op jit(solution)/shard_map/convert_element_type | solution.py:54
  32.6 0.0 copy-start
  32.6 2.6 %copy-done = bf16[8,8,128,320]{3,0,2,1:T(8,128)(2,1)} copy-done((bf16[8,8,128,320]{3,0,2,1:T(8,128)(2,1)}, bf16[8,8,128,320]{3,0,2,1:T(8,128)(2,1)S(1)}, u32[]{:S(2)}) %copy-start) | copy-done | bytes 5242904
  35.2 0.2 fusion.33
  35.4 0.5 copy.10
  35.9 1.9 collective-permute-start.1
  37.9 0.5 copy.9
  38.4 4.9 %collective-permute-start = (bf16[8,1,128,320]{2,3,1,0:T(8,128)(2,1)S(1)}, bf16[8,1,128,320]{2,3,1,0:T(8,128)(2,1)S(1)}, u32[]{:S(2)}, u32[]{:S(2)}) collective-permute-start(bf16[8,1,128,320]{2,3,1,0:T(8,128)(2,1)S(1)} %copy.9), channel_id=1, source_target_pairs={{0,1},{1,2},{2,3},{3,4},{4,5},{5,6},{6,7},{7,8},{8,9},{9,10},{10,1... | collective-permute-start | bytes 1966088 | tf_op jit(solution)/shard_map/ppermute | solution.py:23
  43.3 8.5 %collective-permute-done.1 = bf16[8,1,128,320]{2,3,1,0:T(8,128)(2,1)S(1)} collective-permute-done((bf16[8,1,128,320]{2,3,1,0:T(8,128)(2,1)S(1)}, bf16[8,1,128,320]{2,3,1,0:T(8,128)(2,1)S(1)}, u32[]{:S(2)}, u32[]{:S(2)}) %collective-permute-start.1) | collective-permute-done | bytes 655392 | tf_op jit(solution)/shard_map/ppermute | solution.py:25
  51.8 0.5 copy.12
  52.3 1.9 collective-permute-done
  54.3 0.5 copy.11
  54.8 84.5 %all-reduce.3.cloned.1.call-done = (bf16[3,3,320,320]{3,2,1,0:T(8,128)(2,1)}, bf16[3,3,320,320]{3,2,1,0:T(8,128)(2,1)}) async-done(((bf16[3,3,320,320]{3,2,1,0:T(8,128)(2,1)}, bf16[3,3,320,320]{3,2,1,0:T(8,128)(2,1)}), (bf16[3,3,320,320]{3,2,1,0:T(8,128)(2,1)}, bf16[3,3,320,320]{3,2,1,0:T(8,128)(2,1)})) %all-reduce.3.cloned.1.call-update) | async-done | bytes 3686416 | tf_op jit(solution)/shard_map/psum | solution.py:12
  139.3 32.1 %fusion.8 = (bf16[8,8,128,320]{3,0,2,1:T(8,128)(2,1)S(1)}, bf16[8,8,128,320]{3,0,2,1:T(8,128)(2,1)}) fusion(bf16[3,3,320,320]{3,2,1,0:T(8,128)(2,1)} %get-tuple-element.5, bf16[8,1,128,320]{3,0,2,1:T(8,128)(2,1)S(1)} %copy.12, bf16[8,8,128,320]{3,0,2,1:T(8,128)(2,1)} %copy-done, bf16[8,1,128,320]{3,0,2,1:T(8,128)(2,1)S(1)} %copy.11, ...), kind=kOutput, calls=%fused_computation.14 | convolution fusion | flops 15064104960 | bytes 24125440 | tf_op jit(solution)/shard_map/conv_general_dilated | solution.py:33
  171.4 0.0 copy-start.1
  171.4 0.2 fusion.32
  171.5 2.5 %copy-done.1 = bf16[8,8,128,320]{3,0,2,1:T(8,128)(2,1)} copy-done((bf16[8,8,128,320]{3,0,2,1:T(8,128)(2,1)}, bf16[8,8,128,320]{3,0,2,1:T(8,128)(2,1)S(1)}, u32[]{:S(2)}) %copy-start.1) | copy-done | bytes 5242904
  174.0 0.5 copy.14
  174.5 3.9 %collective-permute-start.3 = (bf16[8,1,128,320]{2,3,1,0:T(8,128)(2,1)S(1)}, bf16[8,1,128,320]{2,3,1,0:T(8,128)(2,1)S(1)}, u32[]{:S(2)}, u32[]{:S(2)}) collective-permute-start(bf16[8,1,128,320]{2,3,1,0:T(8,128)(2,1)S(1)} %copy.14), channel_id=1, source_target_pairs={{1,0},{2,1},{3,2},{4,3},{5,4},{6,5},{7,6},{8,7},{9,8},{10,9},{11,1... | collective-permute-start | bytes 1966088 | tf_op jit(solution)/shard_map/ppermute | solution.py:25
  178.4 0.5 copy.13
  178.9 3.0 %collective-permute-start.2 = (bf16[8,1,128,320]{2,3,1,0:T(8,128)(2,1)S(1)}, bf16[8,1,128,320]{2,3,1,0:T(8,128)(2,1)S(1)}, u32[]{:S(2)}, u32[]{:S(2)}) collective-permute-start(bf16[8,1,128,320]{2,3,1,0:T(8,128)(2,1)S(1)} %copy.13), channel_id=1, source_target_pairs={{0,1},{1,2},{2,3},{3,4},{4,5},{5,6},{6,7},{7,8},{8,9},{9,10},{10,1... | collective-permute-start | bytes 1966088 | tf_op jit(solution)/shard_map/ppermute | solution.py:23
  181.9 5.6 %collective-permute-done.3 = bf16[8,1,128,320]{2,3,1,0:T(8,128)(2,1)S(1)} collective-permute-done((bf16[8,1,128,320]{2,3,1,0:T(8,128)(2,1)S(1)}, bf16[8,1,128,320]{2,3,1,0:T(8,128)(2,1)S(1)}, u32[]{:S(2)}, u32[]{:S(2)}) %collective-permute-start.3) | collective-permute-done | bytes 655392 | tf_op jit(solution)/shard_map/ppermute | solution.py:25
  187.5 0.5 copy.16
  188.1 5.7 %collective-permute-done.2 = bf16[8,1,128,320]{2,3,1,0:T(8,128)(2,1)S(1)} collective-permute-done((bf16[8,1,128,320]{2,3,1,0:T(8,128)(2,1)S(1)}, bf16[8,1,128,320]{2,3,1,0:T(8,128)(2,1)S(1)}, u32[]{:S(2)}, u32[]{:S(2)}) %collective-permute-start.2) | collective-permute-done | bytes 655392 | tf_op jit(solution)/shard_map/ppermute | solution.py:23
  193.8 0.5 copy.15
  194.3 30.2 %fusion.9 = bf16[8,8,128,320]{3,0,2,1:T(8,128)(2,1)} fusion(bf16[8,8,128,320]{3,0,2,1:T(8,128)(2,1)} %get-tuple-element.16, bf16[3,3,320,320]{3,2,1,0:T(8,128)(2,1)} %get-tuple-element.6, bf16[8,1,128,320]{3,0,2,1:T(8,128)(2,1)S(1)} %copy.16, bf16[8,8,128,320]{3,0,2,1:T(8,128)(2,1)} %copy-done.1, bf16[8,1,128,320]{3,0,2,1:T(8,128)(2,1)S(1)} %copy.15), kind=kOutput, calls=%fused_computation.15 | convolution fusion | flops 15048376320 | bytes 18882560 | tf_op jit(solution)/shard_map/conv_general_dilated | solution.py:33
  224.4 8.5 %copy.17 = bf16[8,8,128,320]{2,3,1,0:T(8,128)(2,1)} copy(bf16[8,8,128,320]{3,0,2,1:T(8,128)(2,1)} %fusion.9) | data formatting | bytes 10485760 | tf_op jit(solution)/shard_map/convert_element_type | solution.py:64
Async XLA Ops:
  6.5 132.8 %all-reduce.3.cloned.1.call-start = ((), (), s32[]{:S(2)}) async-start(), calls=%async_computation | async-start | bytes 8847360 | tf_op jit(solution)/shard_map/psum | solution.py:12
  32.6 2.6 %copy-start = (bf16[8,8,128,320]{3,0,2,1:T(8,128)(2,1)}, bf16[8,8,128,320]{3,0,2,1:T(8,128)(2,1)S(1)}, u32[]{:S(2)}) copy-start(bf16[8,8,128,320]{3,0,2,1:T(8,128)(2,1)S(1)} %fusion.3) | copy-start | bytes 15728644
  35.9 15.8 %collective-permute-start.1 = (bf16[8,1,128,320]{2,3,1,0:T(8,128)(2,1)S(1)}, bf16[8,1,128,320]{2,3,1,0:T(8,128)(2,1)S(1)}, u32[]{:S(2)}, u32[]{:S(2)}) collective-permute-start(bf16[8,1,128,320]{2,3,1,0:T(8,128)(2,1)S(1)} %copy.10), channel_id=1, source_target_pairs={{1,0},{2,1},{3,2},{4,3},{5,4},{6,5},{7,6},{8,7},{9,8},{10,9},{11,1... | collective-permute-start | bytes 1966088 | tf_op jit(solution)/shard_map/ppermute | solution.py:25
  38.4 15.9 %collective-permute-start = (bf16[8,1,128,320]{2,3,1,0:T(8,128)(2,1)S(1)}, bf16[8,1,128,320]{2,3,1,0:T(8,128)(2,1)S(1)}, u32[]{:S(2)}, u32[]{:S(2)}) collective-permute-start(bf16[8,1,128,320]{2,3,1,0:T(8,128)(2,1)S(1)} %copy.9), channel_id=1, source_target_pairs={{0,1},{1,2},{2,3},{3,4},{4,5},{5,6},{6,7},{7,8},{8,9},{9,10},{10,1... | collective-permute-start | bytes 1966088 | tf_op jit(solution)/shard_map/ppermute | solution.py:23
  171.4 2.6 %copy-start.1 = (bf16[8,8,128,320]{3,0,2,1:T(8,128)(2,1)}, bf16[8,8,128,320]{3,0,2,1:T(8,128)(2,1)S(1)}, u32[]{:S(2)}) copy-start(bf16[8,8,128,320]{3,0,2,1:T(8,128)(2,1)S(1)} %get-tuple-element.15) | copy-start | bytes 15728644
  174.5 13.0 %collective-permute-start.3 = (bf16[8,1,128,320]{2,3,1,0:T(8,128)(2,1)S(1)}, bf16[8,1,128,320]{2,3,1,0:T(8,128)(2,1)S(1)}, u32[]{:S(2)}, u32[]{:S(2)}) collective-permute-start(bf16[8,1,128,320]{2,3,1,0:T(8,128)(2,1)S(1)} %copy.14), channel_id=1, source_target_pairs={{1,0},{2,1},{3,2},{4,3},{5,4},{6,5},{7,6},{8,7},{9,8},{10,9},{11,1... | collective-permute-start | bytes 1966088 | tf_op jit(solution)/shard_map/ppermute | solution.py:25
  178.9 14.8 %collective-permute-start.2 = (bf16[8,1,128,320]{2,3,1,0:T(8,128)(2,1)S(1)}, bf16[8,1,128,320]{2,3,1,0:T(8,128)(2,1)S(1)}, u32[]{:S(2)}, u32[]{:S(2)}) collective-permute-start(bf16[8,1,128,320]{2,3,1,0:T(8,128)(2,1)S(1)} %copy.13), channel_id=1, source_target_pairs={{0,1},{1,2},{2,3},{3,4},{4,5},{5,6},{6,7},{7,8},{8,9},{9,10},{10,1... | collective-permute-start | bytes 1966088 | tf_op jit(solution)/shard_map/ppermute | solution.py:23
Sparse Core Ops, SparseCore 0:
  18.6 120.6 all-reduce.2
where the time goes:
time: 241 us; the launch traced here: 240 us
  waiting for transfers between devices  106 us (44%)
  matrix products  62.2 us (26%)
  local copies, waits for them, and re-layouts  28.2 us (12%)
  other arithmetic  14.8 us (6%)
  between operations  14.7 us (6%)
  starting transfers between devices  13.6 us (6%)
    psum x1, waiting for transfers between devices, from_root(): return lax.psum(jnp.where(mine, x, jnp.zeros_like(x)), axis)  84.5 us
    conv_general_dilated x2, matrix products, conv_rows(): lax.conv_general_dilated(activated, kernel, (1, 1), ((0, 0), (1, 1)), dim...  62.2 us
    ppermute x2, waiting for transfers between devices, padded(): lax.ppermute(head, axis, [((i + 1) % count, i) for i in range(ends)])  14.1 us
    unnamed x5, local copies, waits for them, and re-layouts  13.8 us
    select_n x1, other arithmetic, from_root(): return lax.psum(jnp.where(mine, x, jnp.zeros_like(x)), axis)  9.39 us
    convert_element_type x1, local copies, waits for them, and re-layouts, local(): return residual_conv(hidden, second_kernel).astype(jnp.bfloat16)  8.51 us
    ppermute x2, starting transfers between devices, padded(): lax.ppermute(tail, axis, [(i, (i + 1) % count) for i in range(ends)])  7.86 us
    ppermute x2, waiting for transfers between devices, padded(): lax.ppermute(tail, axis, [(i, (i + 1) % count) for i in range(ends)])  7.65 us
  transfers between devices with their start and end apart: 5, of which 5 were waited for; matrix products, arithmetic and copies ran while one was open for 7% of the time, Pallas kernels for 0%

commit v1 on v0

v1 whole, which is shorter than its diff:
```python
import functools

import jax
import jax.numpy as jnp
from jax import lax
from jax.experimental import pallas as pl
from jax.experimental.pallas import tpu as pltpu
from jax.sharding import PartitionSpec as P

momentum_decay = 0.9
learn_rate = 0.5
axes = ("groups", "dp")
lanes = 128


def silu(v):
    half = v.astype(jnp.float32) * 0.5
    return (half * jnp.tanh(half) + half).astype(jnp.bfloat16)


def update_body(place, w_ref, m_ref, g_ref, mine0, mine1, theirs0, theirs1, *, depth):
    core = place[2]
    step = pl.program_id(0)
    first = (2 * place[0] + lax.bitwise_xor(place[1], step)) * 2 * lanes
    for row in range(w_ref.shape[1]):
        velocity = momentum_decay * m_ref[0, row] + g_ref[0, row].astype(jnp.float32)
        fresh = w_ref[0, row].astype(jnp.float32) - learn_rate * velocity
        at = first + lax.broadcasted_iota(jnp.int32, fresh.shape, 0)
        fresh = jnp.where(at < depth, fresh, 0.0)
        flipped = fresh.T.astype(jnp.bfloat16)
        low, high = flipped[:, :lanes], flipped[:, lanes:]
        own = jnp.where(core == 0, low, high)
        other = jnp.where(core == 0, high, low)

        @pl.when(step == 0)
        def _():
            mine0[row] = own
            theirs0[row] = other

        @pl.when(step == 1)
        def _():
            mine1[row] = own
            theirs1[row] = other


def update(place, weights, momentum, grads, which):
    taps, depth, outs = weights.shape[1:]
    block = pl.BlockSpec(
        (1, taps, 2 * lanes, outs),
        lambda i, place: (which, 0, 2 * place[0] + lax.bitwise_xor(place[1], i), 0),
    )
    piece = pl.BlockSpec((taps, outs, lanes), lambda i, place: (0, 0, 0))
    return pl.pallas_call(
        functools.partial(update_body, depth=depth),
        grid_spec=pltpu.PrefetchScalarGridSpec(
            num_scalar_prefetch=1, grid=(2,), in_specs=[block] * 3, out_specs=[piece] * 4
        ),
        out_shape=[jax.ShapeDtypeStruct((taps, outs, lanes), jnp.bfloat16)] * 4,
        compiler_params=pltpu.CompilerParams(vmem_limit_bytes=40 * 2**20),
        name="kernel_update",
    )(place, weights, momentum, grads)


def swap(x, groups, count, change):
    pairs = []
    for g in range(groups):
        for d in range(count):
            to_g, to_d = change(g, d)
            pairs.append((g * count + d, to_g * count + to_d))
    return lax.ppermute(x, axes, pairs)


def spread(pieces, owner, groups, count):
    dp = lax.axis_index("dp")
    differs = lax.bitwise_xor(dp, owner)
    mine0, mine1, theirs0, theirs1 = pieces

    def swap_dp(x, bit):
        return swap(x, groups, count, lambda g, d: (g, d ^ bit))

    def keep(bit, own, got):
        return jnp.where(lax.bitwise_and(differs, bit) == 0, own, got)

    got1 = swap_dp(theirs1, 1)
    got0 = swap_dp(theirs0, 1)
    far = keep(1, mine1, got1)
    near = keep(1, mine0, got0)
    piece = keep(2, near, swap_dp(far, 2))
    bit = count // 2
    while bit >= 4:
        piece = keep(bit, piece, swap_dp(piece, bit))
        bit //= 2
    ring = [
        piece,
        swap_dp(piece, 2),
        swap(piece, groups, count, lambda g, d: (g ^ 1, d)),
        swap(piece, groups, count, lambda g, d: (g ^ 1, d ^ 2)),
    ]
    return ring + [swap_dp(x, 1) for x in ring]


def conv_body(place, x_ref, up_ref, down_ref, *rest):
    piece_refs, (out_ref, top_ref, bottom_ref, mixed, shifted) = rest[:8], rest[8:]
    n, rows, chans, cols = x_ref.shape
    depth = 3 * chans

    @pl.when(pl.program_id(0) == 0)
    def _():
        for relation, ref in enumerate(piece_refs):
            tile = (
                4 * lax.bitwise_xor(place[0], (relation >> 1) & 1)
                + 2 * lax.bitwise_xor(place[1], relation & 1)
                + lax.bitwise_xor(place[2], relation >> 2)
            )
            at = pl.ds(pl.multiple_of(tile * lanes, lanes), lanes)
            outer = (ref[0].astype(jnp.float32) + ref[2].astype(jnp.float32)) * 0.5
            inner = ref[1].astype(jnp.float32) * 0.5
            mixed[0, :, at] = ref[0]
            mixed[1, :, at] = (outer + inner).astype(jnp.bfloat16)
            mixed[2, :, at] = (outer - inner).astype(jnp.bfloat16)
            mixed[3, :, at] = ref[2]

    def put(row):
        for i in range(n):
            raw = up_ref[i] if row == 0 else down_ref[i] if row == rows + 1 else x_ref[i, row - 1]
            act = silu(raw)
            lane = lax.broadcasted_iota(jnp.int32, act.shape, 1)
            zero = jnp.zeros_like(act)
            at = pl.ds(i * cols, cols)
            shifted[row, 0:chans, at] = jnp.where(lane == 0, zero, pltpu.roll(act, 1, 1))
            shifted[row, chans : 2 * chans, at] = act
            shifted[row, 2 * chans : depth, at] = jnp.where(
                lane == cols - 1, zero, pltpu.roll(act, cols - 1, 1)
            )

    def product(t, field):
        return jnp.dot(mixed[t, :, 0:depth], field, preferred_element_type=jnp.float32)

    def emit(row, i, branch):
        result = (x_ref[i, row].astype(jnp.float32) + branch).astype(out_ref.dtype)
        out_ref[i, row] = result
        if row == 0:
            top_ref[i] = result
        if row == rows - 1:
            bottom_ref[i] = result

    for row in range(4):
        put(row)
    for block in range(rows // 2):
        if block + 1 < rows // 2:
            put(2 * block + 4)
            put(2 * block + 5)
        d = [shifted.at[2 * block + j] for j in range(4)]
        plus = product(1, d[1][...] + d[2][...])
        minus = product(2, d[2][...] - d[1][...])
        even = plus + minus + product(0, d[0][...] - d[2][...])
        odd = plus - minus - product(3, d[1][...] - d[3][...])
        for i in range(n):
            at = slice(i * cols, (i + 1) * cols)
            emit(2 * block, i, even[:, at])
            emit(2 * block + 1, i, odd[:, at])


def residual_conv(place, field, up, down, pieces):
    images, rows, chans, cols = field.shape
    n = 2
    strip = pl.BlockSpec((n, rows, chans, cols), lambda i, place: (i, 0, 0, 0))
    edge = pl.BlockSpec((n, chans, cols), lambda i, place: (i, 0, 0))
    piece = pl.BlockSpec(pieces[0].shape, lambda i, place: (0, 0, 0))
    return pl.pallas_call(
        conv_body,
        grid_spec=pltpu.PrefetchScalarGridSpec(
            num_scalar_prefetch=1,
            grid=(images // n,),
            in_specs=[strip, edge, edge] + [piece] * 8,
            out_specs=[strip, edge, edge],
            scratch_shapes=[
                pltpu.VMEM((4, chans, 8 * lanes), jnp.bfloat16),
                pltpu.VMEM((rows + 2, 3 * chans, n * cols), jnp.bfloat16),
            ],
        ),
        out_shape=[
            jax.ShapeDtypeStruct(field.shape, field.dtype),
            jax.ShapeDtypeStruct(up.shape, field.dtype),
            jax.ShapeDtypeStruct(up.shape, field.dtype),
        ],
        compiler_params=pltpu.CompilerParams(vmem_limit_bytes=40 * 2**20),
        cost_estimate=pl.CostEstimate(
            flops=2 * images * rows * cols * 9 * chans * chans,
            bytes_accessed=4 * images * rows * cols * chans,
            transcendentals=images * rows * cols * chans,
        ),
        name="residual_conv",
    )(place, field, up, down, *pieces)


def borders(top, bottom, count):
    up = lax.ppermute(bottom, "dp", [(i, i + 1) for i in range(count - 1)])
    down = lax.ppermute(top, "dp", [(i + 1, i) for i in range(count - 1)])
    return up, down


def local(groups, count, images, kernel_weights, kernel_momentum, kernel_grads, owners):
    g, dp = lax.axis_index("groups"), lax.axis_index("dp")
    place = jnp.stack([g % 2, (dp // 2) % 2, dp % 2]).astype(jnp.int32)

    def flat(x):
        _, kernels, taps, across, ins, outs = x.shape
        return x.reshape(kernels, taps, across * ins, outs)

    state = [flat(x) for x in (kernel_weights, kernel_momentum, kernel_grads)]
    first = spread(update(place, *state, 0), owners[0], groups, count)
    second = spread(update(place, *state, 1), owners[1], groups, count)
    field = jnp.swapaxes(images, 2, 3)
    up, down = borders(field[:, 0], field[:, -1], count)
    hidden, top, bottom = residual_conv(place, field, up, down, first)
    up, down = borders(top, bottom, count)
    result = residual_conv(place, hidden, up, down, second)[0]
    return jnp.swapaxes(result, 2, 3)


def solution(mesh):
    groups, count = mesh.shape["groups"], mesh.shape["dp"]
    assert groups % 2 == 0 and count % 4 == 0 and count & (count - 1) == 0
    state = P("dp", None, None, None, None, None)
    return jax.shard_map(
        functools.partial(local, groups, count),
        mesh=mesh,
        in_specs=(P("groups", "dp", None, None), state, state, state, P()),
        out_specs=P("groups", "dp", None, None),
        check_vma=False,
    )
```

time: 241 us -> 144 us (0.60)
  the two profiles are of different devices: /device:TPU:1 before, /device:TPU:9 now
where the time goes in v1:
time: 144 us; the launch traced here: 143 us
  starting transfers between devices  52.9 us (37%)
  Pallas kernels  40.5 us (28%)
  waiting for transfers between devices  36.5 us (25%)
  local copies, waits for them, and re-layouts  9.01 us (6%)
  other arithmetic  2.89 us (2%)
  between operations  1.52 us (1%)
    ppermute x24, waiting for transfers between devices, swap(): return lax.ppermute(x, axes, pairs)  36.4 us
    ppermute x24, starting transfers between devices, swap(): return lax.ppermute(x, axes, pairs)  36.2 us
    pallas_call x2, Pallas kernels, residual_conv(): pl.pallas_call(conv_body, grid_spec=pltpu.PrefetchScalarGridSpec(num_scal...  34.2 us
    ppermute x2, starting transfers between devices, borders(): up = lax.ppermute(bottom, 'dp', [(i, i + 1) for i in range(count - 1)])  11.5 us
    unnamed x7, local copies, waits for them, and re-layouts  7.45 us
    pallas_call x2, Pallas kernels, update(): pl.pallas_call(functools.partial(update_body, depth=depth), grid_spec=plt...  6.27 us
    ppermute x2, starting transfers between devices, borders(): down = lax.ppermute(top, 'dp', [(i + 1, i) for i in range(count - 1)])  5.19 us
  transfers between devices with their start and end apart: 28, of which 10 were waited for; matrix products, arithmetic and copies ran while one was open for 5% of the time, Pallas kernels for 14%

profile of v1, /device:TPU:9, one launch (start us, length us, event | category | flops | bytes accessed | tf_op | source)
XLA Modules:
  0.0 143.3 jit_solution(8918129633049662656)
XLA Ops:
  0.0 0.1 pad_add_fusion.place
  0.1 2.3 %copy-done = bf16[1,2,3,3,320,320]{5,4,3,2,1,0:T(8,128)(2,1)S(1)} copy-done((bf16[1,2,3,3,320,320]{5,4,3,2,1,0:T(8,128)(2,1)S(1)}, bf16[1,2,3,3,320,320]{5,4,3,2,1,0:T(8,128)(2,1)}, u32[]{:S(2)}) %copy-start) | copy-done | bytes 3686424
  2.3 2.3 %copy-done.1 = bf16[1,2,3,3,320,320]{5,4,3,2,1,0:T(8,128)(2,1)S(1)} copy-done((bf16[1,2,3,3,320,320]{5,4,3,2,1,0:T(8,128)(2,1)S(1)}, bf16[1,2,3,3,320,320]{5,4,3,2,1,0:T(8,128)(2,1)}, u32[]{:S(2)}) %copy-start.1) | copy-done | bytes 3686424
  4.6 3.1 %kernel_update.2 = (bf16[3,320,128]{2,1,0:T(8,128)(2,1)S(1)}, bf16[3,320,128]{2,1,0:T(8,128)(2,1)S(1)}, bf16[3,320,128]{2,1,0:T(8,128)(2,1)S(1)}, bf16[3,320,128]{2,1,0:T(8,128)(2,1)S(1)}) custom-call(s32[3]{0:T(128)S(1)} %pad_add_fusion.place, bf16[2,3,960,320]{3,2,1,0:T(8,128)(2,1)S(1)} %bitcast.17, f32[2,3,960,320]{3,2,1,0:T(8,128)} %bitcast.21, ...), custom_call_target="tpu_custom_call" | custom-call | tf_op jit(solution)/shard_map/kernel_update/pallas_call | solution.py:53
  7.7 0.0 copy-start.2
  7.7 0.7 collective-permute-start.3
  8.5 3.1 %kernel_update.3 = (bf16[3,320,128]{2,1,0:T(8,128)(2,1)S(1)}, bf16[3,320,128]{2,1,0:T(8,128)(2,1)S(1)}, bf16[3,320,128]{2,1,0:T(8,128)(2,1)S(1)}, bf16[3,320,128]{2,1,0:T(8,128)(2,1)S(1)}) custom-call(s32[3]{0:T(128)S(1)} %pad_add_fusion.place, bf16[2,3,960,320]{3,2,1,0:T(8,128)(2,1)S(1)} %bitcast.18, f32[2,3,960,320]{3,2,1,0:T(8,128)} %bitcast.22, ...), custom_call_target="tpu_custom_call" | custom-call | tf_op jit(solution)/shard_map/kernel_update/pallas_call | solution.py:53
  11.6 0.1 collective-permute-start.16
  11.7 0.5 collective-permute-start.17
  12.2 0.1 collective-permute-start.2
  12.3 0.6 fusion
  13.6 2.9 %copy.10 = bf16[8,8,128,320]{2,3,0,1:T(8,128)(2,1)S(1)} copy(bf16[8,8,128,320]{2,3,1,0:T(8,128)(2,1)} %param.5) | data formatting | bytes 10485760 | tf_op args[0]
  16.5 0.0 collective-permute-done.3
  16.5 0.7 broadcast_select_fusion.3
  17.3 1.2 collective-permute-start.4
  18.5 0.9 slice_bitcast_fusion
  19.4 2.6 %collective-permute-start.1 = (bf16[8,320,128]{2,1,0:T(8,128)(2,1)S(1)}, bf16[8,320,128]{2,1,0:T(8,128)(2,1)S(1)}, u32[]{:S(2)}, u32[]{:S(2)}) collective-permute-start(bf16[8,320,128]{2,1,0:T(8,128)(2,1)S(1)} %get-tuple-element.29), channel_id=1, source_target_pairs={{1,0},{2,1},{3,2},{4,3},{5,4},{6,5},{7,6},{8,7},{9,8},{10,9},{11,1... | collective-permute-start | bytes 1966088 | tf_op jit(solution)/shard_map/ppermute | solution.py:199
  22.7 0.0 collective-permute-done.17
  22.7 0.3 collective-permute-start.18
  23.0 0.0 collective-permute-done.2
  23.0 1.6 %collective-permute-done.4 = bf16[3,320,128]{2,1,0:T(8,128)(2,1)} collective-permute-done((bf16[3,320,128]{2,1,0:T(8,128)(2,1)}, bf16[3,320,128]{2,1,0:T(8,128)(2,1)}, u32[]{:S(2)}, u32[]{:S(2)}) %collective-permute-start.4) | collective-permute-done | bytes 245792 | tf_op jit(solution)/shard_map/ppermute | solution.py:70
  24.7 1.0 select_select_fusion.1
  25.7 2.4 %collective-permute-start.5 = (bf16[3,320,128]{2,1,0:T(8,128)(2,1)S(1)}, bf16[3,320,128]{2,1,0:T(8,128)(2,1)S(1)}, u32[]{:S(2)}, u32[]{:S(2)}) collective-permute-start(bf16[3,320,128]{2,1,0:T(8,128)(2,1)S(1)} %select_select_fusion.1), channel_id=1, source_target_pairs={{0,8},{1,9},{2,10},{3,11},{4,12},{5,13},{6,14},{7,15},{8,0},{9,1},... | collective-permute-start | bytes 737288 | tf_op jit(solution)/shard_map/ppermute | solution.py:70
  28.0 6.5 %collective-permute-done.18 = bf16[3,320,128]{2,1,0:T(8,128)(2,1)S(1)} collective-permute-done((bf16[3,320,128]{2,1,0:T(8,128)(2,1)S(1)}, bf16[3,320,128]{2,1,0:T(8,128)(2,1)S(1)}, u32[]{:S(2)}, u32[]{:S(2)}) %collective-permute-start.18) | collective-permute-done | bytes 245792 | tf_op jit(solution)/shard_map/ppermute | solution.py:70
  34.6 0.1 collective-permute-start.19
  34.6 3.3 %collective-permute-done.5 = bf16[3,320,128]{2,1,0:T(8,128)(2,1)S(1)} collective-permute-done((bf16[3,320,128]{2,1,0:T(8,128)(2,1)S(1)}, bf16[3,320,128]{2,1,0:T(8,128)(2,1)S(1)}, u32[]{:S(2)}, u32[]{:S(2)}) %collective-permute-start.5) | collective-permute-done | bytes 245792 | tf_op jit(solution)/shard_map/ppermute | solution.py:70
  38.0 4.7 %collective-permute-start.6 = (bf16[3,320,128]{2,1,0:T(8,128)(2,1)S(1)}, bf16[3,320,128]{2,1,0:T(8,128)(2,1)S(1)}, u32[]{:S(2)}, u32[]{:S(2)}) collective-permute-start(bf16[3,320,128]{2,1,0:T(8,128)(2,1)S(1)} %broadcast_select_fusion.4), channel_id=1, source_target_pairs={{0,4},{1,5},{2,6},{3,7},{4,0},{5,1},{6,2},{7,3},{8,12},{9,13},{10,... | collective-permute-start | bytes 737288 | tf_op jit(solution)/shard_map/ppermute | solution.py:70
  42.6 9.6 %collective-permute-start = (bf16[8,320,128]{2,1,0:T(8,128)(2,1)}, bf16[8,320,128]{2,1,0:T(8,128)(2,1)S(1)}, u32[]{:S(2)}, u32[]{:S(2)}) collective-permute-start(bf16[8,320,128]{2,1,0:T(8,128)(2,1)} %get-tuple-element.30), channel_id=1, source_target_pairs={{0,1},{1,2},{2,3},{3,4},{4,5},{5,6},{6,7},{7,8},{8,9},{9,10},{10,1... | collective-permute-start | bytes 1966088 | tf_op jit(solution)/shard_map/ppermute | solution.py:198
  52.3 0.1 collective-permute-start.20
  52.3 0.8 collective-permute-done.6
  53.1 4.5 %collective-permute-start.9 = (bf16[3,320,128]{2,1,0:T(8,128)(2,1)S(1)}, bf16[3,320,128]{2,1,0:T(8,128)(2,1)S(1)}, u32[]{:S(2)}, u32[]{:S(2)}) collective-permute-start(bf16[3,320,128]{2,1,0:T(8,128)(2,1)S(1)} %broadcast_select_fusion.5.rest_0_), channel_id=1, source_target_pairs={{0,18},{1,19},{2,16},{3,17},{4,22},{5,23},{6,20},{7,21},{8,26},{9,... | collective-permute-start | bytes 737288 | tf_op jit(solution)/shard_map/ppermute | solution.py:70
  57.7 0.5 collective-permute-start.8
  58.1 0.0 collective-permute-done.1.down_ref
  58.1 0.0 collective-permute-start.7
  58.1 1.8 %collective-permute-done.20 = bf16[3,320,128]{2,1,0:T(8,128)(2,1)} collective-permute-done((bf16[3,320,128]{2,1,0:T(8,128)(2,1)S(1)}, bf16[3,320,128]{2,1,0:T(8,128)(2,1)}, u32[]{:S(2)}, u32[]{:S(2)}) %collective-permute-start.20) | collective-permute-done | bytes 245792 | tf_op jit(solution)/shard_map/ppermute | solution.py:70
  60.0 2.3 %collective-permute-start.10 = (bf16[3,320,128]{2,1,0:T(8,128)(2,1)S(1)}, bf16[3,320,128]{2,1,0:T(8,128)(2,1)S(1)}, u32[]{:S(2)}, u32[]{:S(2)}) collective-permute-start(bf16[3,320,128]{2,1,0:T(8,128)(2,1)S(1)} %broadcast_select_fusion.5.rest_0_), channel_id=1, source_target_pairs={{0,1},{1,0},{2,3},{3,2},{4,5},{5,4},{6,7},{7,6},{8,9},{9,8},{10,11... | collective-permute-start | bytes 737288 | tf_op jit(solution)/shard_map/ppermute | solution.py:70
  62.3 1.9 %collective-permute-done.9.rest_3_ = bf16[3,320,128]{2,1,0:T(8,128)(2,1)S(1)} collective-permute-done((bf16[3,320,128]{2,1,0:T(8,128)(2,1)S(1)}, bf16[3,320,128]{2,1,0:T(8,128)(2,1)S(1)}, u32[]{:S(2)}, u32[]{:S(2)}) %collective-permute-start.9) | collective-permute-done | bytes 245792 | tf_op jit(solution)/shard_map/ppermute | solution.py:70
  64.2 5.7 %collective-permute-start.13 = (bf16[3,320,128]{2,1,0:T(8,128)(2,1)S(1)}, bf16[3,320,128]{2,1,0:T(8,128)(2,1)S(1)}, u32[]{:S(2)}, u32[]{:S(2)}) collective-permute-start(bf16[3,320,128]{2,1,0:T(8,128)(2,1)S(1)} %collective-permute-done.9.rest_3_), channel_id=1, source_target_pairs={{0,1},{1,0},{2,3},{3,2},{4,5},{5,4},{6,7},{7,6},{8,9},{9,8},{10,11... | collective-permute-start | bytes 737288 | tf_op jit(solution)/shard_map/ppermute | solution.py:70
  69.9 0.4 collective-permute-start.12
  70.4 5.2 %collective-permute-done.7.rest_1_ = bf16[3,320,128]{2,1,0:T(8,128)(2,1)S(1)} collective-permute-done((bf16[3,320,128]{2,1,0:T(8,128)(2,1)S(1)}, bf16[3,320,128]{2,1,0:T(8,128)(2,1)S(1)}, u32[]{:S(2)}, u32[]{:S(2)}) %collective-permute-start.7) | collective-permute-done | bytes 245792 | tf_op jit(solution)/shard_map/ppermute | solution.py:70
  75.5 0.5 collective-permute-start.11
  76.0 1.0 broadcast_select_fusion.2.rest_0_
  77.0 0.1 collective-permute-start.24
  77.1 0.0 collective-permute-done.10.rest_4_
  77.1 0.0 collective-permute-done.12.rest_6_
  77.1 0.0 collective-permute-done.11.rest_5_
  77.1 17.2 %residual_conv.2 = (bf16[8,8,320,128]{3,2,1,0:T(8,128)(2,1)S(1)}, bf16[8,320,128]{2,1,0:T(8,128)(2,1)S(1)}, bf16[8,320,128]{2,1,0:T(8,128)(2,1)S(1)}) custom-call(s32[3]{0:T(128)S(1)} %pad_add_fusion.place, bf16[8,8,320,128]{3,2,1,0:T(8,128)(2,1)} %bitcast.24, bf16[8,320,128]{2,1,0:T(8,128)(2,1)S(1)} %collective-permute-done.up_ref, ...), custom_call_target="tpu_custom_call" | custom-call | flops 15099494400 | bytes 10485760 | tf_op jit(solution)/shard_map/residual_conv/pallas_call | solution.py:170
  94.4 1.9 %collective-permute-start.14 = (bf16[8,320,128]{2,1,0:T(8,128)(2,1)S(1)}, bf16[8,320,128]{2,1,0:T(8,128)(2,1)S(1)}, u32[]{:S(2)}, u32[]{:S(2)}) collective-permute-start(bf16[8,320,128]{2,1,0:T(8,128)(2,1)S(1)} %get-tuple-element.22), channel_id=1, source_target_pairs={{0,1},{1,2},{2,3},{3,4},{4,5},{5,6},{6,7},{7,8},{8,9},{9,10},{10,1... | collective-permute-start | bytes 1966088 | tf_op jit(solution)/shard_map/ppermute | solution.py:198
  96.3 2.6 %collective-permute-start.15 = (bf16[8,320,128]{2,1,0:T(8,128)(2,1)S(1)}, bf16[8,320,128]{2,1,0:T(8,128)(2,1)S(1)}, u32[]{:S(2)}, u32[]{:S(2)}) collective-permute-start(bf16[8,320,128]{2,1,0:T(8,128)(2,1)S(1)} %get-tuple-element.23), channel_id=1, source_target_pairs={{1,0},{2,1},{3,2},{4,3},{5,4},{6,5},{7,6},{8,7},{9,8},{10,9},{11,1... | collective-permute-start | bytes 1966088 | tf_op jit(solution)/shard_map/ppermute | solution.py:199
  98.9 0.1 collective-permute-start.23
  99.0 0.9 collective-permute-start.22
  99.9 0.0 collective-permute-done.24.rest_4_
  99.9 1.7 %collective-permute-start.21 = (bf16[3,320,128]{2,1,0:T(8,128)(2,1)S(1)}, bf16[3,320,128]{2,1,0:T(8,128)(2,1)S(1)}, u32[]{:S(2)}, u32[]{:S(2)}) collective-permute-start(bf16[3,320,128]{2,1,0:T(8,128)(2,1)S(1)} %broadcast_select_fusion.2.rest_0_), channel_id=1, source_target_pairs={{0,2},{1,3},{2,0},{3,1},{4,6},{5,7},{6,4},{7,5},{8,10},{9,11},{10,... | collective-permute-start | bytes 737288 | tf_op jit(solution)/shard_map/ppermute | solution.py:70
  101.6 7.2 %collective-permute-done.23.rest_3_ = bf16[3,320,128]{2,1,0:T(8,128)(2,1)S(1)} collective-permute-done((bf16[3,320,128]{2,1,0:T(8,128)(2,1)S(1)}, bf16[3,320,128]{2,1,0:T(8,128)(2,1)S(1)}, u32[]{:S(2)}, u32[]{:S(2)}) %collective-permute-start.23) | collective-permute-done | bytes 245792 | tf_op jit(solution)/shard_map/ppermute | solution.py:70
  108.8 4.2 %collective-permute-start.27 = (bf16[3,320,128]{2,1,0:T(8,128)(2,1)S(1)}, bf16[3,320,128]{2,1,0:T(8,128)(2,1)S(1)}, u32[]{:S(2)}, u32[]{:S(2)}) collective-permute-start(bf16[3,320,128]{2,1,0:T(8,128)(2,1)S(1)} %collective-permute-done.23.rest_3_), channel_id=1, source_target_pairs={{0,1},{1,0},{2,3},{3,2},{4,5},{5,4},{6,7},{7,6},{8,9},{9,8},{10,11... | collective-permute-start | bytes 737288 | tf_op jit(solution)/shard_map/ppermute | solution.py:70
  113.0 0.0 collective-permute-done.22.rest_2_
  113.0 1.5 %collective-permute-start.26 = (bf16[3,320,128]{2,1,0:T(8,128)(2,1)S(1)}, bf16[3,320,128]{2,1,0:T(8,128)(2,1)S(1)}, u32[]{:S(2)}, u32[]{:S(2)}) collective-permute-start(bf16[3,320,128]{2,1,0:T(8,128)(2,1)S(1)} %collective-permute-done.22.rest_2_), channel_id=1, source_target_pairs={{0,1},{1,0},{2,3},{3,2},{4,5},{5,4},{6,7},{7,6},{8,9},{9,8},{10,11... | collective-permute-start | bytes 737288 | tf_op jit(solution)/shard_map/ppermute | solution.py:70
  114.4 6.9 %collective-permute-done.21.rest_1_ = bf16[3,320,128]{2,1,0:T(8,128)(2,1)S(1)} collective-permute-done((bf16[3,320,128]{2,1,0:T(8,128)(2,1)S(1)}, bf16[3,320,128]{2,1,0:T(8,128)(2,1)S(1)}, u32[]{:S(2)}, u32[]{:S(2)}) %collective-permute-start.21) | collective-permute-done | bytes 245792 | tf_op jit(solution)/shard_map/ppermute | solution.py:70
  121.4 3.8 %collective-permute-start.25 = (bf16[3,320,128]{2,1,0:T(8,128)(2,1)S(1)}, bf16[3,320,128]{2,1,0:T(8,128)(2,1)S(1)}, u32[]{:S(2)}, u32[]{:S(2)}) collective-permute-start(bf16[3,320,128]{2,1,0:T(8,128)(2,1)S(1)} %collective-permute-done.21.rest_1_), channel_id=1, source_target_pairs={{0,1},{1,0},{2,3},{3,2},{4,5},{5,4},{6,7},{7,6},{8,9},{9,8},{10,11... | collective-permute-start | bytes 737288 | tf_op jit(solution)/shard_map/ppermute | solution.py:70
  125.2 0.0 collective-permute-done.27.rest_7_
  125.2 1.1 collective-permute-done.25.rest_5_
  126.3 0.0 collective-permute-done.14.up_ref
  126.3 0.0 collective-permute-done.15.down_ref
  126.3 17.0 %residual_conv.3 = (bf16[8,8,320,128]{3,2,1,0:T(8,128)(2,1)}, bf16[8,320,128]{2,1,0:T(8,128)(2,1)}, bf16[8,320,128]{2,1,0:T(8,128)(2,1)}) custom-call(s32[3]{0:T(128)S(1)} %pad_add_fusion.place, bf16[8,8,320,128]{3,2,1,0:T(8,128)(2,1)S(1)} %get-tuple-element.21.x_ref, bf16[8,320,128]{2,1,0:T(8,128)(2,1)S(1)} %collective-permute-done.14.up_ref, ...), custom_call_target="tpu_custom_call" | custom-call | flops 15099494400 | bytes 10485760 | tf_op jit(solution)/shard_map/residual_conv/pallas_call | solution.py:170
  (14 shorter events, 0.2 us)
Async XLA Ops:
  0.1 2.3 %copy-start = (bf16[1,2,3,3,320,320]{5,4,3,2,1,0:T(8,128)(2,1)S(1)}, bf16[1,2,3,3,320,320]{5,4,3,2,1,0:T(8,128)(2,1)}, u32[]{:S(2)}) copy-start(bf16[1,2,3,3,320,320]{5,4,3,2,1,0:T(8,128)(2,1)} %param.6) | copy-start | bytes 11059204
  2.3 2.3 %copy-start.1 = (bf16[1,2,3,3,320,320]{5,4,3,2,1,0:T(8,128)(2,1)S(1)}, bf16[1,2,3,3,320,320]{5,4,3,2,1,0:T(8,128)(2,1)}, u32[]{:S(2)}) copy-start(bf16[1,2,3,3,320,320]{5,4,3,2,1,0:T(8,128)(2,1)} %param.8) | copy-start | bytes 11059204
  7.7 4.5 %copy-start.2 = (s32[2]{0:T(128)S(1)}, s32[2]{0:T(128)}, u32[]{:S(2)}) copy-start(s32[2]{0:T(128)} %param.9) | copy-start | bytes 28
  7.7 8.8 %collective-permute-start.3 = (bf16[3,320,128]{2,1,0:T(8,128)(2,1)S(1)}, bf16[3,320,128]{2,1,0:T(8,128)(2,1)S(1)}, u32[]{:S(2)}, u32[]{:S(2)}) collective-permute-start(bf16[3,320,128]{2,1,0:T(8,128)(2,1)S(1)} %get-tuple-element.20), channel_id=1, source_target_pairs={{0,1},{1,0},{2,3},{3,2},{4,5},{5,4},{6,7},{7,6},{8,9},{9,8},{10,11... | collective-permute-start | bytes 737288 | tf_op jit(solution)/shard_map/ppermute | solution.py:70
  11.6 16.4 %collective-permute-start.16 = (bf16[3,320,128]{2,1,0:T(8,128)(2,1)S(1)}, bf16[3,320,128]{2,1,0:T(8,128)(2,1)S(1)}, u32[]{:S(2)}, u32[]{:S(2)}) collective-permute-start(bf16[3,320,128]{2,1,0:T(8,128)(2,1)S(1)} %get-tuple-element.25), channel_id=1, source_target_pairs={{0,1},{1,0},{2,3},{3,2},{4,5},{5,4},{6,7},{7,6},{8,9},{9,8},{10,11... | collective-permute-start | bytes 737288 | tf_op jit(solution)/shard_map/ppermute | solution.py:70
  11.7 11.0 %collective-permute-start.17 = (bf16[3,320,128]{2,1,0:T(8,128)(2,1)S(1)}, bf16[3,320,128]{2,1,0:T(8,128)(2,1)S(1)}, u32[]{:S(2)}, u32[]{:S(2)}) collective-permute-start(bf16[3,320,128]{2,1,0:T(8,128)(2,1)S(1)} %get-tuple-element.27), channel_id=1, source_target_pairs={{0,1},{1,0},{2,3},{3,2},{4,5},{5,4},{6,7},{7,6},{8,9},{9,8},{10,11... | collective-permute-start | bytes 737288 | tf_op jit(solution)/shard_map/ppermute | solution.py:70
  12.2 10.8 %collective-permute-start.2 = (bf16[3,320,128]{2,1,0:T(8,128)(2,1)S(1)}, bf16[3,320,128]{2,1,0:T(8,128)(2,1)S(1)}, u32[]{:S(2)}, u32[]{:S(2)}) collective-permute-start(bf16[3,320,128]{2,1,0:T(8,128)(2,1)S(1)} %get-tuple-element.18), channel_id=1, source_target_pairs={{0,1},{1,0},{2,3},{3,2},{4,5},{5,4},{6,7},{7,6},{8,9},{9,8},{10,11... | collective-permute-start | bytes 737288 | tf_op jit(solution)/shard_map/ppermute | solution.py:70
  17.3 7.4 %collective-permute-start.4 = (bf16[3,320,128]{2,1,0:T(8,128)(2,1)}, bf16[3,320,128]{2,1,0:T(8,128)(2,1)}, u32[]{:S(2)}, u32[]{:S(2)}) collective-permute-start(bf16[3,320,128]{2,1,0:T(8,128)(2,1)} %broadcast_select_fusion.3), channel_id=1, source_target_pairs={{0,2},{1,3},{2,0},{3,1},{4,6},{5,7},{6,4},{7,5},{8,10},{9,11},{10,... | collective-permute-start | bytes 737288 | tf_op jit(solution)/shard_map/ppermute | solution.py:70
  19.4 38.7 %collective-permute-start.1 = (bf16[8,320,128]{2,1,0:T(8,128)(2,1)S(1)}, bf16[8,320,128]{2,1,0:T(8,128)(2,1)S(1)}, u32[]{:S(2)}, u32[]{:S(2)}) collective-permute-start(bf16[8,320,128]{2,1,0:T(8,128)(2,1)S(1)} %get-tuple-element.29), channel_id=1, source_target_pairs={{1,0},{2,1},{3,2},{4,3},{5,4},{6,5},{7,6},{8,7},{9,8},{10,9},{11,1... | collective-permute-start | bytes 1966088 | tf_op jit(solution)/shard_map/ppermute | solution.py:199
  22.7 11.8 %collective-permute-start.18 = (bf16[3,320,128]{2,1,0:T(8,128)(2,1)S(1)}, bf16[3,320,128]{2,1,0:T(8,128)(2,1)S(1)}, u32[]{:S(2)}, u32[]{:S(2)}) collective-permute-start(bf16[3,320,128]{2,1,0:T(8,128)(2,1)S(1)} %broadcast_select_fusion), channel_id=1, source_target_pairs={{0,2},{1,3},{2,0},{3,1},{4,6},{5,7},{6,4},{7,5},{8,10},{9,11},{10,... | collective-permute-start | bytes 737288 | tf_op jit(solution)/shard_map/ppermute | solution.py:70
  25.7 12.3 %collective-permute-start.5 = (bf16[3,320,128]{2,1,0:T(8,128)(2,1)S(1)}, bf16[3,320,128]{2,1,0:T(8,128)(2,1)S(1)}, u32[]{:S(2)}, u32[]{:S(2)}) collective-permute-start(bf16[3,320,128]{2,1,0:T(8,128)(2,1)S(1)} %select_select_fusion.1), channel_id=1, source_target_pairs={{0,8},{1,9},{2,10},{3,11},{4,12},{5,13},{6,14},{7,15},{8,0},{9,1},... | collective-permute-start | bytes 737288 | tf_op jit(solution)/shard_map/ppermute | solution.py:70
  34.6 17.6 %collective-permute-start.19 = (bf16[3,320,128]{2,1,0:T(8,128)(2,1)S(1)}, bf16[3,320,128]{2,1,0:T(8,128)(2,1)S(1)}, u32[]{:S(2)}, u32[]{:S(2)}) collective-permute-start(bf16[3,320,128]{2,1,0:T(8,128)(2,1)S(1)} %select_select_fusion), channel_id=1, source_target_pairs={{0,8},{1,9},{2,10},{3,11},{4,12},{5,13},{6,14},{7,15},{8,0},{9,1},... | collective-permute-start | bytes 737288 | tf_op jit(solution)/shard_map/ppermute | solution.py:70
  38.0 15.1 %collective-permute-start.6 = (bf16[3,320,128]{2,1,0:T(8,128)(2,1)S(1)}, bf16[3,320,128]{2,1,0:T(8,128)(2,1)S(1)}, u32[]{:S(2)}, u32[]{:S(2)}) collective-permute-start(bf16[3,320,128]{2,1,0:T(8,128)(2,1)S(1)} %broadcast_select_fusion.4), channel_id=1, source_target_pairs={{0,4},{1,5},{2,6},{3,7},{4,0},{5,1},{6,2},{7,3},{8,12},{9,13},{10,... | collective-permute-start | bytes 737288 | tf_op jit(solution)/shard_map/ppermute | solution.py:70
  42.6 34.4 %collective-permute-start = (bf16[8,320,128]{2,1,0:T(8,128)(2,1)}, bf16[8,320,128]{2,1,0:T(8,128)(2,1)S(1)}, u32[]{:S(2)}, u32[]{:S(2)}) collective-permute-start(bf16[8,320,128]{2,1,0:T(8,128)(2,1)} %get-tuple-element.30), channel_id=1, source_target_pairs={{0,1},{1,2},{2,3},{3,4},{4,5},{5,6},{6,7},{7,8},{8,9},{9,10},{10,1... | collective-permute-start | bytes 1966088 | tf_op jit(solution)/shard_map/ppermute | solution.py:198
  52.3 7.7 %collective-permute-start.20 = (bf16[3,320,128]{2,1,0:T(8,128)(2,1)S(1)}, bf16[3,320,128]{2,1,0:T(8,128)(2,1)}, u32[]{:S(2)}, u32[]{:S(2)}) collective-permute-start(bf16[3,320,128]{2,1,0:T(8,128)(2,1)S(1)} %broadcast_select_fusion.1), channel_id=1, source_target_pairs={{0,4},{1,5},{2,6},{3,7},{4,0},{5,1},{6,2},{7,3},{8,12},{9,13},{10,... | collective-permute-start | bytes 737288 | tf_op jit(solution)/shard_map/ppermute | solution.py:70
  53.1 11.1 %collective-permute-start.9 = (bf16[3,320,128]{2,1,0:T(8,128)(2,1)S(1)}, bf16[3,320,128]{2,1,0:T(8,128)(2,1)S(1)}, u32[]{:S(2)}, u32[]{:S(2)}) collective-permute-start(bf16[3,320,128]{2,1,0:T(8,128)(2,1)S(1)} %broadcast_select_fusion.5.rest_0_), channel_id=1, source_target_pairs={{0,18},{1,19},{2,16},{3,17},{4,22},{5,23},{6,20},{7,21},{8,26},{9,... | collective-permute-start | bytes 737288 | tf_op jit(solution)/shard_map/ppermute | solution.py:70
  57.7 12.3 %collective-permute-start.8 = (bf16[3,320,128]{2,1,0:T(8,128)(2,1)S(1)}, bf16[3,320,128]{2,1,0:T(8,128)(2,1)S(1)}, u32[]{:S(2)}, u32[]{:S(2)}) collective-permute-start(bf16[3,320,128]{2,1,0:T(8,128)(2,1)S(1)} %broadcast_select_fusion.5.rest_0_), channel_id=1, source_target_pairs={{0,16},{1,17},{2,18},{3,19},{4,20},{5,21},{6,22},{7,23},{8,24},{9,... | collective-permute-start | bytes 737288 | tf_op jit(solution)/shard_map/ppermute | solution.py:70
  58.1 17.4 %collective-permute-start.7 = (bf16[3,320,128]{2,1,0:T(8,128)(2,1)S(1)}, bf16[3,320,128]{2,1,0:T(8,128)(2,1)S(1)}, u32[]{:S(2)}, u32[]{:S(2)}) collective-permute-start(bf16[3,320,128]{2,1,0:T(8,128)(2,1)S(1)} %broadcast_select_fusion.5.rest_0_), channel_id=1, source_target_pairs={{0,2},{1,3},{2,0},{3,1},{4,6},{5,7},{6,4},{7,5},{8,10},{9,11},{10,... | collective-permute-start | bytes 737288 | tf_op jit(solution)/shard_map/ppermute | solution.py:70
  60.0 17.1 %collective-permute-start.10 = (bf16[3,320,128]{2,1,0:T(8,128)(2,1)S(1)}, bf16[3,320,128]{2,1,0:T(8,128)(2,1)S(1)}, u32[]{:S(2)}, u32[]{:S(2)}) collective-permute-start(bf16[3,320,128]{2,1,0:T(8,128)(2,1)S(1)} %broadcast_select_fusion.5.rest_0_), channel_id=1, source_target_pairs={{0,1},{1,0},{2,3},{3,2},{4,5},{5,4},{6,7},{7,6},{8,9},{9,8},{10,11... | collective-permute-start | bytes 737288 | tf_op jit(solution)/shard_map/ppermute | solution.py:70
  64.2 12.8 %collective-permute-start.13 = (bf16[3,320,128]{2,1,0:T(8,128)(2,1)S(1)}, bf16[3,320,128]{2,1,0:T(8,128)(2,1)S(1)}, u32[]{:S(2)}, u32[]{:S(2)}) collective-permute-start(bf16[3,320,128]{2,1,0:T(8,128)(2,1)S(1)} %collective-permute-done.9.rest_3_), channel_id=1, source_target_pairs={{0,1},{1,0},{2,3},{3,2},{4,5},{5,4},{6,7},{7,6},{8,9},{9,8},{10,11... | collective-permute-start | bytes 737288 | tf_op jit(solution)/shard_map/ppermute | solution.py:70
  69.9 7.1 %collective-permute-start.12 = (bf16[3,320,128]{2,1,0:T(8,128)(2,1)S(1)}, bf16[3,320,128]{2,1,0:T(8,128)(2,1)S(1)}, u32[]{:S(2)}, u32[]{:S(2)}) collective-permute-start(bf16[3,320,128]{2,1,0:T(8,128)(2,1)S(1)} %collective-permute-done.8.rest_2_), channel_id=1, source_target_pairs={{0,1},{1,0},{2,3},{3,2},{4,5},{5,4},{6,7},{7,6},{8,9},{9,8},{10,11... | collective-permute-start | bytes 737288 | tf_op jit(solution)/shard_map/ppermute | solution.py:70
  75.5 1.6 %collective-permute-start.11 = (bf16[3,320,128]{2,1,0:T(8,128)(2,1)S(1)}, bf16[3,320,128]{2,1,0:T(8,128)(2,1)S(1)}, u32[]{:S(2)}, u32[]{:S(2)}) collective-permute-start(bf16[3,320,128]{2,1,0:T(8,128)(2,1)S(1)} %collective-permute-done.7.rest_1_), channel_id=1, source_target_pairs={{0,1},{1,0},{2,3},{3,2},{4,5},{5,4},{6,7},{7,6},{8,9},{9,8},{10,11... | collective-permute-start | bytes 737288 | tf_op jit(solution)/shard_map/ppermute | solution.py:70
  77.0 22.9 %collective-permute-start.24 = (bf16[3,320,128]{2,1,0:T(8,128)(2,1)S(1)}, bf16[3,320,128]{2,1,0:T(8,128)(2,1)S(1)}, u32[]{:S(2)}, u32[]{:S(2)}) collective-permute-start(bf16[3,320,128]{2,1,0:T(8,128)(2,1)S(1)} %broadcast_select_fusion.2.rest_0_), channel_id=1, source_target_pairs={{0,1},{1,0},{2,3},{3,2},{4,5},{5,4},{6,7},{7,6},{8,9},{9,8},{10,11... | collective-permute-start | bytes 737288 | tf_op jit(solution)/shard_map/ppermute | solution.py:70
  94.4 31.9 %collective-permute-start.14 = (bf16[8,320,128]{2,1,0:T(8,128)(2,1)S(1)}, bf16[8,320,128]{2,1,0:T(8,128)(2,1)S(1)}, u32[]{:S(2)}, u32[]{:S(2)}) collective-permute-start(bf16[8,320,128]{2,1,0:T(8,128)(2,1)S(1)} %get-tuple-element.22), channel_id=1, source_target_pairs={{0,1},{1,2},{2,3},{3,4},{4,5},{5,6},{6,7},{7,8},{8,9},{9,10},{10,1... | collective-permute-start | bytes 1966088 | tf_op jit(solution)/shard_map/ppermute | solution.py:198
  96.3 30.0 %collective-permute-start.15 = (bf16[8,320,128]{2,1,0:T(8,128)(2,1)S(1)}, bf16[8,320,128]{2,1,0:T(8,128)(2,1)S(1)}, u32[]{:S(2)}, u32[]{:S(2)}) collective-permute-start(bf16[8,320,128]{2,1,0:T(8,128)(2,1)S(1)} %get-tuple-element.23), channel_id=1, source_target_pairs={{1,0},{2,1},{3,2},{4,3},{5,4},{6,5},{7,6},{8,7},{9,8},{10,9},{11,1... | collective-permute-start | bytes 1966088 | tf_op jit(solution)/shard_map/ppermute | solution.py:199
  98.9 9.9 %collective-permute-start.23 = (bf16[3,320,128]{2,1,0:T(8,128)(2,1)S(1)}, bf16[3,320,128]{2,1,0:T(8,128)(2,1)S(1)}, u32[]{:S(2)}, u32[]{:S(2)}) collective-permute-start(bf16[3,320,128]{2,1,0:T(8,128)(2,1)S(1)} %broadcast_select_fusion.2.rest_0_), channel_id=1, source_target_pairs={{0,18},{1,19},{2,16},{3,17},{4,22},{5,23},{6,20},{7,21},{8,26},{9,... | collective-permute-start | bytes 737288 | tf_op jit(solution)/shard_map/ppermute | solution.py:70
  99.0 14.0 %collective-permute-start.22 = (bf16[3,320,128]{2,1,0:T(8,128)(2,1)S(1)}, bf16[3,320,128]{2,1,0:T(8,128)(2,1)S(1)}, u32[]{:S(2)}, u32[]{:S(2)}) collective-permute-start(bf16[3,320,128]{2,1,0:T(8,128)(2,1)S(1)} %broadcast_select_fusion.2.rest_0_), channel_id=1, source_target_pairs={{0,16},{1,17},{2,18},{3,19},{4,20},{5,21},{6,22},{7,23},{8,24},{9,... | collective-permute-start | bytes 737288 | tf_op jit(solution)/shard_map/ppermute | solution.py:70
  99.9 21.4 %collective-permute-start.21 = (bf16[3,320,128]{2,1,0:T(8,128)(2,1)S(1)}, bf16[3,320,128]{2,1,0:T(8,128)(2,1)S(1)}, u32[]{:S(2)}, u32[]{:S(2)}) collective-permute-start(bf16[3,320,128]{2,1,0:T(8,128)(2,1)S(1)} %broadcast_select_fusion.2.rest_0_), channel_id=1, source_target_pairs={{0,2},{1,3},{2,0},{3,1},{4,6},{5,7},{6,4},{7,5},{8,10},{9,11},{10,... | collective-permute-start | bytes 737288 | tf_op jit(solution)/shard_map/ppermute | solution.py:70
  108.8 16.4 %collective-permute-start.27 = (bf16[3,320,128]{2,1,0:T(8,128)(2,1)S(1)}, bf16[3,320,128]{2,1,0:T(8,128)(2,1)S(1)}, u32[]{:S(2)}, u32[]{:S(2)}) collective-permute-start(bf16[3,320,128]{2,1,0:T(8,128)(2,1)S(1)} %collective-permute-done.23.rest_3_), channel_id=1, source_target_pairs={{0,1},{1,0},{2,3},{3,2},{4,5},{5,4},{6,7},{7,6},{8,9},{9,8},{10,11... | collective-permute-start | bytes 737288 | tf_op jit(solution)/shard_map/ppermute | solution.py:70
  113.0 12.2 %collective-permute-start.26 = (bf16[3,320,128]{2,1,0:T(8,128)(2,1)S(1)}, bf16[3,320,128]{2,1,0:T(8,128)(2,1)S(1)}, u32[]{:S(2)}, u32[]{:S(2)}) collective-permute-start(bf16[3,320,128]{2,1,0:T(8,128)(2,1)S(1)} %collective-permute-done.22.rest_2_), channel_id=1, source_target_pairs={{0,1},{1,0},{2,3},{3,2},{4,5},{5,4},{6,7},{7,6},{8,9},{9,8},{10,11... | collective-permute-start | bytes 737288 | tf_op jit(solution)/shard_map/ppermute | solution.py:70
  121.4 4.9 %collective-permute-start.25 = (bf16[3,320,128]{2,1,0:T(8,128)(2,1)S(1)}, bf16[3,320,128]{2,1,0:T(8,128)(2,1)S(1)}, u32[]{:S(2)}, u32[]{:S(2)}) collective-permute-start(bf16[3,320,128]{2,1,0:T(8,128)(2,1)S(1)} %collective-permute-done.21.rest_1_), channel_id=1, source_target_pairs={{0,1},{1,0},{2,3},{3,2},{4,5},{5,4},{6,7},{7,6},{8,9},{9,8},{10,11... | collective-permute-start | bytes 737288 | tf_op jit(solution)/shard_map/ppermute | solution.py:70

commit v2 on v1

v2 whole, which is shorter than its diff:
```python
import functools

import jax
import jax.numpy as jnp
from jax import lax
from jax.experimental import pallas as pl
from jax.experimental.pallas import tpu as pltpu
from jax.sharding import PartitionSpec as P

momentum_decay = 0.9
learn_rate = 0.5
axes = ("groups", "dp")
lanes = 128


def silu(v):
    half = v.astype(jnp.float32) * 0.5
    return (half * jnp.tanh(half) + half).astype(jnp.bfloat16)


def bits_of(ids, split):
    g, dp = ids[0], ids[1]
    return lax.rem(g, 2), lax.bitwise_and(lax.div(dp, split), 1), lax.bitwise_and(dp, 1)


def tile_pair(ids, kernel, step, splits):
    split = jnp.where(kernel == 0, splits[0], splits[1])
    half, bit, _ = bits_of(ids, split)
    return 2 * half + lax.bitwise_xor(bit, step)


def update_body(ids, owners, w_ref, m_ref, g_ref, *refs, depth, splits):
    kernel, step = pl.program_id(0), pl.program_id(1)
    core = lax.bitwise_and(ids[1], 1)
    taps, _, outs = w_ref.shape[1:]
    first = tile_pair(ids, kernel, step, splits) * 2 * lanes

    @pl.when(owners[kernel] == ids[1])
    def _():
        for tap in range(taps):
            velocity = momentum_decay * m_ref[0, tap] + g_ref[0, tap].astype(jnp.float32)
            fresh = w_ref[0, tap].astype(jnp.float32) - learn_rate * velocity
            at = first + lax.broadcasted_iota(jnp.int32, fresh.shape, 0)
            flipped = jnp.where(at < depth, fresh, 0.0).astype(jnp.bfloat16).T
            low, high = flipped[:, :lanes], flipped[:, lanes:]
            own = jnp.where(core == 0, low, high)
            other = jnp.where(core == 0, high, low)
            for at_step in range(2):

                @pl.when(step == at_step)
                def _():
                    refs[at_step][kernel, tap] = own
                    refs[2 + at_step][kernel, tap] = other


def update(ids, owners, weights, momentum, grads, splits):
    kernels, taps, depth, outs = weights.shape

    def which(k, i, ids, owners):
        last = (owners[1] == ids[1]).astype(jnp.int32)
        mine = owners[k] == ids[1]
        k = jnp.where(mine, k, last)
        return (k, 0, tile_pair(ids, k, jnp.where(mine, i, k * (1 - last)), splits), 0)

    block = pl.BlockSpec((1, taps, 2 * lanes, outs), which)
    shape = (kernels, taps, outs, lanes)
    return pl.pallas_call(
        functools.partial(update_body, depth=depth, splits=splits),
        grid_spec=pltpu.PrefetchScalarGridSpec(
            num_scalar_prefetch=2,
            grid=(kernels, 2),
            in_specs=[block] * 3,
            out_specs=[pl.BlockSpec(shape, lambda k, i, ids, owners: (0, 0, 0, 0))] * 4,
        ),
        out_shape=[jax.ShapeDtypeStruct(shape, jnp.bfloat16)] * 4,
        compiler_params=pltpu.CompilerParams(vmem_limit_bytes=62 * 2**20),
        name="kernel_update",
    )(ids, owners, weights, momentum, grads)


def swap(x, groups, count, change):
    pairs = []
    for g in range(groups):
        for d in range(count):
            to_g, to_d = change(g, d)
            pairs.append((g * count + d, to_g * count + to_d))
    return lax.ppermute(x, axes, pairs)


def after(x, other, owners):
    return jnp.where(owners[0] < 0, other, x)


def spread(pieces, owners, splits, groups, count):
    differs = lax.bitwise_xor(lax.axis_index("dp"), owners)
    mine0, mine1, theirs0, theirs1 = pieces

    def swap_dp(x, bit):
        return swap(x, groups, count, lambda g, d: (g, d ^ bit))

    def keep(bit, own, got, kernel):
        return jnp.where(lax.bitwise_and(differs[kernel], bit) == 0, own, got)

    got1 = swap_dp(theirs1, 1)
    got0 = swap_dp(theirs0, 1)
    far = [keep(1, mine1[k], got1[k], k) for k in range(2)]
    near = [keep(1, mine0[k], got0[k], k) for k in range(2)]
    held = [keep(splits[k], near[k], swap_dp(far[k], splits[k]), k) for k in range(2)]
    high = [1 << b for b in range(3, count.bit_length() - 1)]
    turns = (high[::-1] + [2], [4] + high[::-1])
    for bits in zip(*turns):
        held[0] = after(held[0], held[1], owners)
        held = [keep(bits[k], held[k], swap_dp(held[k], bits[k]), k) for k in range(2)]
    return after(held[0], held[1], owners), held[1]


def gather(piece, split, groups, count):
    def move(x, bit, group):
        return swap(x, groups, count, lambda g, d: (g ^ group, d ^ bit))

    return [piece, move(piece, split, 0), move(piece, 0, 1), move(piece, split, 1)]


def gather_cores(ring, groups, count):
    return ring + [swap(x, groups, count, lambda g, d: (g, d ^ 1)) for x in ring]


def conv_body(ids, *refs, split, rows, blocks, sources, drains, waits):
    piece_refs, refs = refs[:8], refs[8:]
    source_refs, refs = refs[: len(sources)], refs[len(sources) + waits :]
    drain_refs, (mixed, shifted) = refs[: len(drains)], refs[len(drains) :]
    where_in = {row: (at, pos) for at, held in enumerate(sources) for pos, row in enumerate(held)}
    n, _, chans, cols = source_refs[0].shape
    depth = 3 * chans

    @pl.when(pl.program_id(0) == 0)
    def _():
        half, bit, core = bits_of(ids, split)
        for relation, ref in enumerate(piece_refs):
            tile = (
                4 * lax.bitwise_xor(half, (relation >> 1) & 1)
                + 2 * lax.bitwise_xor(bit, relation & 1)
                + lax.bitwise_xor(core, relation >> 2)
            )
            at = pl.ds(pl.multiple_of(tile * lanes, lanes), lanes)
            outer = (ref[0].astype(jnp.float32) + ref[2].astype(jnp.float32)) * 0.5
            inner = ref[1].astype(jnp.float32) * 0.5
            mixed[0, :, at] = ref[0]
            mixed[1, :, at] = (outer + inner).astype(jnp.bfloat16)
            mixed[2, :, at] = (outer - inner).astype(jnp.bfloat16)
            mixed[3, :, at] = ref[2]

    def load(row, i):
        at, pos = where_in[row]
        return source_refs[at][i, pos]

    done = set()

    def put(row):
        if row in done:
            return
        done.add(row)
        for i in range(n):
            act = silu(load(row, i))
            lane = lax.broadcasted_iota(jnp.int32, act.shape, 1)
            zero = jnp.zeros_like(act)
            at = pl.ds(i * cols, cols)
            shifted[row + 1, 0:chans, at] = jnp.where(lane == 0, zero, pltpu.roll(act, 1, 1))
            shifted[row + 1, chans : 2 * chans, at] = act
            shifted[row + 1, 2 * chans : depth, at] = jnp.where(
                lane == cols - 1, zero, pltpu.roll(act, cols - 1, 1)
            )

    def product(t, field):
        return jnp.dot(mixed[t, :, 0:depth], field, preferred_element_type=jnp.float32)

    def emit(row, i, branch):
        result = (load(row, i).astype(jnp.float32) + branch).astype(jnp.bfloat16)
        for ref, held in zip(drain_refs, drains):
            if row in held:
                ref[i, held.index(row)] = result

    for row in range(2 * blocks[0] - 1, 2 * blocks[0] + 3):
        put(row)
    for at, block in enumerate(blocks):
        if at + 1 < len(blocks):
            for row in range(2 * blocks[at + 1] - 1, 2 * blocks[at + 1] + 3):
                put(row)
        d = [shifted.at[2 * block + j] for j in range(4)]
        plus = product(1, d[1][...] + d[2][...])
        minus = product(2, d[2][...] - d[1][...])
        even = plus + minus + product(0, d[0][...] - d[2][...])
        odd = plus - minus - product(3, d[1][...] - d[3][...])
        for i in range(n):
            at = slice(i * cols, (i + 1) * cols)
            emit(2 * block, i, even[:, at])
            emit(2 * block + 1, i, odd[:, at])
    made = {row for block in blocks for row in (2 * block, 2 * block + 1)}
    for ref, held in zip(drain_refs, drains):
        for pos, row in enumerate(held):
            if row not in made:
                at = len(sources) - 1
                for i in range(n):
                    ref[i, pos] = source_refs[at][i, sources[at].index(("made", row))]


def residual_conv(ids, split, pieces, rows, blocks, sources, drains, waits=()):
    held, arrays = zip(*sources)
    images, _, chans, cols = arrays[0].shape
    n = 2

    def strip(count):
        return pl.BlockSpec((n, count, chans, cols), lambda i, ids: (i, 0, 0, 0))

    piece = pl.BlockSpec(pieces[0].shape, lambda i, ids: (0, 0, 0))
    return pl.pallas_call(
        functools.partial(
            conv_body, split=split, rows=rows, blocks=blocks, sources=held, drains=drains, waits=len(waits)
        ),
        grid_spec=pltpu.PrefetchScalarGridSpec(
            num_scalar_prefetch=1,
            grid=(images // n,),
            in_specs=[piece] * 8
            + [strip(len(x)) for x in held]
            + [pl.BlockSpec(memory_space=pl.ANY)] * len(waits),
            out_specs=[strip(len(x)) for x in drains],
            scratch_shapes=[
                pltpu.VMEM((4, chans, 8 * lanes), jnp.bfloat16),
                pltpu.VMEM((rows + 2, 3 * chans, n * cols), jnp.bfloat16),
            ],
        ),
        out_shape=[
            jax.ShapeDtypeStruct((images, len(x), chans, cols), jnp.bfloat16) for x in drains
        ],
        compiler_params=pltpu.CompilerParams(vmem_limit_bytes=28 * 2**20),
        cost_estimate=pl.CostEstimate(
            flops=4 * images * len(blocks) * cols * 9 * chans * chans,
            bytes_accessed=4 * images * rows * cols * chans,
            transcendentals=images * rows * cols * chans,
        ),
        name="residual_conv",
    )(ids, *pieces, *arrays, *waits)


def borders(top, bottom, count):
    up = lax.ppermute(bottom, "dp", [(i, i + 1) for i in range(count - 1)])
    down = lax.ppermute(top, "dp", [(i + 1, i) for i in range(count - 1)])
    return up, down


def local(groups, count, images, kernel_weights, kernel_momentum, kernel_grads, owners):
    g, dp = lax.axis_index("groups"), lax.axis_index("dp")
    splits = (4, 2)
    ids = jnp.stack([g, dp]).astype(jnp.int32)

    def flat(x):
        _, kernels, taps, across, ins, outs = x.shape
        return x.reshape(kernels, taps, across * ins, outs)

    state = [flat(x) for x in (kernel_weights, kernel_momentum, kernel_grads)]
    field = jnp.swapaxes(images, 2, 3)
    rows = field.shape[1]
    everything = tuple(range(rows))
    up, down = borders(field[:, :1], field[:, -1:], count)

    one, two = spread(update(ids, owners, *state, splits), owners, splits, groups, count)
    ring = gather(one, splits[0], groups, count)
    first = gather_cores(ring, groups, count)
    two = after(two, ring[3], owners)
    ring = gather(two, splits[1], groups, count)

    around = [((-1,), up), ((rows,), down)]
    hidden, top, bottom = residual_conv(
        ids,
        splits[0],
        first,
        rows,
        tuple(range(rows // 2)),
        [(everything, field)] + around,
        (everything, (0,), (rows - 1,)),
        (two,),
    )
    ring = [after(x, top[: x.shape[0], 0], owners) for x in ring]
    second = gather_cores(ring, groups, count)
    up, down = borders(top, bottom, count)
    edge_blocks, inner_blocks = (0, rows // 2 - 1), tuple(range(1, rows // 2 - 1))
    inner = everything[2:-2]
    around = [((-1,), up), ((rows,), down)]
    parts = [(everything, hidden)]
    (out_inner,) = residual_conv(ids, splits[1], second, rows, inner_blocks, parts, (inner,))
    made = [(tuple(("made", row) for row in inner), out_inner)]
    (out,) = residual_conv(ids, splits[1], second, rows, edge_blocks, parts + around + made, (everything,))
    return jnp.swapaxes(out, 2, 3)


def solution(mesh):
    groups, count = mesh.shape["groups"], mesh.shape["dp"]
    assert groups % 2 == 0 and count % 8 == 0 and count & (count - 1) == 0
    state = P("dp", None, None, None, None, None)
    return jax.shard_map(
        functools.partial(local, groups, count),
        mesh=mesh,
        in_specs=(P("groups", "dp", None, None), state, state, state, P()),
        out_specs=P("groups", "dp", None, None),
        check_vma=False,
    )
```

time: 144 us -> 118 us (0.82)
  the two profiles are of different devices: /device:TPU:9 before, /device:TPU:1 now
where the time goes in v2:
time: 118 us; the launch traced here: 117 us
  Pallas kernels  40.5 us (34%)
  starting transfers between devices  39.4 us (33%)
  waiting for transfers between devices  24.7 us (21%)
  between operations  5.19 us (4%)
  local copies, waits for them, and re-layouts  4.45 us (4%)
  other arithmetic  3.04 us (3%)
    pallas_call x3, Pallas kernels, residual_conv(): pl.pallas_call(functools.partial(conv_body, split=split, rows=rows, block...  36.7 us
    ppermute x22, starting transfers between devices, swap(): return lax.ppermute(x, axes, pairs)  26.2 us
    ppermute x22, waiting for transfers between devices, swap(): return lax.ppermute(x, axes, pairs)  22.6 us
    ppermute x2, starting transfers between devices, borders(): down = lax.ppermute(top, 'dp', [(i + 1, i) for i in range(count - 1)])  6.95 us
    ppermute x2, starting transfers between devices, borders(): up = lax.ppermute(bottom, 'dp', [(i, i + 1) for i in range(count - 1)])  6.28 us
    pallas_call x1, Pallas kernels, update(): pl.pallas_call(functools.partial(update_body, depth=depth, splits=splits)...  3.81 us
    unnamed x6, local copies, waits for them, and re-layouts  2.49 us
  transfers between devices with their start and end apart: 26, of which 6 were waited for; matrix products, arithmetic and copies ran while one was open for 3% of the time, Pallas kernels for 22%

profile of v2, /device:TPU:1, one launch (start us, length us, event | category | flops | bytes accessed | tf_op | source)
XLA Modules:
  0.0 117.4 jit_solution(15548335985397475921)
XLA Ops:
  0.0 0.6 pad_add_fusion.ids
  0.6 3.8 %kernel_update.1 = (bf16[2,3,320,128]{3,2,1,0:T(8,128)(2,1)}, bf16[2,3,320,128]{3,2,1,0:T(8,128)(2,1)}, bf16[2,3,320,128]{3,2,1,0:T(8,128)(2,1)}, bf16[2,3,320,128]{3,2,1,0:T(8,128)(2,1)}) custom-call(s32[2]{0:T(128)} %pad_add_fusion.ids, s32[2]{0:T(128)} %owners.1, bf16[2,3,960,320]{3,2,1,0:T(8,128)(2,1)} %bitcast.47, f32[2,3,960,320]{3,2,1,0:T(8,128)} %bitcast.46, ...), custom_call_target="tpu_custom_call" | custom-call | tf_op jit(solution)/shard_map/kernel_update/pallas_call | solution.py:67
  4.4 0.1 collective-permute-start.1
  4.5 0.5 collective-permute-start
  4.9 0.6 fusion.9
  6.7 0.0 collective-permute-done.1
  6.7 1.1 fusion.4
  7.9 2.4 %collective-permute-start.2 = (bf16[3,320,128]{2,1,0:T(8,128)(2,1)S(1)}, bf16[3,320,128]{2,1,0:T(8,128)(2,1)S(1)}, u32[]{:S(2)}, u32[]{:S(2)}) collective-permute-start(bf16[3,320,128]{2,1,0:T(8,128)(2,1)S(1)} %get-tuple-element.25), channel_id=1, source_target_pairs={{0,2},{1,3},{2,0},{3,1},{4,6},{5,7},{6,4},{7,5},{8,10},{9,11},{10,... | collective-permute-start | bytes 737288 | tf_op jit(solution)/shard_map/ppermute | solution.py:87
  10.2 3.5 %collective-permute-start.5 = (bf16[3,320,128]{2,1,0:T(8,128)(2,1)S(1)}, bf16[3,320,128]{2,1,0:T(8,128)(2,1)S(1)}, u32[]{:S(2)}, u32[]{:S(2)}) collective-permute-start(bf16[3,320,128]{2,1,0:T(8,128)(2,1)S(1)} %get-tuple-element.26), channel_id=1, source_target_pairs={{0,4},{1,5},{2,6},{3,7},{4,0},{5,1},{6,2},{7,3},{8,12},{9,13},{10,... | collective-permute-start | bytes 737288 | tf_op jit(solution)/shard_map/ppermute | solution.py:87
  15.0 0.0 collective-permute-done
  15.1 1.1 collective-permute-done.2
  16.2 3.2 %collective-permute-done.5 = bf16[3,320,128]{2,1,0:T(8,128)(2,1)S(1)} collective-permute-done((bf16[3,320,128]{2,1,0:T(8,128)(2,1)S(1)}, bf16[3,320,128]{2,1,0:T(8,128)(2,1)S(1)}, u32[]{:S(2)}, u32[]{:S(2)}) %collective-permute-start.5) | collective-permute-done | bytes 245792 | tf_op jit(solution)/shard_map/ppermute | solution.py:87
  19.4 1.1 fusion.3
  20.5 0.1 collective-permute-start.6
  20.6 1.2 %collective-permute-start.3 = (bf16[3,320,128]{2,1,0:T(8,128)(2,1)S(1)}, bf16[3,320,128]{2,1,0:T(8,128)(2,1)S(1)}, u32[]{:S(2)}, u32[]{:S(2)}) collective-permute-start(bf16[3,320,128]{2,1,0:T(8,128)(2,1)S(1)} %get-tuple-element.22), channel_id=1, source_target_pairs={{0,4},{1,5},{2,6},{3,7},{4,0},{5,1},{6,2},{7,3},{8,12},{9,13},{10,... | collective-permute-start | bytes 737288 | tf_op jit(solution)/shard_map/ppermute | solution.py:87
  23.1 10.7 %collective-permute-done.6 = bf16[3,320,128]{2,1,0:T(8,128)(2,1)S(1)} collective-permute-done((bf16[3,320,128]{2,1,0:T(8,128)(2,1)S(1)}, bf16[3,320,128]{2,1,0:T(8,128)(2,1)S(1)}, u32[]{:S(2)}, u32[]{:S(2)}) %collective-permute-start.6) | collective-permute-done | bytes 245792 | tf_op jit(solution)/shard_map/ppermute | solution.py:87
  33.7 0.0 collective-permute-done.3
  33.7 0.1 select_select_fusion.1
  33.8 0.5 collective-permute-start.7
  34.3 0.4 collective-permute-start.4
  34.7 1.4 %fusion.8 = (bf16[8,1,320,128]{3,2,1,0:T(8,128)(2,1)S(1)}, bf16[8,1,320,128]{3,2,1,0:T(8,128)(2,1)S(1)}) fusion(bf16[8,8,320,128]{3,2,1,0:T(8,128)(2,1)} %bitcast.43), kind=kLoop, calls=%fused_computation.23 | loop fusion | bytes 2621440 | tf_op jit(solution)/shard_map/slice | solution.py:264
  36.1 4.6 %collective-permute-start.16 = (bf16[8,1,320,128]{3,2,1,0:T(8,128)(2,1)S(1)}, bf16[8,1,320,128]{3,2,1,0:T(8,128)(2,1)S(1)}, u32[]{:S(2)}, u32[]{:S(2)}) collective-permute-start(bf16[8,1,320,128]{3,2,1,0:T(8,128)(2,1)S(1)} %get-tuple-element.23), channel_id=1, source_target_pairs={{1,0},{2,1},{3,2},{4,3},{5,4},{6,5},{7,6},{8,7},{9,8},{10,9},{11,1... | collective-permute-start | bytes 1966088 | tf_op jit(solution)/shard_map/ppermute | solution.py:247
  40.7 2.9 %collective-permute-start.15 = (bf16[8,1,320,128]{3,2,1,0:T(8,128)(2,1)S(1)}, bf16[8,1,320,128]{3,2,1,0:T(8,128)(2,1)S(1)}, u32[]{:S(2)}, u32[]{:S(2)}) collective-permute-start(bf16[8,1,320,128]{3,2,1,0:T(8,128)(2,1)S(1)} %get-tuple-element.24), channel_id=1, source_target_pairs={{0,1},{1,2},{2,3},{3,4},{4,5},{5,6},{6,7},{7,8},{8,9},{9,10},{10,1... | collective-permute-start | bytes 1966088 | tf_op jit(solution)/shard_map/ppermute | solution.py:246
  44.8 0.0 collective-permute-done.7
  44.8 2.9 %collective-permute-done.4 = bf16[3,320,128]{2,1,0:T(8,128)(2,1)S(1)} collective-permute-done((bf16[3,320,128]{2,1,0:T(8,128)(2,1)S(1)}, bf16[3,320,128]{2,1,0:T(8,128)(2,1)S(1)}, u32[]{:S(2)}, u32[]{:S(2)}) %collective-permute-start.4) | collective-permute-done | bytes 245792 | tf_op jit(solution)/shard_map/ppermute | solution.py:87
  47.8 0.1 collective-permute-start.10
  47.9 1.1 collective-permute-start.9
  48.9 1.6 %collective-permute-start.8 = (bf16[3,320,128]{2,1,0:T(8,128)(2,1)S(1)}, bf16[3,320,128]{2,1,0:T(8,128)(2,1)S(1)}, u32[]{:S(2)}, u32[]{:S(2)}) collective-permute-start(bf16[3,320,128]{2,1,0:T(8,128)(2,1)S(1)} %select_select_fusion.refs_0_), channel_id=1, source_target_pairs={{0,4},{1,5},{2,6},{3,7},{4,0},{5,1},{6,2},{7,3},{8,12},{9,13},{10,... | collective-permute-start | bytes 737288 | tf_op jit(solution)/shard_map/ppermute | solution.py:87
  50.5 0.0 collective-permute-done.16.refs_10_
  50.5 1.4 %collective-permute-start.11 = (bf16[3,320,128]{2,1,0:T(8,128)(2,1)S(1)}, bf16[3,320,128]{2,1,0:T(8,128)(2,1)S(1)}, u32[]{:S(2)}, u32[]{:S(2)}) collective-permute-start(bf16[3,320,128]{2,1,0:T(8,128)(2,1)S(1)} %select_select_fusion.refs_0_), channel_id=1, source_target_pairs={{0,1},{1,0},{2,3},{3,2},{4,5},{5,4},{6,7},{7,6},{8,9},{9,8},{10,11... | collective-permute-start | bytes 737288 | tf_op jit(solution)/shard_map/ppermute | solution.py:87
  51.9 4.6 %collective-permute-done.10.refs_3_ = bf16[3,320,128]{2,1,0:T(8,128)(2,1)S(1)} collective-permute-done((bf16[3,320,128]{2,1,0:T(8,128)(2,1)S(1)}, bf16[3,320,128]{2,1,0:T(8,128)(2,1)S(1)}, u32[]{:S(2)}, u32[]{:S(2)}) %collective-permute-start.10) | collective-permute-done | bytes 245792 | tf_op jit(solution)/shard_map/ppermute | solution.py:87
  56.5 7.4 %collective-permute-start.14 = (bf16[3,320,128]{2,1,0:T(8,128)(2,1)S(1)}, bf16[3,320,128]{2,1,0:T(8,128)(2,1)S(1)}, u32[]{:S(2)}, u32[]{:S(2)}) collective-permute-start(bf16[3,320,128]{2,1,0:T(8,128)(2,1)S(1)} %collective-permute-done.10.refs_3_), channel_id=1, source_target_pairs={{0,1},{1,0},{2,3},{3,2},{4,5},{5,4},{6,7},{7,6},{8,9},{9,8},{10,11... | collective-permute-start | bytes 737288 | tf_op jit(solution)/shard_map/ppermute | solution.py:87
  63.9 0.0 collective-permute-done.9.refs_2_
  63.9 0.0 collective-permute-start.13
  63.9 0.0 collective-permute-done.8.refs_1_
  63.9 1.9 %collective-permute-start.12 = (bf16[3,320,128]{2,1,0:T(8,128)(2,1)S(1)}, bf16[3,320,128]{2,1,0:T(8,128)(2,1)S(1)}, u32[]{:S(2)}, u32[]{:S(2)}) collective-permute-start(bf16[3,320,128]{2,1,0:T(8,128)(2,1)S(1)} %collective-permute-done.8.refs_1_), channel_id=1, source_target_pairs={{0,1},{1,0},{2,3},{3,2},{4,5},{5,4},{6,7},{7,6},{8,9},{9,8},{10,11... | collective-permute-start | bytes 737288 | tf_op jit(solution)/shard_map/ppermute | solution.py:87
  65.9 0.0 collective-permute-done.15.refs_9_
  65.9 0.1 collective-permute-start.19
  65.9 0.0 collective-permute-done.11.refs_4_
  66.0 1.1 collective-permute-start.18
  67.0 0.0 collective-permute-done.14.refs_7_
  67.0 1.6 %collective-permute-start.17 = (bf16[3,320,128]{2,1,0:T(8,128)(2,1)S(1)}, bf16[3,320,128]{2,1,0:T(8,128)(2,1)S(1)}, u32[]{:S(2)}, u32[]{:S(2)}) collective-permute-start(bf16[3,320,128]{2,1,0:T(8,128)(2,1)S(1)} %broadcast_select_fusion.6.refs_11_), channel_id=1, source_target_pairs={{0,2},{1,3},{2,0},{3,1},{4,6},{5,7},{6,4},{7,5},{8,10},{9,11},{10,... | collective-permute-start | bytes 737288 | tf_op jit(solution)/shard_map/ppermute | solution.py:87
  68.6 0.0 collective-permute-done.13.refs_6_
  68.6 0.0 collective-permute-done.12.refs_5_
  68.6 0.0 copy-start
  68.6 2.5 %copy-done = bf16[8,8,128,320]{2,3,1,0:T(8,128)(2,1)S(1)} copy-done((bf16[8,8,128,320]{2,3,1,0:T(8,128)(2,1)S(1)}, bf16[8,8,128,320]{2,3,1,0:T(8,128)(2,1)}, u32[]{:S(2)}) %copy-start) | copy-done | bytes 5242904
  71.1 15.9 %residual_conv.3 = (bf16[8,8,320,128]{3,2,1,0:T(8,128)(2,1)S(1)}, bf16[8,1,320,128]{3,2,1,0:T(8,128)(2,1)S(1)}, bf16[8,1,320,128]{3,2,1,0:T(8,128)(2,1)S(1)}) custom-call(s32[2]{0:T(128)S(1)} %copy-done.1, bf16[3,320,128]{2,1,0:T(8,128)(2,1)S(1)} %select_select_fusion.refs_0_, bf16[3,320,128]{2,1,0:T(8,128)(2,1)S(1)} %collective-permute-done.8.refs_1_, ...), custom_call_target="tpu_custom_call" | custom-call | flops 15099494400 | bytes 10485760 | tf_op jit(solution)/shard_map/residual_conv/pallas_call | solution.py:216
  87.0 0.0 collective-permute-done.19
  87.0 0.0 collective-permute-done.18
  87.0 0.0 collective-permute-done.17
  87.0 0.1 broadcast_select_fusion.2
  87.1 0.9 collective-permute-start.23
  88.0 0.1 collective-permute-start.20
  88.1 0.4 collective-permute-start.21
  88.5 0.1 collective-permute-start.22
  88.6 2.3 %collective-permute-start.25 = (bf16[8,1,320,128]{3,2,1,0:T(8,128)(2,1)S(1)}, bf16[8,1,320,128]{3,2,1,0:T(8,128)(2,1)S(1)}, u32[]{:S(2)}, u32[]{:S(2)}) collective-permute-start(bf16[8,1,320,128]{3,2,1,0:T(8,128)(2,1)S(1)} %get-tuple-element.16), channel_id=1, source_target_pairs={{1,0},{2,1},{3,2},{4,3},{5,4},{6,5},{7,6},{8,7},{9,8},{10,9},{11,1... | collective-permute-start | bytes 1966088 | tf_op jit(solution)/shard_map/ppermute | solution.py:247
  90.9 0.0 collective-permute-done.23.refs_7_
  90.9 3.4 %collective-permute-start.24 = (bf16[8,1,320,128]{3,2,1,0:T(8,128)(2,1)S(1)}, bf16[8,1,320,128]{3,2,1,0:T(8,128)(2,1)S(1)}, u32[]{:S(2)}, u32[]{:S(2)}) collective-permute-start(bf16[8,1,320,128]{3,2,1,0:T(8,128)(2,1)S(1)} %get-tuple-element.18), channel_id=1, source_target_pairs={{0,1},{1,2},{2,3},{3,4},{4,5},{5,6},{6,7},{7,8},{8,9},{9,10},{10,1... | collective-permute-start | bytes 1966088 | tf_op jit(solution)/shard_map/ppermute | solution.py:246
  94.4 0.0 collective-permute-done.20.refs_4_
  94.4 0.0 collective-permute-done.21.refs_5_
  94.4 0.0 collective-permute-done.22.refs_6_
  94.4 9.7 %residual_conv.4.refs_11_ = bf16[8,4,320,128]{3,2,1,0:T(8,128)(2,1)S(1)} custom-call(s32[2]{0:T(128)S(1)} %copy-done.1, bf16[3,320,128]{2,1,0:T(8,128)(2,1)S(1)} %get-tuple-element.28.refs_0_, bf16[3,320,128]{2,1,0:T(8,128)(2,1)S(1)} %get-tuple-element.29.refs_1_, bf16[3,320,128]{2,1,0:T(8,128)(2,1)S(1)} %get-tuple-element.30.refs_2_, ...), custom_call_target="tpu_custom_call" | custom-call | flops 7549747200 | bytes 10485760 | tf_op jit(solution)/shard_map/residual_conv/pallas_call | solution.py:216
  104.1 2.1 %collective-permute-done.24.refs_9_ = bf16[8,1,320,128]{3,2,1,0:T(8,128)(2,1)S(1)} collective-permute-done((bf16[8,1,320,128]{3,2,1,0:T(8,128)(2,1)S(1)}, bf16[8,1,320,128]{3,2,1,0:T(8,128)(2,1)S(1)}, u32[]{:S(2)}, u32[]{:S(2)}) %collective-permute-start.24) | collective-permute-done | bytes 655392 | tf_op jit(solution)/shard_map/ppermute | solution.py:246
  106.2 11.1 %residual_conv.5 = bf16[8,8,320,128]{3,2,1,0:T(8,128)(2,1)} custom-call(s32[2]{0:T(128)S(1)} %copy-done.1, bf16[3,320,128]{2,1,0:T(8,128)(2,1)S(1)} %get-tuple-element.28.refs_0_, bf16[3,320,128]{2,1,0:T(8,128)(2,1)S(1)} %get-tuple-element.29.refs_1_, bf16[3,320,128]{2,1,0:T(8,128)(2,1)S(1)} %get-tuple-element.30.refs_2_, ...), custom_call_target="tpu_custom_call" | custom-call | flops 7549747200 | bytes 10485760 | tf_op jit(solution)/shard_map/residual_conv/pallas_call | solution.py:216
  (8 shorter events, 0.1 us)
Async XLA Ops:
  0.6 4.3 %copy-start.2 = (s32[2]{0:T(128)S(1)}, s32[2]{0:T(128)}, u32[]{:S(2)}) copy-start(s32[2]{0:T(128)} %owners.1) | copy-start | bytes 28
  4.4 64.2 %copy-start.1 = (s32[2]{0:T(128)S(1)}, s32[2]{0:T(128)}, u32[]{:S(2)}) copy-start(s32[2]{0:T(128)} %pad_add_fusion.ids) | copy-start | bytes 28
  4.4 2.3 %collective-permute-start.1 = (bf16[2,3,320,128]{3,2,1,0:T(8,128)(2,1)}, bf16[2,3,320,128]{3,2,1,0:T(8,128)(2,1)S(1)}, u32[]{:S(2)}, u32[]{:S(2)}) collective-permute-start(bf16[2,3,320,128]{3,2,1,0:T(8,128)(2,1)} %get-tuple-element.15), channel_id=1, source_target_pairs={{0,1},{1,0},{2,3},{3,2},{4,5},{5,4},{6,7},{7,6},{8,9},{9,8},{10,11... | collective-permute-start | bytes 1474568 | tf_op jit(solution)/shard_map/ppermute | solution.py:87
  4.5 10.6 %collective-permute-start = (bf16[2,3,320,128]{3,2,1,0:T(8,128)(2,1)}, bf16[2,3,320,128]{3,2,1,0:T(8,128)(2,1)S(1)}, u32[]{:S(2)}, u32[]{:S(2)}) collective-permute-start(bf16[2,3,320,128]{3,2,1,0:T(8,128)(2,1)} %get-tuple-element.13), channel_id=1, source_target_pairs={{0,1},{1,0},{2,3},{3,2},{4,5},{5,4},{6,7},{7,6},{8,9},{9,8},{10,11... | collective-permute-start | bytes 1474568 | tf_op jit(solution)/shard_map/ppermute | solution.py:87
  7.9 8.3 %collective-permute-start.2 = (bf16[3,320,128]{2,1,0:T(8,128)(2,1)S(1)}, bf16[3,320,128]{2,1,0:T(8,128)(2,1)S(1)}, u32[]{:S(2)}, u32[]{:S(2)}) collective-permute-start(bf16[3,320,128]{2,1,0:T(8,128)(2,1)S(1)} %get-tuple-element.25), channel_id=1, source_target_pairs={{0,2},{1,3},{2,0},{3,1},{4,6},{5,7},{6,4},{7,5},{8,10},{9,11},{10,... | collective-permute-start | bytes 737288 | tf_op jit(solution)/shard_map/ppermute | solution.py:87
  10.2 9.2 %collective-permute-start.5 = (bf16[3,320,128]{2,1,0:T(8,128)(2,1)S(1)}, bf16[3,320,128]{2,1,0:T(8,128)(2,1)S(1)}, u32[]{:S(2)}, u32[]{:S(2)}) collective-permute-start(bf16[3,320,128]{2,1,0:T(8,128)(2,1)S(1)} %get-tuple-element.26), channel_id=1, source_target_pairs={{0,4},{1,5},{2,6},{3,7},{4,0},{5,1},{6,2},{7,3},{8,12},{9,13},{10,... | collective-permute-start | bytes 737288 | tf_op jit(solution)/shard_map/ppermute | solution.py:87
  20.5 13.2 %collective-permute-start.6 = (bf16[3,320,128]{2,1,0:T(8,128)(2,1)S(1)}, bf16[3,320,128]{2,1,0:T(8,128)(2,1)S(1)}, u32[]{:S(2)}, u32[]{:S(2)}) collective-permute-start(bf16[3,320,128]{2,1,0:T(8,128)(2,1)S(1)} %get-tuple-element.21), channel_id=1, source_target_pairs={{0,8},{1,9},{2,10},{3,11},{4,12},{5,13},{6,14},{7,15},{8,0},{9,1},... | collective-permute-start | bytes 737288 | tf_op jit(solution)/shard_map/ppermute | solution.py:87
  20.6 13.1 %collective-permute-start.3 = (bf16[3,320,128]{2,1,0:T(8,128)(2,1)S(1)}, bf16[3,320,128]{2,1,0:T(8,128)(2,1)S(1)}, u32[]{:S(2)}, u32[]{:S(2)}) collective-permute-start(bf16[3,320,128]{2,1,0:T(8,128)(2,1)S(1)} %get-tuple-element.22), channel_id=1, source_target_pairs={{0,4},{1,5},{2,6},{3,7},{4,0},{5,1},{6,2},{7,3},{8,12},{9,13},{10,... | collective-permute-start | bytes 737288 | tf_op jit(solution)/shard_map/ppermute | solution.py:87
  33.8 11.0 %collective-permute-start.7 = (bf16[3,320,128]{2,1,0:T(8,128)(2,1)S(1)}, bf16[3,320,128]{2,1,0:T(8,128)(2,1)S(1)}, u32[]{:S(2)}, u32[]{:S(2)}) collective-permute-start(bf16[3,320,128]{2,1,0:T(8,128)(2,1)S(1)} %get-tuple-element.19), channel_id=1, source_target_pairs={{0,2},{1,3},{2,0},{3,1},{4,6},{5,7},{6,4},{7,5},{8,10},{9,11},{10,... | collective-permute-start | bytes 737288 | tf_op jit(solution)/shard_map/ppermute | solution.py:87
  34.3 13.5 %collective-permute-start.4 = (bf16[3,320,128]{2,1,0:T(8,128)(2,1)S(1)}, bf16[3,320,128]{2,1,0:T(8,128)(2,1)S(1)}, u32[]{:S(2)}, u32[]{:S(2)}) collective-permute-start(bf16[3,320,128]{2,1,0:T(8,128)(2,1)S(1)} %get-tuple-element.20), channel_id=1, source_target_pairs={{0,8},{1,9},{2,10},{3,11},{4,12},{5,13},{6,14},{7,15},{8,0},{9,1},... | collective-permute-start | bytes 737288 | tf_op jit(solution)/shard_map/ppermute | solution.py:87
  36.1 14.5 %collective-permute-start.16 = (bf16[8,1,320,128]{3,2,1,0:T(8,128)(2,1)S(1)}, bf16[8,1,320,128]{3,2,1,0:T(8,128)(2,1)S(1)}, u32[]{:S(2)}, u32[]{:S(2)}) collective-permute-start(bf16[8,1,320,128]{3,2,1,0:T(8,128)(2,1)S(1)} %get-tuple-element.23), channel_id=1, source_target_pairs={{1,0},{2,1},{3,2},{4,3},{5,4},{6,5},{7,6},{8,7},{9,8},{10,9},{11,1... | collective-permute-start | bytes 1966088 | tf_op jit(solution)/shard_map/ppermute | solution.py:247
  40.7 25.1 %collective-permute-start.15 = (bf16[8,1,320,128]{3,2,1,0:T(8,128)(2,1)S(1)}, bf16[8,1,320,128]{3,2,1,0:T(8,128)(2,1)S(1)}, u32[]{:S(2)}, u32[]{:S(2)}) collective-permute-start(bf16[8,1,320,128]{3,2,1,0:T(8,128)(2,1)S(1)} %get-tuple-element.24), channel_id=1, source_target_pairs={{0,1},{1,2},{2,3},{3,4},{4,5},{5,6},{6,7},{7,8},{8,9},{9,10},{10,1... | collective-permute-start | bytes 1966088 | tf_op jit(solution)/shard_map/ppermute | solution.py:246
  47.8 8.7 %collective-permute-start.10 = (bf16[3,320,128]{2,1,0:T(8,128)(2,1)S(1)}, bf16[3,320,128]{2,1,0:T(8,128)(2,1)S(1)}, u32[]{:S(2)}, u32[]{:S(2)}) collective-permute-start(bf16[3,320,128]{2,1,0:T(8,128)(2,1)S(1)} %select_select_fusion.refs_0_), channel_id=1, source_target_pairs={{0,20},{1,21},{2,22},{3,23},{4,16},{5,17},{6,18},{7,19},{8,28},{9,... | collective-permute-start | bytes 737288 | tf_op jit(solution)/shard_map/ppermute | solution.py:87
  47.9 16.0 %collective-permute-start.9 = (bf16[3,320,128]{2,1,0:T(8,128)(2,1)S(1)}, bf16[3,320,128]{2,1,0:T(8,128)(2,1)S(1)}, u32[]{:S(2)}, u32[]{:S(2)}) collective-permute-start(bf16[3,320,128]{2,1,0:T(8,128)(2,1)S(1)} %select_select_fusion.refs_0_), channel_id=1, source_target_pairs={{0,16},{1,17},{2,18},{3,19},{4,20},{5,21},{6,22},{7,23},{8,24},{9,... | collective-permute-start | bytes 737288 | tf_op jit(solution)/shard_map/ppermute | solution.py:87
  48.9 14.9 %collective-permute-start.8 = (bf16[3,320,128]{2,1,0:T(8,128)(2,1)S(1)}, bf16[3,320,128]{2,1,0:T(8,128)(2,1)S(1)}, u32[]{:S(2)}, u32[]{:S(2)}) collective-permute-start(bf16[3,320,128]{2,1,0:T(8,128)(2,1)S(1)} %select_select_fusion.refs_0_), channel_id=1, source_target_pairs={{0,4},{1,5},{2,6},{3,7},{4,0},{5,1},{6,2},{7,3},{8,12},{9,13},{10,... | collective-permute-start | bytes 737288 | tf_op jit(solution)/shard_map/ppermute | solution.py:87
  50.5 15.4 %collective-permute-start.11 = (bf16[3,320,128]{2,1,0:T(8,128)(2,1)S(1)}, bf16[3,320,128]{2,1,0:T(8,128)(2,1)S(1)}, u32[]{:S(2)}, u32[]{:S(2)}) collective-permute-start(bf16[3,320,128]{2,1,0:T(8,128)(2,1)S(1)} %select_select_fusion.refs_0_), channel_id=1, source_target_pairs={{0,1},{1,0},{2,3},{3,2},{4,5},{5,4},{6,7},{7,6},{8,9},{9,8},{10,11... | collective-permute-start | bytes 737288 | tf_op jit(solution)/shard_map/ppermute | solution.py:87
  56.5 10.5 %collective-permute-start.14 = (bf16[3,320,128]{2,1,0:T(8,128)(2,1)S(1)}, bf16[3,320,128]{2,1,0:T(8,128)(2,1)S(1)}, u32[]{:S(2)}, u32[]{:S(2)}) collective-permute-start(bf16[3,320,128]{2,1,0:T(8,128)(2,1)S(1)} %collective-permute-done.10.refs_3_), channel_id=1, source_target_pairs={{0,1},{1,0},{2,3},{3,2},{4,5},{5,4},{6,7},{7,6},{8,9},{9,8},{10,11... | collective-permute-start | bytes 737288 | tf_op jit(solution)/shard_map/ppermute | solution.py:87
  63.9 4.7 %collective-permute-start.13 = (bf16[3,320,128]{2,1,0:T(8,128)(2,1)S(1)}, bf16[3,320,128]{2,1,0:T(8,128)(2,1)S(1)}, u32[]{:S(2)}, u32[]{:S(2)}) collective-permute-start(bf16[3,320,128]{2,1,0:T(8,128)(2,1)S(1)} %collective-permute-done.9.refs_2_), channel_id=1, source_target_pairs={{0,1},{1,0},{2,3},{3,2},{4,5},{5,4},{6,7},{7,6},{8,9},{9,8},{10,11... | collective-permute-start | bytes 737288 | tf_op jit(solution)/shard_map/ppermute | solution.py:87
  63.9 4.7 %collective-permute-start.12 = (bf16[3,320,128]{2,1,0:T(8,128)(2,1)S(1)}, bf16[3,320,128]{2,1,0:T(8,128)(2,1)S(1)}, u32[]{:S(2)}, u32[]{:S(2)}) collective-permute-start(bf16[3,320,128]{2,1,0:T(8,128)(2,1)S(1)} %collective-permute-done.8.refs_1_), channel_id=1, source_target_pairs={{0,1},{1,0},{2,3},{3,2},{4,5},{5,4},{6,7},{7,6},{8,9},{9,8},{10,11... | collective-permute-start | bytes 737288 | tf_op jit(solution)/shard_map/ppermute | solution.py:87
  65.9 21.1 %collective-permute-start.19 = (bf16[3,320,128]{2,1,0:T(8,128)(2,1)S(1)}, bf16[3,320,128]{2,1,0:T(8,128)(2,1)S(1)}, u32[]{:S(2)}, u32[]{:S(2)}) collective-permute-start(bf16[3,320,128]{2,1,0:T(8,128)(2,1)S(1)} %broadcast_select_fusion.6.refs_11_), channel_id=1, source_target_pairs={{0,18},{1,19},{2,16},{3,17},{4,22},{5,23},{6,20},{7,21},{8,26},{9,... | collective-permute-start | bytes 737288 | tf_op jit(solution)/shard_map/ppermute | solution.py:87
  66.0 21.0 %collective-permute-start.18 = (bf16[3,320,128]{2,1,0:T(8,128)(2,1)S(1)}, bf16[3,320,128]{2,1,0:T(8,128)(2,1)S(1)}, u32[]{:S(2)}, u32[]{:S(2)}) collective-permute-start(bf16[3,320,128]{2,1,0:T(8,128)(2,1)S(1)} %broadcast_select_fusion.6.refs_11_), channel_id=1, source_target_pairs={{0,16},{1,17},{2,18},{3,19},{4,20},{5,21},{6,22},{7,23},{8,24},{9,... | collective-permute-start | bytes 737288 | tf_op jit(solution)/shard_map/ppermute | solution.py:87
  67.0 20.0 %collective-permute-start.17 = (bf16[3,320,128]{2,1,0:T(8,128)(2,1)S(1)}, bf16[3,320,128]{2,1,0:T(8,128)(2,1)S(1)}, u32[]{:S(2)}, u32[]{:S(2)}) collective-permute-start(bf16[3,320,128]{2,1,0:T(8,128)(2,1)S(1)} %broadcast_select_fusion.6.refs_11_), channel_id=1, source_target_pairs={{0,2},{1,3},{2,0},{3,1},{4,6},{5,7},{6,4},{7,5},{8,10},{9,11},{10,... | collective-permute-start | bytes 737288 | tf_op jit(solution)/shard_map/ppermute | solution.py:87
  68.6 2.5 %copy-start = (bf16[8,8,128,320]{2,3,1,0:T(8,128)(2,1)S(1)}, bf16[8,8,128,320]{2,3,1,0:T(8,128)(2,1)}, u32[]{:S(2)}) copy-start(bf16[8,8,128,320]{2,3,1,0:T(8,128)(2,1)} %param.5) | copy-start | bytes 15728644
  87.1 3.8 %collective-permute-start.23 = (bf16[3,320,128]{2,1,0:T(8,128)(2,1)S(1)}, bf16[3,320,128]{2,1,0:T(8,128)(2,1)S(1)}, u32[]{:S(2)}, u32[]{:S(2)}) collective-permute-start(bf16[3,320,128]{2,1,0:T(8,128)(2,1)S(1)} %get-tuple-element.27.refs_3_), channel_id=1, source_target_pairs={{0,1},{1,0},{2,3},{3,2},{4,5},{5,4},{6,7},{7,6},{8,9},{9,8},{10,11... | collective-permute-start | bytes 737288 | tf_op jit(solution)/shard_map/ppermute | solution.py:87
  88.0 6.3 %collective-permute-start.20 = (bf16[3,320,128]{2,1,0:T(8,128)(2,1)S(1)}, bf16[3,320,128]{2,1,0:T(8,128)(2,1)S(1)}, u32[]{:S(2)}, u32[]{:S(2)}) collective-permute-start(bf16[3,320,128]{2,1,0:T(8,128)(2,1)S(1)} %get-tuple-element.28.refs_0_), channel_id=1, source_target_pairs={{0,1},{1,0},{2,3},{3,2},{4,5},{5,4},{6,7},{7,6},{8,9},{9,8},{10,11... | collective-permute-start | bytes 737288 | tf_op jit(solution)/shard_map/ppermute | solution.py:87
  88.1 6.3 %collective-permute-start.21 = (bf16[3,320,128]{2,1,0:T(8,128)(2,1)S(1)}, bf16[3,320,128]{2,1,0:T(8,128)(2,1)S(1)}, u32[]{:S(2)}, u32[]{:S(2)}) collective-permute-start(bf16[3,320,128]{2,1,0:T(8,128)(2,1)S(1)} %get-tuple-element.29.refs_1_), channel_id=1, source_target_pairs={{0,1},{1,0},{2,3},{3,2},{4,5},{5,4},{6,7},{7,6},{8,9},{9,8},{10,11... | collective-permute-start | bytes 737288 | tf_op jit(solution)/shard_map/ppermute | solution.py:87
  88.5 5.9 %collective-permute-start.22 = (bf16[3,320,128]{2,1,0:T(8,128)(2,1)S(1)}, bf16[3,320,128]{2,1,0:T(8,128)(2,1)S(1)}, u32[]{:S(2)}, u32[]{:S(2)}) collective-permute-start(bf16[3,320,128]{2,1,0:T(8,128)(2,1)S(1)} %get-tuple-element.30.refs_2_), channel_id=1, source_target_pairs={{0,1},{1,0},{2,3},{3,2},{4,5},{5,4},{6,7},{7,6},{8,9},{9,8},{10,11... | collective-permute-start | bytes 737288 | tf_op jit(solution)/shard_map/ppermute | solution.py:87
  88.6 17.7 %collective-permute-start.25 = (bf16[8,1,320,128]{3,2,1,0:T(8,128)(2,1)S(1)}, bf16[8,1,320,128]{3,2,1,0:T(8,128)(2,1)S(1)}, u32[]{:S(2)}, u32[]{:S(2)}) collective-permute-start(bf16[8,1,320,128]{3,2,1,0:T(8,128)(2,1)S(1)} %get-tuple-element.16), channel_id=1, source_target_pairs={{1,0},{2,1},{3,2},{4,3},{5,4},{6,5},{7,6},{8,7},{9,8},{10,9},{11,1... | collective-permute-start | bytes 1966088 | tf_op jit(solution)/shard_map/ppermute | solution.py:247
  90.9 15.3 %collective-permute-start.24 = (bf16[8,1,320,128]{3,2,1,0:T(8,128)(2,1)S(1)}, bf16[8,1,320,128]{3,2,1,0:T(8,128)(2,1)S(1)}, u32[]{:S(2)}, u32[]{:S(2)}) collective-permute-start(bf16[8,1,320,128]{3,2,1,0:T(8,128)(2,1)S(1)} %get-tuple-element.18), channel_id=1, source_target_pairs={{0,1},{1,2},{2,3},{3,4},{4,5},{5,6},{6,7},{7,8},{8,9},{9,10},{10,1... | collective-permute-start | bytes 1966088 | tf_op jit(solution)/shard_map/ppermute | solution.py:246

commit v3 on v2

v3 whole, which is shorter than its diff:
```python
import functools

import jax
import jax.numpy as jnp
from jax import lax
from jax.experimental import pallas as pl
from jax.experimental.pallas import tpu as pltpu
from jax.sharding import PartitionSpec as P

momentum_decay = 0.9
learn_rate = 0.5
axes = ("groups", "dp")
lanes = 128
group = 4


def silu(v):
    half = v.astype(jnp.float32) * 0.5
    return (half * jnp.tanh(half) + half).astype(jnp.bfloat16)


def bits_of(ids, split):
    g, dp = ids[0], ids[1]
    return lax.rem(g, 2), lax.bitwise_and(lax.div(dp, split), 1), lax.bitwise_and(dp, 1)


def tile_pair(ids, kernel, step, splits):
    split = jnp.where(kernel == 0, splits[0], splits[1])
    half, bit, _ = bits_of(ids, split)
    return 2 * half + lax.bitwise_xor(bit, step)


def update_body(ids, owners, w_ref, m_ref, g_ref, *refs, depth, splits):
    kernel, step = pl.program_id(0), pl.program_id(1)
    core = lax.bitwise_and(ids[1], 1)
    taps, _, outs = w_ref.shape[1:]
    first = tile_pair(ids, kernel, step, splits) * 2 * lanes

    @pl.when(owners[kernel] == ids[1])
    def _():
        for tap in range(taps):
            velocity = momentum_decay * m_ref[0, tap] + g_ref[0, tap].astype(jnp.float32)
            fresh = w_ref[0, tap].astype(jnp.float32) - learn_rate * velocity
            at = first + lax.broadcasted_iota(jnp.int32, fresh.shape, 0)
            flipped = jnp.where(at < depth, fresh, 0.0).astype(jnp.bfloat16).T
            low, high = flipped[:, :lanes], flipped[:, lanes:]
            own = jnp.where(core == 0, low, high)
            other = jnp.where(core == 0, high, low)
            for at_step in range(2):

                @pl.when(step == at_step)
                def _():
                    refs[at_step][kernel, tap] = own
                    refs[2 + at_step][kernel, tap] = other


def update(ids, owners, weights, momentum, grads, splits):
    kernels, taps, depth, outs = weights.shape

    def which(k, i, ids, owners):
        last = (owners[1] == ids[1]).astype(jnp.int32)
        mine = owners[k] == ids[1]
        k = jnp.where(mine, k, last)
        return (k, 0, tile_pair(ids, k, jnp.where(mine, i, k * (1 - last)), splits), 0)

    block = pl.BlockSpec((1, taps, 2 * lanes, outs), which)
    shape = (kernels, taps, outs, lanes)
    return pl.pallas_call(
        functools.partial(update_body, depth=depth, splits=splits),
        grid_spec=pltpu.PrefetchScalarGridSpec(
            num_scalar_prefetch=2,
            grid=(kernels, 2),
            in_specs=[block] * 3,
            out_specs=[pl.BlockSpec(shape, lambda k, i, ids, owners: (0, 0, 0, 0))] * 4,
        ),
        out_shape=[jax.ShapeDtypeStruct(shape, jnp.bfloat16)] * 4,
        compiler_params=pltpu.CompilerParams(vmem_limit_bytes=57 * 2**20),
        name="kernel_update",
    )(ids, owners, weights, momentum, grads)


def swap(x, groups, count, change):
    pairs = []
    for g in range(groups):
        for d in range(count):
            to_g, to_d = change(g, d)
            pairs.append((g * count + d, to_g * count + to_d))
    return lax.ppermute(x, axes, pairs)


def after(x, other, owners):
    return jnp.where(owners[0] < 0, other, x)


def spread(pieces, owners, splits, groups, count, edges_after):
    differs = lax.bitwise_xor(lax.axis_index("dp"), owners)
    mine0, mine1, theirs0, theirs1 = pieces

    def swap_dp(x, bit):
        return swap(x, groups, count, lambda g, d: (g, d ^ bit))

    def keep(bit, own, got, kernel):
        return jnp.where(lax.bitwise_and(differs[kernel], bit) == 0, own, got)

    got1 = swap_dp(theirs1, 1)
    got0 = swap_dp(theirs0, 1)
    far = [keep(1, mine1[k], got1[k], k) for k in range(2)]
    near = [keep(1, mine0[k], got0[k], k) for k in range(2)]
    held = [keep(splits[k], near[k], swap_dp(far[k], splits[k]), k) for k in range(2)]
    edge_rows = edges_after(far[0])
    held[0] = after(held[0], edge_rows[1][: held[0].shape[0], 0], owners)
    high = [1 << b for b in range(3, count.bit_length() - 1)]
    turns = (high[::-1] + [4], [2] + high[::-1])
    for bits in zip(*turns):
        held[0] = after(held[0], held[1], owners)
        held = [keep(bits[k], held[k], swap_dp(held[k], bits[k]), k) for k in range(2)]
    return edge_rows, (after(held[0], held[1], owners), held[1])


def gather(piece, split, groups, count):
    def move(x, bit, group):
        return swap(x, groups, count, lambda g, d: (g ^ group, d ^ bit))

    return [piece, move(piece, split, 0), move(piece, 0, 1), move(piece, split, 1)]


def gather_cores(ring, groups, count):
    return ring + [swap(x, groups, count, lambda g, d: (g, d ^ 1)) for x in ring]


def mix(ids, split, piece_refs, mixed):
    half, bit, core = bits_of(ids, split)
    for relation, ref in enumerate(piece_refs):
        tile = (
            4 * lax.bitwise_xor(half, (relation >> 1) & 1)
            + 2 * lax.bitwise_xor(bit, relation & 1)
            + lax.bitwise_xor(core, relation >> 2)
        )
        at = pl.ds(pl.multiple_of(tile * lanes, lanes), lanes)
        outer = (ref[0].astype(jnp.float32) + ref[2].astype(jnp.float32)) * 0.5
        inner = ref[1].astype(jnp.float32) * 0.5
        mixed[0, :, at] = ref[0]
        mixed[1, :, at] = (outer + inner).astype(jnp.bfloat16)
        mixed[2, :, at] = (outer - inner).astype(jnp.bfloat16)
        mixed[3, :, at] = ref[2]


def put(shifted, slot, raws):
    for i, raw in enumerate(raws):
        shifted[slot, :, pl.ds(i * raw.shape[1], raw.shape[1])] = silu(raw)


def three_columns(field, cols):
    chans, width = field.shape
    lane = lax.broadcasted_iota(jnp.int32, (chans, cols), 1)
    zero = jnp.zeros((chans, cols), field.dtype)
    parts = [field[:, at : at + cols] for at in range(0, width, cols)]
    left = [jnp.where(lane == 0, zero, pltpu.roll(x, 1, 1)) for x in parts]
    right = [jnp.where(lane == cols - 1, zero, pltpu.roll(x, cols - 1, 1)) for x in parts]
    return jnp.concatenate(
        [jnp.concatenate(left, axis=1), field, jnp.concatenate(right, axis=1)], axis=0
    )


def two_rows(mixed, shifted, slot, cols=lanes):
    d = [shifted[slot + j] for j in range(4)]
    depth, step = 3 * shifted.shape[1], 2 * lanes

    def product(t, field):
        wide = three_columns(field, cols)
        parts = [slice(at, min(at + step, depth)) for at in range(0, depth, step)]
        return sum(
            jnp.dot(mixed[t, :, at], wide[at], preferred_element_type=jnp.float32) for at in parts
        )

    plus = product(1, d[1] + d[2])
    minus = product(2, d[2] - d[1])
    even = plus + minus + product(0, d[0] - d[2])
    odd = plus - minus - product(3, d[1] - d[3])
    return even, odd


def add(raw, branch, i):
    cols = raw.shape[1]
    return (raw.astype(jnp.float32) + branch[:, i * cols : (i + 1) * cols]).astype(jnp.bfloat16)


def whole_body(ids, *refs, split, count):
    *arrays, mixed, shifted = refs[8:11] + refs[-5:]
    pl.when(pl.program_id(0) == 0)(lambda: mix(ids, split, refs[:8], mixed))
    for pair in range(arrays[0].shape[0] // 2):
        parts = [x.at[2 * pair : 2 * pair + 2] for x in arrays]
        whole_pair(ids, *parts, mixed, shifted.at[pair], count=count)


def whole_pair(ids, x, core, outer, out, core_out, outer_out, mixed, shifted, *, count):
    n, rows = x.shape[:2]
    dp = ids[1]
    first_core = lax.bitwise_and(dp, 1) == 0

    def raw(row, i):
        if 0 <= row < rows:
            return x[i, row]
        ends = (outer[i, 0], core[i, 0]) if row < 0 else (core[i, 0], outer[i, 0])
        edge = jnp.where(first_core, *ends)
        inside = dp > 0 if row < 0 else dp < count - 1
        return jnp.where(inside, edge, jnp.zeros_like(edge))

    for row in range(-1, 3):
        put(shifted, row + 1, [raw(row, i) for i in range(n)])
    for block in range(rows // 2):
        if block + 1 < rows // 2:
            for row in (2 * block + 3, 2 * block + 4):
                put(shifted, row + 1, [raw(row, i) for i in range(n)])
        made = two_rows(mixed, shifted, 2 * block)
        for row, branch in zip((2 * block, 2 * block + 1), made):
            for i in range(n):
                result = add(x[i, row], branch, i)
                out[i, row] = result
                if row in (0, rows - 1):
                    facing = core_out, outer_out
                    for ref, faces in zip(facing, (~first_core, first_core)):

                        @pl.when(faces if row == 0 else ~faces)
                        def _():
                            ref[i, 0] = result


def near_body(ids, *refs, split, count):
    *arrays, mixed, shifted = refs[8:]
    pl.when(pl.program_id(0) == 0)(lambda: mix(ids, split, refs[:8], mixed))
    for pair in range(arrays[0].shape[0] // 2):
        parts = [x.at[2 * pair : 2 * pair + 2] for x in arrays]
        near_pair(ids, *parts, mixed, shifted.at[pair])


def near_pair(ids, x, core, out, mixed, shifted):
    n, rows = x.shape[:2]
    first_core = lax.bitwise_and(ids[1], 1) == 0
    last = rows // 2 - 1
    for row in range(5):
        put(shifted, row + 1, [x[i, row] for i in range(n)])
    for block in range(1, last + 1):
        at = block
        for row in range(2 * block + 3, min(2 * block + 5, rows)):
            put(shifted, row + 1, [x[i, row] for i in range(n)])
        if block == last - 1:
            put(shifted, jnp.where(first_core, rows + 1, 0), [core[i, 0] for i in range(n)])
        if block == last:
            at = jnp.where(first_core, last, 0)
        for step, branch in enumerate(two_rows(mixed, shifted, 2 * at)):
            for i in range(n):
                out[i, 2 * at + step] = add(x[i, 2 * at + step], branch, i)


def far_body(ids, *refs, split, count):
    x, outer, _, out, mixed, shifted = refs[8:]
    pl.when(pl.program_id(0) == 0)(lambda: mix(ids, split, refs[:8], mixed))
    for pair in range(x.shape[0] // 2):
        parts = [x.at[2 * pair : 2 * pair + 2] for x in (x, outer, out)]
        far_pair(ids, *parts, mixed, shifted.at[pair], count=count)


def far_pair(ids, x, outer, out, mixed, shifted, *, count):
    n, rows = x.shape[:2]
    dp = ids[1]
    first_core = lax.bitwise_and(dp, 1) == 0
    inside = jnp.where(first_core, dp > 0, dp < count - 1)
    near = jnp.where(first_core, 0, rows - 2)
    edge = [jnp.where(inside, outer[i, 0], jnp.zeros_like(outer[i, 0])) for i in range(n)]
    put(shifted, 0, [jnp.where(first_core, edge[i], x[i, rows - 3]) for i in range(n)])
    put(shifted, 1, [x[i, near] for i in range(n)])
    put(shifted, 2, [x[i, near + 1] for i in range(n)])
    put(shifted, 3, [jnp.where(first_core, x[i, 2], edge[i]) for i in range(n)])
    for step, branch in enumerate(two_rows(mixed, shifted, 0)):
        for i in range(n):
            out[i, step] = add(x[i, near + step], branch, i)


def conv_call(body, ids, split, count, pieces, operands, specs, outs, out_specs, share, limit, **more):
    images, rows, chans, cols = operands[0].shape
    return pl.pallas_call(
        functools.partial(body, split=split, count=count),
        grid_spec=pltpu.PrefetchScalarGridSpec(
            num_scalar_prefetch=1,
            grid=(images // group,),
            in_specs=[pl.BlockSpec(pieces[0].shape, lambda i, ids: (0, 0, 0))] * 8 + specs,
            out_specs=out_specs,
            scratch_shapes=[
                pltpu.VMEM((4, chans, 8 * lanes), jnp.bfloat16),
                pltpu.VMEM((group // 2, rows + 2, chans, 2 * cols), jnp.bfloat16),
            ],
        ),
        out_shape=[jax.ShapeDtypeStruct((images, x, chans, cols), jnp.bfloat16) for x in outs],
        compiler_params=pltpu.CompilerParams(vmem_limit_bytes=limit * 2**20),
        cost_estimate=pl.CostEstimate(
            flops=share * 2 * images * rows * cols * 9 * chans * chans // 4,
            bytes_accessed=4 * images * rows * cols * chans,
            transcendentals=images * rows * cols * chans,
        ),
        name="residual_conv",
        **more,
    )(ids, *pieces, *operands)


def strip(field, height, block=None):
    shape = (group, height) + field.shape[2:]
    if block is None:
        return pl.BlockSpec(shape, lambda i, ids: (i, 0, 0, 0))
    return pl.BlockSpec(shape, lambda i, ids: (i, lax.bitwise_and(ids[1], 1) * block, 0, 0))


def edges_body(ids, x, _, held, core_out, outer_out):
    rows = x.shape[1]
    first_core = lax.bitwise_and(ids[1], 1) == 0
    held[...] = x[...]
    core_out[:, 0] = x[:, jnp.where(first_core, rows - 1, 0)]
    outer_out[:, 0] = x[:, jnp.where(first_core, 0, rows - 1)]


def edges(ids, field, wait):
    images, rows, chans, cols = field.shape
    whole, edge = strip(field, rows), strip(field, 1)
    return pl.pallas_call(
        edges_body,
        grid_spec=pltpu.PrefetchScalarGridSpec(
            num_scalar_prefetch=1,
            grid=(images // group,),
            in_specs=[whole, pl.BlockSpec(memory_space=pl.ANY)],
            out_specs=[whole, edge, edge],
        ),
        out_shape=[
            jax.ShapeDtypeStruct((images, x, chans, cols), field.dtype) for x in (rows, 1, 1)
        ],
        compiler_params=pltpu.CompilerParams(vmem_limit_bytes=28 * 2**20),
        cost_estimate=pl.CostEstimate(
            flops=0, bytes_accessed=4 * images * rows * cols * chans, transcendentals=0
        ),
        name="edge_rows",
    )(ids, field, wait)


def borders(core, outer, groups, count):
    def across(g, d):
        to = d + (1 if d % 2 else -1)
        return g, to if 0 <= to < count else d

    return swap(core, groups, count, lambda g, d: (g, d ^ 1)), swap(outer, groups, count, across)


def local(groups, count, images, kernel_weights, kernel_momentum, kernel_grads, owners):
    g, dp = lax.axis_index("groups"), lax.axis_index("dp")
    splits = (2, 4)
    ids = jnp.stack([g, dp]).astype(jnp.int32)

    def flat(x):
        _, kernels, taps, across, ins, outs = x.shape
        return x.reshape(kernels, taps, across * ins, outs)

    state = [flat(x) for x in (kernel_weights, kernel_momentum, kernel_grads)]
    field = jnp.swapaxes(images, 2, 3)
    rows = field.shape[1]
    assert rows % 4 == 0 and rows >= 8
    fresh = update(ids, owners, *state, splits)
    (field, core, outer), (one, two) = spread(
        fresh, owners, splits, groups, count, functools.partial(edges, ids, field)
    )
    core, outer = borders(core, outer, groups, count)
    ring = gather(one, splits[0], groups, count)
    first = gather_cores(ring, groups, count)
    two = after(two, ring[3], owners)
    ring = gather(two, splits[1], groups, count)

    whole, edge, anywhere = strip(field, rows), strip(field, 1), pl.BlockSpec(memory_space=pl.ANY)
    hidden, core, outer = conv_call(
        whole_body,
        ids,
        splits[0],
        count,
        first,
        (field, core, outer, two),
        [whole, edge, edge, anywhere],
        (rows, 1, 1),
        [whole, edge, edge],
        4,
        28,
    )
    ring = [after(x, core[: x.shape[0], 0], owners) for x in ring]
    second = gather_cores(ring, groups, count)
    core, outer = borders(core, outer, groups, count)
    (out,) = conv_call(
        near_body,
        ids,
        splits[1],
        count,
        second,
        (hidden, core),
        [whole, edge],
        (rows,),
        [whole],
        3,
        28,
    )
    (out,) = conv_call(
        far_body,
        ids,
        splits[1],
        count,
        second,
        (hidden, outer, out),
        [strip(field, rows // 2, 1), edge, anywhere],
        (rows,),
        [strip(field, 2, rows // 2 - 1)],
        1,
        28,
        input_output_aliases={11: 0},
    )
    return jnp.swapaxes(out, 2, 3)


def solution(mesh):
    groups, count = mesh.shape["groups"], mesh.shape["dp"]
    assert groups % 2 == 0 and count % 8 == 0 and count & (count - 1) == 0
    state = P("dp", None, None, None, None, None)
    return jax.shard_map(
        functools.partial(local, groups, count),
        mesh=mesh,
        in_specs=(P("groups", "dp", None, None), state, state, state, P()),
        out_specs=P("groups", "dp", None, None),
        check_vma=False,
    )
```

time: 118 us -> 113 us (0.958)
  starting transfers between devices: 39.4 us -> 29.3 us
  waiting for transfers between devices: 24.7 us -> 31 us
  local copies, waits for them, and re-layouts: 4.45 us -> 0.61 us
  Pallas kernels: 40.5 us -> 44.1 us
    ppermute x4 -> x0, starting transfers between devices: 13.2 us -> none  [the longest x2 6.95 us: borders(): down = lax.ppermute(top, 'dp', [(i + 1, i) for i in range(count - 1)])]
    ppermute x22 -> x26, waiting for transfers between devices: 22.6 us -> 31 us  [swap(): return lax.ppermute(x, axes, pairs)]
    ppermute x22 -> x26, starting transfers between devices: 26.2 us -> 29.3 us  [swap(): return lax.ppermute(x, axes, pairs)]
    pallas_call x1, Pallas kernels: 3.81 us -> 6.38 us  [update(): pl.pallas_call(functools.partial(update_body, depth=depth, splits=splits)...]
    unnamed x6 -> x8, local copies, waits for them, and re-layouts: 2.49 us -> 0.01 us
    ppermute x4 -> x0, waiting for transfers between devices: 2.14 us -> none  [the longest x2 2.13 us: borders(): up = lax.ppermute(bottom, 'dp', [(i, i + 1) for i in range(count - 1)])]
    slice x1 -> x0, local copies, waits for them, and re-layouts: 1.37 us -> none  [local(): up, down = borders(field[:, :1], field[:, -1:], count)]
    pallas_call x3 -> x4, Pallas kernels: 36.7 us -> 37.7 us  [the longest x3 36.7 us: conv_call(): pl.pallas_call(functools.partial(body, split=split, count=count), grid_sp...]
  transfers between devices with their start and end apart: 26 -> 26, of which waited for: 6 -> 9; matrix products, arithmetic and copies ran while one was open for 3% -> 2% of each run, Pallas kernels for 22% -> 28%
where the time goes in v3:
time: 113 us; the launch traced here: 112 us
  Pallas kernels  44.1 us (39%)
  waiting for transfers between devices  31 us (27%)
  starting transfers between devices  29.3 us (26%)
  between operations  5.15 us (5%)
  other arithmetic  2.04 us (2%)
    pallas_call x3, Pallas kernels, conv_call(): pl.pallas_call(functools.partial(body, split=split, count=count), grid_sp...  36.7 us
    ppermute x26, waiting for transfers between devices, swap(): return lax.ppermute(x, axes, pairs)  31 us
    ppermute x26, starting transfers between devices, swap(): return lax.ppermute(x, axes, pairs)  29.3 us
    pallas_call x1, Pallas kernels, update(): pl.pallas_call(functools.partial(update_body, depth=depth, splits=splits)...  6.38 us
  transfers between devices with their start and end apart: 26, of which 9 were waited for; matrix products, arithmetic and copies ran while one was open for 2% of the time, Pallas kernels for 28%

profile of v3, /device:TPU:1, one launch (start us, length us, event | category | flops | bytes accessed | tf_op | source)
XLA Modules:
  0.0 112.2 jit_solution(14911196902376709236)
XLA Ops:
  0.0 0.6 pad_add_fusion.ids
  0.6 6.4 %kernel_update.1 = (bf16[2,3,320,128]{3,2,1,0:T(8,128)(2,1)}, bf16[2,3,320,128]{3,2,1,0:T(8,128)(2,1)}, bf16[2,3,320,128]{3,2,1,0:T(8,128)(2,1)}, bf16[2,3,320,128]{3,2,1,0:T(8,128)(2,1)}) custom-call(s32[2]{0:T(128)} %pad_add_fusion.ids, s32[2]{0:T(128)} %owners.1, bf16[2,3,960,320]{3,2,1,0:T(8,128)(2,1)} %bitcast.54, f32[2,3,960,320]{3,2,1,0:T(8,128)} %bitcast.53, ...), custom_call_target="tpu_custom_call" | custom-call | tf_op jit(solution)/shard_map/kernel_update/pallas_call | solution.py:68
  7.0 0.0 collective-permute-start.1
  7.0 0.5 collective-permute-start
  7.5 0.0 copy-done.3
  7.5 0.6 fusion.9
  9.3 0.0 collective-permute-done.1
  9.3 1.2 %fusion.5 = (bf16[3,320,128]{2,1,0:T(8,128)(2,1)S(1)}, bf16[3,320,128]{2,1,0:T(8,128)(2,1)S(1)}) fusion(bf16[2,3,320,128]{3,2,1,0:T(8,128)(2,1)S(1)} %collective-permute-done.1, bf16[2,3,320,128]{3,2,1,0:T(8,128)(2,1)} %get-tuple-element.17, pred[]{:T(512)} %bitcast.6, pred[]{:T(512)} %bitcast.15), kind=kLoop, calls=%fused_computation.10 | loop fusion | flops 245760 | bytes 1474562 | tf_op jit(solution)/shard_map/jit(_where)/select_n | solution.py:103
  10.5 0.3 collective-permute-start.2
  10.8 3.5 %collective-permute-start.5 = (bf16[3,320,128]{2,1,0:T(8,128)(2,1)S(1)}, bf16[3,320,128]{2,1,0:T(8,128)(2,1)S(1)}, u32[]{:S(2)}, u32[]{:S(2)}) collective-permute-start(bf16[3,320,128]{2,1,0:T(8,128)(2,1)S(1)} %get-tuple-element.30._), channel_id=1, source_target_pairs={{0,2},{1,3},{2,0},{3,1},{4,6},{5,7},{6,4},{7,5},{8,10},{9,11},{10,... | collective-permute-start | bytes 737288 | tf_op jit(solution)/shard_map/ppermute | solution.py:88
  15.5 1.0 edge_rows.1
  16.6 0.0 collective-permute-done
  16.6 1.5 %collective-permute-done.2 = bf16[3,320,128]{2,1,0:T(8,128)(2,1)S(1)} collective-permute-done((bf16[3,320,128]{2,1,0:T(8,128)(2,1)S(1)}, bf16[3,320,128]{2,1,0:T(8,128)(2,1)S(1)}, u32[]{:S(2)}, u32[]{:S(2)}) %collective-permute-start.2) | collective-permute-done | bytes 245792 | tf_op jit(solution)/shard_map/ppermute | solution.py:88
  18.1 1.8 %collective-permute-done.5 = bf16[3,320,128]{2,1,0:T(8,128)(2,1)S(1)} collective-permute-done((bf16[3,320,128]{2,1,0:T(8,128)(2,1)S(1)}, bf16[3,320,128]{2,1,0:T(8,128)(2,1)S(1)}, u32[]{:S(2)}, u32[]{:S(2)}) %collective-permute-start.5) | collective-permute-done | bytes 245792 | tf_op jit(solution)/shard_map/ppermute | solution.py:88
  19.9 0.1 fusion.3
  20.0 0.1 collective-permute-start.6
  20.0 1.2 %collective-permute-start.3 = (bf16[3,320,128]{2,1,0:T(8,128)(2,1)S(1)}, bf16[3,320,128]{2,1,0:T(8,128)(2,1)S(1)}, u32[]{:S(2)}, u32[]{:S(2)}) collective-permute-start(bf16[3,320,128]{2,1,0:T(8,128)(2,1)S(1)} %get-tuple-element.28), channel_id=1, source_target_pairs={{0,2},{1,3},{2,0},{3,1},{4,6},{5,7},{6,4},{7,5},{8,10},{9,11},{10,... | collective-permute-start | bytes 737288 | tf_op jit(solution)/shard_map/ppermute | solution.py:88
  22.5 11.5 %collective-permute-done.6 = bf16[3,320,128]{2,1,0:T(8,128)(2,1)S(1)} collective-permute-done((bf16[3,320,128]{2,1,0:T(8,128)(2,1)S(1)}, bf16[3,320,128]{2,1,0:T(8,128)(2,1)S(1)}, u32[]{:S(2)}, u32[]{:S(2)}) %collective-permute-start.6) | collective-permute-done | bytes 245792 | tf_op jit(solution)/shard_map/ppermute | solution.py:88
  33.9 0.0 collective-permute-done.3
  33.9 0.1 select_select_fusion.1
  34.0 0.1 collective-permute-start.7
  34.1 0.1 collective-permute-start.4
  34.2 4.4 %collective-permute-start.16 = (bf16[8,1,320,128]{3,2,1,0:T(8,128)(2,1)S(1)}, bf16[8,1,320,128]{3,2,1,0:T(8,128)(2,1)S(1)}, u32[]{:S(2)}, u32[]{:S(2)}) collective-permute-start(bf16[8,1,320,128]{3,2,1,0:T(8,128)(2,1)S(1)} %get-tuple-element.21), channel_id=1, source_target_pairs={{0,0},{1,2},{2,1},{3,4},{4,3},{5,6},{6,5},{7,8},{8,7},{9,10},{10,9... | collective-permute-start | bytes 1966088 | tf_op jit(solution)/shard_map/ppermute | solution.py:88
  39.8 0.1 collective-permute-start.15
  39.9 4.4 %collective-permute-done.7 = bf16[3,320,128]{2,1,0:T(8,128)(2,1)S(1)} collective-permute-done((bf16[3,320,128]{2,1,0:T(8,128)(2,1)S(1)}, bf16[3,320,128]{2,1,0:T(8,128)(2,1)S(1)}, u32[]{:S(2)}, u32[]{:S(2)}) %collective-permute-start.7) | collective-permute-done | bytes 245792 | tf_op jit(solution)/shard_map/ppermute | solution.py:88
  44.3 3.0 %collective-permute-done.4 = bf16[3,320,128]{2,1,0:T(8,128)(2,1)S(1)} collective-permute-done((bf16[3,320,128]{2,1,0:T(8,128)(2,1)S(1)}, bf16[3,320,128]{2,1,0:T(8,128)(2,1)S(1)}, u32[]{:S(2)}, u32[]{:S(2)}) %collective-permute-start.4) | collective-permute-done | bytes 245792 | tf_op jit(solution)/shard_map/ppermute | solution.py:88
  47.3 1.8 %collective-permute-start.10 = (bf16[3,320,128]{2,1,0:T(8,128)(2,1)S(1)}, bf16[3,320,128]{2,1,0:T(8,128)(2,1)S(1)}, u32[]{:S(2)}, u32[]{:S(2)}) collective-permute-start(bf16[3,320,128]{2,1,0:T(8,128)(2,1)S(1)} %select_select_fusion.refs_0_), channel_id=1, source_target_pairs={{0,18},{1,19},{2,16},{3,17},{4,22},{5,23},{6,20},{7,21},{8,26},{9,... | collective-permute-start | bytes 737288 | tf_op jit(solution)/shard_map/ppermute | solution.py:88
  49.1 0.6 collective-permute-start.9
  49.8 0.3 collective-permute-start.8
  50.1 0.0 collective-permute-done.16.refs_10_
  50.1 2.4 %collective-permute-start.11 = (bf16[3,320,128]{2,1,0:T(8,128)(2,1)S(1)}, bf16[3,320,128]{2,1,0:T(8,128)(2,1)S(1)}, u32[]{:S(2)}, u32[]{:S(2)}) collective-permute-start(bf16[3,320,128]{2,1,0:T(8,128)(2,1)S(1)} %select_select_fusion.refs_0_), channel_id=1, source_target_pairs={{0,1},{1,0},{2,3},{3,2},{4,5},{5,4},{6,7},{7,6},{8,9},{9,8},{10,11... | collective-permute-start | bytes 737288 | tf_op jit(solution)/shard_map/ppermute | solution.py:88
  52.4 3.8 %collective-permute-done.10.refs_3_ = bf16[3,320,128]{2,1,0:T(8,128)(2,1)S(1)} collective-permute-done((bf16[3,320,128]{2,1,0:T(8,128)(2,1)S(1)}, bf16[3,320,128]{2,1,0:T(8,128)(2,1)S(1)}, u32[]{:S(2)}, u32[]{:S(2)}) %collective-permute-start.10) | collective-permute-done | bytes 245792 | tf_op jit(solution)/shard_map/ppermute | solution.py:88
  56.2 3.4 %collective-permute-start.14 = (bf16[3,320,128]{2,1,0:T(8,128)(2,1)S(1)}, bf16[3,320,128]{2,1,0:T(8,128)(2,1)S(1)}, u32[]{:S(2)}, u32[]{:S(2)}) collective-permute-start(bf16[3,320,128]{2,1,0:T(8,128)(2,1)S(1)} %collective-permute-done.10.refs_3_), channel_id=1, source_target_pairs={{0,1},{1,0},{2,3},{3,2},{4,5},{5,4},{6,7},{7,6},{8,9},{9,8},{10,11... | collective-permute-start | bytes 737288 | tf_op jit(solution)/shard_map/ppermute | solution.py:88
  59.6 3.2 %collective-permute-done.9.refs_2_ = bf16[3,320,128]{2,1,0:T(8,128)(2,1)S(1)} collective-permute-done((bf16[3,320,128]{2,1,0:T(8,128)(2,1)S(1)}, bf16[3,320,128]{2,1,0:T(8,128)(2,1)S(1)}, u32[]{:S(2)}, u32[]{:S(2)}) %collective-permute-start.9) | collective-permute-done | bytes 245792 | tf_op jit(solution)/shard_map/ppermute | solution.py:88
  62.9 1.9 %collective-permute-start.13 = (bf16[3,320,128]{2,1,0:T(8,128)(2,1)S(1)}, bf16[3,320,128]{2,1,0:T(8,128)(2,1)S(1)}, u32[]{:S(2)}, u32[]{:S(2)}) collective-permute-start(bf16[3,320,128]{2,1,0:T(8,128)(2,1)S(1)} %collective-permute-done.9.refs_2_), channel_id=1, source_target_pairs={{0,1},{1,0},{2,3},{3,2},{4,5},{5,4},{6,7},{7,6},{8,9},{9,8},{10,11... | collective-permute-start | bytes 737288 | tf_op jit(solution)/shard_map/ppermute | solution.py:88
  64.8 0.0 collective-permute-done.8.refs_1_
  64.8 0.0 collective-permute-start.12
  64.8 0.0 collective-permute-done.15.refs_9_
  64.8 2.0 %collective-permute-start.19 = (bf16[3,320,128]{2,1,0:T(8,128)(2,1)S(1)}, bf16[3,320,128]{2,1,0:T(8,128)(2,1)S(1)}, u32[]{:S(2)}, u32[]{:S(2)}) collective-permute-start(bf16[3,320,128]{2,1,0:T(8,128)(2,1)S(1)} %broadcast_select_fusion.5.refs_11_), channel_id=1, source_target_pairs={{0,20},{1,21},{2,22},{3,23},{4,16},{5,17},{6,18},{7,19},{8,28},{9,... | collective-permute-start | bytes 737288 | tf_op jit(solution)/shard_map/ppermute | solution.py:88
  66.9 0.0 collective-permute-done.11.refs_4_
  66.9 0.6 collective-permute-start.18
  67.5 0.0 collective-permute-done.14.refs_7_
  67.5 0.1 collective-permute-start.17
  67.6 0.0 collective-permute-done.13.refs_6_
  67.6 0.0 collective-permute-done.12.refs_5_
  67.6 16.6 %residual_conv.3 = (bf16[8,8,320,128]{3,2,1,0:T(8,128)(2,1)S(1)}, bf16[8,1,320,128]{3,2,1,0:T(8,128)(2,1)S(1)}, bf16[8,1,320,128]{3,2,1,0:T(8,128)(2,1)S(1)}) custom-call(s32[2]{0:T(128)S(1)} %copy-done.1, bf16[3,320,128]{2,1,0:T(8,128)(2,1)S(1)} %select_select_fusion.refs_0_, bf16[3,320,128]{2,1,0:T(8,128)(2,1)S(1)} %collective-permute-done.8.refs_1_, ...), custom_call_target="tpu_custom_call" | custom-call | flops 15099494400 | bytes 10485760 | tf_op jit(solution)/shard_map/residual_conv/pallas_call | solution.py:282
  84.2 1.4 %collective-permute-start.25 = (bf16[8,1,320,128]{3,2,1,0:T(8,128)(2,1)S(1)}, bf16[8,1,320,128]{3,2,1,0:T(8,128)(2,1)S(1)}, u32[]{:S(2)}, u32[]{:S(2)}) collective-permute-start(bf16[8,1,320,128]{3,2,1,0:T(8,128)(2,1)S(1)} %get-tuple-element.22), channel_id=1, source_target_pairs={{0,1},{1,0},{2,3},{3,2},{4,5},{5,4},{6,7},{7,6},{8,9},{9,8},{10,11... | collective-permute-start | bytes 1966088 | tf_op jit(solution)/shard_map/ppermute | solution.py:88
  85.6 0.0 collective-permute-done.19
  85.6 0.0 collective-permute-done.18
  85.6 0.0 collective-permute-done.17
  85.6 0.1 broadcast_select_fusion.6
  85.7 0.1 collective-permute-start.23
  85.8 0.5 collective-permute-start.20
  86.3 0.1 collective-permute-start.21
  86.4 0.4 collective-permute-start.22
  86.8 0.9 collective-permute-done.23.refs_7_
  87.7 3.5 %collective-permute-start.24 = (bf16[8,1,320,128]{3,2,1,0:T(8,128)(2,1)S(1)}, bf16[8,1,320,128]{3,2,1,0:T(8,128)(2,1)S(1)}, u32[]{:S(2)}, u32[]{:S(2)}) collective-permute-start(bf16[8,1,320,128]{3,2,1,0:T(8,128)(2,1)S(1)} %get-tuple-element.24), channel_id=1, source_target_pairs={{0,0},{1,2},{2,1},{3,4},{4,3},{5,6},{6,5},{7,8},{8,7},{9,10},{10,9... | collective-permute-start | bytes 1966088 | tf_op jit(solution)/shard_map/ppermute | solution.py:88
  91.2 0.0 collective-permute-done.20.refs_4_
  91.3 0.0 collective-permute-done.21.refs_5_
  91.3 0.0 collective-permute-done.22.refs_6_
  91.3 0.0 collective-permute-done.25.refs_9_
  91.3 13.5 %residual_conv.4.refs_10_ = bf16[8,8,320,128]{3,2,1,0:T(8,128)(2,1)} custom-call(s32[2]{0:T(128)S(1)} %copy-done.1, bf16[3,320,128]{2,1,0:T(8,128)(2,1)S(1)} %get-tuple-element.32.refs_0_, bf16[3,320,128]{2,1,0:T(8,128)(2,1)S(1)} %get-tuple-element.33.refs_1_, bf16[3,320,128]{2,1,0:T(8,128)(2,1)S(1)} %get-tuple-element.34.refs_2_, ...), custom_call_target="tpu_custom_call" | custom-call | flops 11324620800 | bytes 10485760 | tf_op jit(solution)/shard_map/residual_conv/pallas_call | solution.py:282
  104.8 0.8 collective-permute-done.24.refs_9_
  105.6 6.6 %residual_conv.5 = bf16[8,8,320,128]{3,2,1,0:T(8,128)(2,1)} custom-call(s32[2]{0:T(128)S(1)} %copy-done.1, bf16[3,320,128]{2,1,0:T(8,128)(2,1)S(1)} %get-tuple-element.32.refs_0_, bf16[3,320,128]{2,1,0:T(8,128)(2,1)S(1)} %get-tuple-element.33.refs_1_, bf16[3,320,128]{2,1,0:T(8,128)(2,1)S(1)} %get-tuple-element.34.refs_2_, ...), custom_call_target="tpu_custom_call", output_to_operand_aliasing={{}: (11, {})} | custom-call | flops 3774873600 | bytes 10485760 | tf_op jit(solution)/shard_map/residual_conv/pallas_call | solution.py:282
  (10 shorter events, 0.1 us)
Async XLA Ops:
  0.6 6.9 %copy-start.3 = (s32[2]{0:T(128)S(1)}, s32[2]{0:T(128)}, u32[]{:S(2)}) copy-start(s32[2]{0:T(128)} %owners.1) | copy-start | bytes 28
  0.6 14.9 %copy-start = (bf16[8,8,128,320]{2,3,1,0:T(8,128)(2,1)S(1)}, bf16[8,8,128,320]{2,3,1,0:T(8,128)(2,1)}, u32[]{:S(2)}) copy-start(bf16[8,8,128,320]{2,3,1,0:T(8,128)(2,1)} %param.5) | copy-start | bytes 15728644
  0.6 14.9 %copy-start.1 = (s32[2]{0:T(128)S(1)}, s32[2]{0:T(128)}, u32[]{:S(2)}) copy-start(s32[2]{0:T(128)} %pad_add_fusion.ids) | copy-start | bytes 28
  7.0 12.9 %copy-start.2 = (bf16[2,3,320,128]{3,2,1,0:T(8,128)(2,1)S(1)}, bf16[2,3,320,128]{3,2,1,0:T(8,128)(2,1)}, u32[]{:S(2)}) copy-start(bf16[2,3,320,128]{3,2,1,0:T(8,128)(2,1)} %get-tuple-element.15) | copy-start | bytes 1474564
  7.0 2.3 %collective-permute-start.1 = (bf16[2,3,320,128]{3,2,1,0:T(8,128)(2,1)}, bf16[2,3,320,128]{3,2,1,0:T(8,128)(2,1)S(1)}, u32[]{:S(2)}, u32[]{:S(2)}) collective-permute-start(bf16[2,3,320,128]{3,2,1,0:T(8,128)(2,1)} %get-tuple-element.18), channel_id=1, source_target_pairs={{0,1},{1,0},{2,3},{3,2},{4,5},{5,4},{6,7},{7,6},{8,9},{9,8},{10,11... | collective-permute-start | bytes 1474568 | tf_op jit(solution)/shard_map/ppermute | solution.py:88
  7.0 9.6 %collective-permute-start = (bf16[2,3,320,128]{3,2,1,0:T(8,128)(2,1)}, bf16[2,3,320,128]{3,2,1,0:T(8,128)(2,1)S(1)}, u32[]{:S(2)}, u32[]{:S(2)}) collective-permute-start(bf16[2,3,320,128]{3,2,1,0:T(8,128)(2,1)} %get-tuple-element.16), channel_id=1, source_target_pairs={{0,1},{1,0},{2,3},{3,2},{4,5},{5,4},{6,7},{7,6},{8,9},{9,8},{10,11... | collective-permute-start | bytes 1474568 | tf_op jit(solution)/shard_map/ppermute | solution.py:88
  10.5 7.6 %collective-permute-start.2 = (bf16[3,320,128]{2,1,0:T(8,128)(2,1)S(1)}, bf16[3,320,128]{2,1,0:T(8,128)(2,1)S(1)}, u32[]{:S(2)}, u32[]{:S(2)}) collective-permute-start(bf16[3,320,128]{2,1,0:T(8,128)(2,1)S(1)} %get-tuple-element.29), channel_id=1, source_target_pairs={{0,4},{1,5},{2,6},{3,7},{4,0},{5,1},{6,2},{7,3},{8,12},{9,13},{10,... | collective-permute-start | bytes 737288 | tf_op jit(solution)/shard_map/ppermute | solution.py:88
  10.8 9.1 %collective-permute-start.5 = (bf16[3,320,128]{2,1,0:T(8,128)(2,1)S(1)}, bf16[3,320,128]{2,1,0:T(8,128)(2,1)S(1)}, u32[]{:S(2)}, u32[]{:S(2)}) collective-permute-start(bf16[3,320,128]{2,1,0:T(8,128)(2,1)S(1)} %get-tuple-element.30._), channel_id=1, source_target_pairs={{0,2},{1,3},{2,0},{3,1},{4,6},{5,7},{6,4},{7,5},{8,10},{9,11},{10,... | collective-permute-start | bytes 737288 | tf_op jit(solution)/shard_map/ppermute | solution.py:88
  20.0 14.0 %collective-permute-start.6 = (bf16[3,320,128]{2,1,0:T(8,128)(2,1)S(1)}, bf16[3,320,128]{2,1,0:T(8,128)(2,1)S(1)}, u32[]{:S(2)}, u32[]{:S(2)}) collective-permute-start(bf16[3,320,128]{2,1,0:T(8,128)(2,1)S(1)} %get-tuple-element.27), channel_id=1, source_target_pairs={{0,8},{1,9},{2,10},{3,11},{4,12},{5,13},{6,14},{7,15},{8,0},{9,1},... | collective-permute-start | bytes 737288 | tf_op jit(solution)/shard_map/ppermute | solution.py:88
  20.0 13.9 %collective-permute-start.3 = (bf16[3,320,128]{2,1,0:T(8,128)(2,1)S(1)}, bf16[3,320,128]{2,1,0:T(8,128)(2,1)S(1)}, u32[]{:S(2)}, u32[]{:S(2)}) collective-permute-start(bf16[3,320,128]{2,1,0:T(8,128)(2,1)S(1)} %get-tuple-element.28), channel_id=1, source_target_pairs={{0,2},{1,3},{2,0},{3,1},{4,6},{5,7},{6,4},{7,5},{8,10},{9,11},{10,... | collective-permute-start | bytes 737288 | tf_op jit(solution)/shard_map/ppermute | solution.py:88
  34.0 10.3 %collective-permute-start.7 = (bf16[3,320,128]{2,1,0:T(8,128)(2,1)S(1)}, bf16[3,320,128]{2,1,0:T(8,128)(2,1)S(1)}, u32[]{:S(2)}, u32[]{:S(2)}) collective-permute-start(bf16[3,320,128]{2,1,0:T(8,128)(2,1)S(1)} %get-tuple-element.25), channel_id=1, source_target_pairs={{0,4},{1,5},{2,6},{3,7},{4,0},{5,1},{6,2},{7,3},{8,12},{9,13},{10,... | collective-permute-start | bytes 737288 | tf_op jit(solution)/shard_map/ppermute | solution.py:88
  34.1 13.2 %collective-permute-start.4 = (bf16[3,320,128]{2,1,0:T(8,128)(2,1)S(1)}, bf16[3,320,128]{2,1,0:T(8,128)(2,1)S(1)}, u32[]{:S(2)}, u32[]{:S(2)}) collective-permute-start(bf16[3,320,128]{2,1,0:T(8,128)(2,1)S(1)} %get-tuple-element.26), channel_id=1, source_target_pairs={{0,8},{1,9},{2,10},{3,11},{4,12},{5,13},{6,14},{7,15},{8,0},{9,1},... | collective-permute-start | bytes 737288 | tf_op jit(solution)/shard_map/ppermute | solution.py:88
  34.2 15.9 %collective-permute-start.16 = (bf16[8,1,320,128]{3,2,1,0:T(8,128)(2,1)S(1)}, bf16[8,1,320,128]{3,2,1,0:T(8,128)(2,1)S(1)}, u32[]{:S(2)}, u32[]{:S(2)}) collective-permute-start(bf16[8,1,320,128]{3,2,1,0:T(8,128)(2,1)S(1)} %get-tuple-element.21), channel_id=1, source_target_pairs={{0,0},{1,2},{2,1},{3,4},{4,3},{5,6},{6,5},{7,8},{8,7},{9,10},{10,9... | collective-permute-start | bytes 1966088 | tf_op jit(solution)/shard_map/ppermute | solution.py:88
  39.8 25.0 %collective-permute-start.15 = (bf16[8,1,320,128]{3,2,1,0:T(8,128)(2,1)S(1)}, bf16[8,1,320,128]{3,2,1,0:T(8,128)(2,1)S(1)}, u32[]{:S(2)}, u32[]{:S(2)}) collective-permute-start(bf16[8,1,320,128]{3,2,1,0:T(8,128)(2,1)S(1)} %get-tuple-element.19), channel_id=1, source_target_pairs={{0,1},{1,0},{2,3},{3,2},{4,5},{5,4},{6,7},{7,6},{8,9},{9,8},{10,11... | collective-permute-start | bytes 1966088 | tf_op jit(solution)/shard_map/ppermute | solution.py:88
  47.3 8.9 %collective-permute-start.10 = (bf16[3,320,128]{2,1,0:T(8,128)(2,1)S(1)}, bf16[3,320,128]{2,1,0:T(8,128)(2,1)S(1)}, u32[]{:S(2)}, u32[]{:S(2)}) collective-permute-start(bf16[3,320,128]{2,1,0:T(8,128)(2,1)S(1)} %select_select_fusion.refs_0_), channel_id=1, source_target_pairs={{0,18},{1,19},{2,16},{3,17},{4,22},{5,23},{6,20},{7,21},{8,26},{9,... | collective-permute-start | bytes 737288 | tf_op jit(solution)/shard_map/ppermute | solution.py:88
  49.1 13.8 %collective-permute-start.9 = (bf16[3,320,128]{2,1,0:T(8,128)(2,1)S(1)}, bf16[3,320,128]{2,1,0:T(8,128)(2,1)S(1)}, u32[]{:S(2)}, u32[]{:S(2)}) collective-permute-start(bf16[3,320,128]{2,1,0:T(8,128)(2,1)S(1)} %select_select_fusion.refs_0_), channel_id=1, source_target_pairs={{0,16},{1,17},{2,18},{3,19},{4,20},{5,21},{6,22},{7,23},{8,24},{9,... | collective-permute-start | bytes 737288 | tf_op jit(solution)/shard_map/ppermute | solution.py:88
  49.8 15.0 %collective-permute-start.8 = (bf16[3,320,128]{2,1,0:T(8,128)(2,1)S(1)}, bf16[3,320,128]{2,1,0:T(8,128)(2,1)S(1)}, u32[]{:S(2)}, u32[]{:S(2)}) collective-permute-start(bf16[3,320,128]{2,1,0:T(8,128)(2,1)S(1)} %select_select_fusion.refs_0_), channel_id=1, source_target_pairs={{0,2},{1,3},{2,0},{3,1},{4,6},{5,7},{6,4},{7,5},{8,10},{9,11},{10,... | collective-permute-start | bytes 737288 | tf_op jit(solution)/shard_map/ppermute | solution.py:88
  50.1 16.8 %collective-permute-start.11 = (bf16[3,320,128]{2,1,0:T(8,128)(2,1)S(1)}, bf16[3,320,128]{2,1,0:T(8,128)(2,1)S(1)}, u32[]{:S(2)}, u32[]{:S(2)}) collective-permute-start(bf16[3,320,128]{2,1,0:T(8,128)(2,1)S(1)} %select_select_fusion.refs_0_), channel_id=1, source_target_pairs={{0,1},{1,0},{2,3},{3,2},{4,5},{5,4},{6,7},{7,6},{8,9},{9,8},{10,11... | collective-permute-start | bytes 737288 | tf_op jit(solution)/shard_map/ppermute | solution.py:88
  56.2 11.2 %collective-permute-start.14 = (bf16[3,320,128]{2,1,0:T(8,128)(2,1)S(1)}, bf16[3,320,128]{2,1,0:T(8,128)(2,1)S(1)}, u32[]{:S(2)}, u32[]{:S(2)}) collective-permute-start(bf16[3,320,128]{2,1,0:T(8,128)(2,1)S(1)} %collective-permute-done.10.refs_3_), channel_id=1, source_target_pairs={{0,1},{1,0},{2,3},{3,2},{4,5},{5,4},{6,7},{7,6},{8,9},{9,8},{10,11... | collective-permute-start | bytes 737288 | tf_op jit(solution)/shard_map/ppermute | solution.py:88
  62.9 4.7 %collective-permute-start.13 = (bf16[3,320,128]{2,1,0:T(8,128)(2,1)S(1)}, bf16[3,320,128]{2,1,0:T(8,128)(2,1)S(1)}, u32[]{:S(2)}, u32[]{:S(2)}) collective-permute-start(bf16[3,320,128]{2,1,0:T(8,128)(2,1)S(1)} %collective-permute-done.9.refs_2_), channel_id=1, source_target_pairs={{0,1},{1,0},{2,3},{3,2},{4,5},{5,4},{6,7},{7,6},{8,9},{9,8},{10,11... | collective-permute-start | bytes 737288 | tf_op jit(solution)/shard_map/ppermute | solution.py:88
  64.8 2.8 %collective-permute-start.12 = (bf16[3,320,128]{2,1,0:T(8,128)(2,1)S(1)}, bf16[3,320,128]{2,1,0:T(8,128)(2,1)S(1)}, u32[]{:S(2)}, u32[]{:S(2)}) collective-permute-start(bf16[3,320,128]{2,1,0:T(8,128)(2,1)S(1)} %collective-permute-done.8.refs_1_), channel_id=1, source_target_pairs={{0,1},{1,0},{2,3},{3,2},{4,5},{5,4},{6,7},{7,6},{8,9},{9,8},{10,11... | collective-permute-start | bytes 737288 | tf_op jit(solution)/shard_map/ppermute | solution.py:88
  64.8 20.8 %collective-permute-start.19 = (bf16[3,320,128]{2,1,0:T(8,128)(2,1)S(1)}, bf16[3,320,128]{2,1,0:T(8,128)(2,1)S(1)}, u32[]{:S(2)}, u32[]{:S(2)}) collective-permute-start(bf16[3,320,128]{2,1,0:T(8,128)(2,1)S(1)} %broadcast_select_fusion.5.refs_11_), channel_id=1, source_target_pairs={{0,20},{1,21},{2,22},{3,23},{4,16},{5,17},{6,18},{7,19},{8,28},{9,... | collective-permute-start | bytes 737288 | tf_op jit(solution)/shard_map/ppermute | solution.py:88
  66.9 18.8 %collective-permute-start.18 = (bf16[3,320,128]{2,1,0:T(8,128)(2,1)S(1)}, bf16[3,320,128]{2,1,0:T(8,128)(2,1)S(1)}, u32[]{:S(2)}, u32[]{:S(2)}) collective-permute-start(bf16[3,320,128]{2,1,0:T(8,128)(2,1)S(1)} %broadcast_select_fusion.5.refs_11_), channel_id=1, source_target_pairs={{0,16},{1,17},{2,18},{3,19},{4,20},{5,21},{6,22},{7,23},{8,24},{9,... | collective-permute-start | bytes 737288 | tf_op jit(solution)/shard_map/ppermute | solution.py:88
  67.5 18.1 %collective-permute-start.17 = (bf16[3,320,128]{2,1,0:T(8,128)(2,1)S(1)}, bf16[3,320,128]{2,1,0:T(8,128)(2,1)S(1)}, u32[]{:S(2)}, u32[]{:S(2)}) collective-permute-start(bf16[3,320,128]{2,1,0:T(8,128)(2,1)S(1)} %broadcast_select_fusion.5.refs_11_), channel_id=1, source_target_pairs={{0,4},{1,5},{2,6},{3,7},{4,0},{5,1},{6,2},{7,3},{8,12},{9,13},{10,... | collective-permute-start | bytes 737288 | tf_op jit(solution)/shard_map/ppermute | solution.py:88
  84.2 7.1 %collective-permute-start.25 = (bf16[8,1,320,128]{3,2,1,0:T(8,128)(2,1)S(1)}, bf16[8,1,320,128]{3,2,1,0:T(8,128)(2,1)S(1)}, u32[]{:S(2)}, u32[]{:S(2)}) collective-permute-start(bf16[8,1,320,128]{3,2,1,0:T(8,128)(2,1)S(1)} %get-tuple-element.22), channel_id=1, source_target_pairs={{0,1},{1,0},{2,3},{3,2},{4,5},{5,4},{6,7},{7,6},{8,9},{9,8},{10,11... | collective-permute-start | bytes 1966088 | tf_op jit(solution)/shard_map/ppermute | solution.py:88
  85.7 2.0 %collective-permute-start.23 = (bf16[3,320,128]{2,1,0:T(8,128)(2,1)S(1)}, bf16[3,320,128]{2,1,0:T(8,128)(2,1)S(1)}, u32[]{:S(2)}, u32[]{:S(2)}) collective-permute-start(bf16[3,320,128]{2,1,0:T(8,128)(2,1)S(1)} %get-tuple-element.31.refs_3_), channel_id=1, source_target_pairs={{0,1},{1,0},{2,3},{3,2},{4,5},{5,4},{6,7},{7,6},{8,9},{9,8},{10,11... | collective-permute-start | bytes 737288 | tf_op jit(solution)/shard_map/ppermute | solution.py:88
  85.8 5.4 %collective-permute-start.20 = (bf16[3,320,128]{2,1,0:T(8,128)(2,1)S(1)}, bf16[3,320,128]{2,1,0:T(8,128)(2,1)S(1)}, u32[]{:S(2)}, u32[]{:S(2)}) collective-permute-start(bf16[3,320,128]{2,1,0:T(8,128)(2,1)S(1)} %get-tuple-element.32.refs_0_), channel_id=1, source_target_pairs={{0,1},{1,0},{2,3},{3,2},{4,5},{5,4},{6,7},{7,6},{8,9},{9,8},{10,11... | collective-permute-start | bytes 737288 | tf_op jit(solution)/shard_map/ppermute | solution.py:88
  86.3 5.0 %collective-permute-start.21 = (bf16[3,320,128]{2,1,0:T(8,128)(2,1)S(1)}, bf16[3,320,128]{2,1,0:T(8,128)(2,1)S(1)}, u32[]{:S(2)}, u32[]{:S(2)}) collective-permute-start(bf16[3,320,128]{2,1,0:T(8,128)(2,1)S(1)} %get-tuple-element.33.refs_1_), channel_id=1, source_target_pairs={{0,1},{1,0},{2,3},{3,2},{4,5},{5,4},{6,7},{7,6},{8,9},{9,8},{10,11... | collective-permute-start | bytes 737288 | tf_op jit(solution)/shard_map/ppermute | solution.py:88
  86.4 4.9 %collective-permute-start.22 = (bf16[3,320,128]{2,1,0:T(8,128)(2,1)S(1)}, bf16[3,320,128]{2,1,0:T(8,128)(2,1)S(1)}, u32[]{:S(2)}, u32[]{:S(2)}) collective-permute-start(bf16[3,320,128]{2,1,0:T(8,128)(2,1)S(1)} %get-tuple-element.34.refs_2_), channel_id=1, source_target_pairs={{0,1},{1,0},{2,3},{3,2},{4,5},{5,4},{6,7},{7,6},{8,9},{9,8},{10,11... | collective-permute-start | bytes 737288 | tf_op jit(solution)/shard_map/ppermute | solution.py:88
  87.7 17.9 %collective-permute-start.24 = (bf16[8,1,320,128]{3,2,1,0:T(8,128)(2,1)S(1)}, bf16[8,1,320,128]{3,2,1,0:T(8,128)(2,1)S(1)}, u32[]{:S(2)}, u32[]{:S(2)}) collective-permute-start(bf16[8,1,320,128]{3,2,1,0:T(8,128)(2,1)S(1)} %get-tuple-element.24), channel_id=1, source_target_pairs={{0,0},{1,2},{2,1},{3,4},{4,3},{5,6},{6,5},{7,8},{8,7},{9,10},{10,9... | collective-permute-start | bytes 1966088 | tf_op jit(solution)/shard_map/ppermute | solution.py:88

commit v4 on v3

--- a/solution.py
+++ b/solution.py
@@ -74,7 +74,7 @@
             out_specs=[pl.BlockSpec(shape, lambda k, i, ids, owners: (0, 0, 0, 0))] * 4,
         ),
         out_shape=[jax.ShapeDtypeStruct(shape, jnp.bfloat16)] * 4,
-        compiler_params=pltpu.CompilerParams(vmem_limit_bytes=57 * 2**20),
+        compiler_params=pltpu.CompilerParams(vmem_limit_bytes=50 * 2**20),
         name="kernel_update",
     )(ids, owners, weights, momentum, grads)
 
@@ -110,7 +110,7 @@
     edge_rows = edges_after(far[0])
     held[0] = after(held[0], edge_rows[1][: held[0].shape[0], 0], owners)
     high = [1 << b for b in range(3, count.bit_length() - 1)]
-    turns = (high[::-1] + [4], [2] + high[::-1])
+    turns = (high[::-1] + [2], [4] + high[::-1])
     for bits in zip(*turns):
         held[0] = after(held[0], held[1], owners)
         held = [keep(bits[k], held[k], swap_dp(held[k], bits[k]), k) for k in range(2)]
@@ -350,7 +350,7 @@
 
 def local(groups, count, images, kernel_weights, kernel_momentum, kernel_grads, owners):
     g, dp = lax.axis_index("groups"), lax.axis_index("dp")
-    splits = (2, 4)
+    splits = (4, 2)
     ids = jnp.stack([g, dp]).astype(jnp.int32)
 
     def flat(x):

time: 113 us -> 107 us (0.947)
  Pallas kernels: 44.1 us -> 40.3 us
  waiting for transfers between devices: 31 us -> 28 us
  starting transfers between devices: 29.3 us -> 31.6 us
  other arithmetic: 2.04 us -> 0.48 us
    pallas_call x1, Pallas kernels: 6.38 us -> 2.54 us  [update(): pl.pallas_call(functools.partial(update_body, depth=depth, splits=splits)...]
    ppermute x26, waiting for transfers between devices: 31 us -> 28 us  [swap(): return lax.ppermute(x, axes, pairs)]
    ppermute x26, starting transfers between devices: 29.3 us -> 31.6 us  [swap(): return lax.ppermute(x, axes, pairs)]
  transfers between devices with their start and end apart: 26 -> 26, of which waited for: 9 -> 8; matrix products, arithmetic and copies ran while one was open for 2% -> 1% of each run, Pallas kernels for 28% -> 29%
where the time goes in v4:
time: 107 us
  Pallas kernels  40.3 us (38%)
  starting transfers between devices  31.6 us (30%)
  waiting for transfers between devices  28 us (26%)
  between operations  5.06 us (5%)
  local copies, waits for them, and re-layouts  1.24 us (1%)
    pallas_call x3, Pallas kernels, conv_call(): pl.pallas_call(functools.partial(body, split=split, count=count), grid_sp...  36.7 us
    ppermute x26, starting transfers between devices, swap(): return lax.ppermute(x, axes, pairs)  31.6 us
    ppermute x26, waiting for transfers between devices, swap(): return lax.ppermute(x, axes, pairs)  28 us
    pallas_call x1, Pallas kernels, update(): pl.pallas_call(functools.partial(update_body, depth=depth, splits=splits)...  2.54 us
  transfers between devices with their start and end apart: 26, of which 8 were waited for; matrix products, arithmetic and copies ran while one was open for 1% of the time, Pallas kernels for 29%

profile of v4, /device:TPU:1, one launch (start us, length us, event | category | flops | bytes accessed | tf_op | source)
XLA Modules:
  0.0 106.6 jit_solution(15060938582090505559)
XLA Ops:
  0.0 0.1 pad_add_fusion.ids
  0.1 0.7 copy-done.1
  0.7 2.5 %kernel_update.1 = (bf16[2,3,320,128]{3,2,1,0:T(8,128)(2,1)S(1)}, bf16[2,3,320,128]{3,2,1,0:T(8,128)(2,1)S(1)}, bf16[2,3,320,128]{3,2,1,0:T(8,128)(2,1)S(1)}, bf16[2,3,320,128]{3,2,1,0:T(8,128)(2,1)S(1)}) custom-call(s32[2]{0:T(128)S(1)} %pad_add_fusion.ids, s32[2]{0:T(128)S(1)} %copy-done.1, bf16[2,3,960,320]{3,2,1,0:T(8,128)(2,1)} %bitcast.55, ...), custom_call_target="tpu_custom_call" | custom-call | tf_op jit(solution)/shard_map/kernel_update/pallas_call | solution.py:68
  3.3 0.1 collective-permute-start.1
  3.3 0.5 collective-permute-start
  3.8 0.6 fusion.9
  5.6 0.0 collective-permute-done.1
  5.6 0.1 fusion.5
  5.7 2.3 %collective-permute-start.2 = (bf16[3,320,128]{2,1,0:T(8,128)(2,1)S(1)}, bf16[3,320,128]{2,1,0:T(8,128)(2,1)S(1)}, u32[]{:S(2)}, u32[]{:S(2)}) collective-permute-start(bf16[3,320,128]{2,1,0:T(8,128)(2,1)S(1)} %get-tuple-element.29), channel_id=1, source_target_pairs={{0,2},{1,3},{2,0},{3,1},{4,6},{5,7},{6,4},{7,5},{8,10},{9,11},{10,... | collective-permute-start | bytes 737288 | tf_op jit(solution)/shard_map/ppermute | solution.py:88
  8.0 1.3 %collective-permute-start.5 = (bf16[3,320,128]{2,1,0:T(8,128)(2,1)S(1)}, bf16[3,320,128]{2,1,0:T(8,128)(2,1)S(1)}, u32[]{:S(2)}, u32[]{:S(2)}) collective-permute-start(bf16[3,320,128]{2,1,0:T(8,128)(2,1)S(1)} %get-tuple-element.30._), channel_id=1, source_target_pairs={{0,4},{1,5},{2,6},{3,7},{4,0},{5,1},{6,2},{7,3},{8,12},{9,13},{10,... | collective-permute-start | bytes 737288 | tf_op jit(solution)/shard_map/ppermute | solution.py:88
  10.5 1.0 edge_rows.1
  11.6 0.0 collective-permute-done
  11.6 2.3 %collective-permute-done.2 = bf16[3,320,128]{2,1,0:T(8,128)(2,1)S(1)} collective-permute-done((bf16[3,320,128]{2,1,0:T(8,128)(2,1)S(1)}, bf16[3,320,128]{2,1,0:T(8,128)(2,1)S(1)}, u32[]{:S(2)}, u32[]{:S(2)}) %collective-permute-start.2) | collective-permute-done | bytes 245792 | tf_op jit(solution)/shard_map/ppermute | solution.py:88
  13.8 0.8 collective-permute-done.5
  14.7 0.1 fusion.3
  14.8 3.8 %collective-permute-start.6 = (bf16[3,320,128]{2,1,0:T(8,128)(2,1)S(1)}, bf16[3,320,128]{2,1,0:T(8,128)(2,1)S(1)}, u32[]{:S(2)}, u32[]{:S(2)}) collective-permute-start(bf16[3,320,128]{2,1,0:T(8,128)(2,1)S(1)} %get-tuple-element.27), channel_id=1, source_target_pairs={{0,8},{1,9},{2,10},{3,11},{4,12},{5,13},{6,14},{7,15},{8,0},{9,1},... | collective-permute-start | bytes 737288 | tf_op jit(solution)/shard_map/ppermute | solution.py:88
  18.5 0.0 collective-permute-start.3
  19.8 10.2 %collective-permute-done.6 = bf16[3,320,128]{2,1,0:T(8,128)(2,1)S(1)} collective-permute-done((bf16[3,320,128]{2,1,0:T(8,128)(2,1)S(1)}, bf16[3,320,128]{2,1,0:T(8,128)(2,1)S(1)}, u32[]{:S(2)}, u32[]{:S(2)}) %collective-permute-start.6) | collective-permute-done | bytes 245792 | tf_op jit(solution)/shard_map/ppermute | solution.py:88
  30.0 0.0 collective-permute-done.3
  30.0 0.1 select_select_fusion.1
  30.0 1.4 %collective-permute-start.7 = (bf16[3,320,128]{2,1,0:T(8,128)(2,1)S(1)}, bf16[3,320,128]{2,1,0:T(8,128)(2,1)S(1)}, u32[]{:S(2)}, u32[]{:S(2)}) collective-permute-start(bf16[3,320,128]{2,1,0:T(8,128)(2,1)S(1)} %get-tuple-element.25), channel_id=1, source_target_pairs={{0,2},{1,3},{2,0},{3,1},{4,6},{5,7},{6,4},{7,5},{8,10},{9,11},{10,... | collective-permute-start | bytes 737288 | tf_op jit(solution)/shard_map/ppermute | solution.py:88
  31.4 0.0 collective-permute-start.4
  31.4 4.3 %collective-permute-start.16 = (bf16[8,1,320,128]{3,2,1,0:T(8,128)(2,1)S(1)}, bf16[8,1,320,128]{3,2,1,0:T(8,128)(2,1)S(1)}, u32[]{:S(2)}, u32[]{:S(2)}) collective-permute-start(bf16[8,1,320,128]{3,2,1,0:T(8,128)(2,1)S(1)} %get-tuple-element.21), channel_id=1, source_target_pairs={{0,0},{1,2},{2,1},{3,4},{4,3},{5,6},{6,5},{7,8},{8,7},{9,10},{10,9... | collective-permute-start | bytes 1966088 | tf_op jit(solution)/shard_map/ppermute | solution.py:88
  37.0 0.1 collective-permute-start.15
  37.0 0.0 collective-permute-done.7
  37.0 6.9 %collective-permute-done.4 = bf16[3,320,128]{2,1,0:T(8,128)(2,1)S(1)} collective-permute-done((bf16[3,320,128]{2,1,0:T(8,128)(2,1)S(1)}, bf16[3,320,128]{2,1,0:T(8,128)(2,1)S(1)}, u32[]{:S(2)}, u32[]{:S(2)}) %collective-permute-start.4) | collective-permute-done | bytes 245792 | tf_op jit(solution)/shard_map/ppermute | solution.py:88
  44.0 0.6 collective-permute-start.10
  44.6 0.8 collective-permute-start.9
  45.4 1.4 %collective-permute-start.8 = (bf16[3,320,128]{2,1,0:T(8,128)(2,1)S(1)}, bf16[3,320,128]{2,1,0:T(8,128)(2,1)S(1)}, u32[]{:S(2)}, u32[]{:S(2)}) collective-permute-start(bf16[3,320,128]{2,1,0:T(8,128)(2,1)S(1)} %select_select_fusion.refs_0_), channel_id=1, source_target_pairs={{0,4},{1,5},{2,6},{3,7},{4,0},{5,1},{6,2},{7,3},{8,12},{9,13},{10,... | collective-permute-start | bytes 737288 | tf_op jit(solution)/shard_map/ppermute | solution.py:88
  46.7 4.2 %collective-permute-done.16.refs_10_ = bf16[8,1,320,128]{3,2,1,0:T(8,128)(2,1)S(1)} collective-permute-done((bf16[8,1,320,128]{3,2,1,0:T(8,128)(2,1)S(1)}, bf16[8,1,320,128]{3,2,1,0:T(8,128)(2,1)S(1)}, u32[]{:S(2)}, u32[]{:S(2)}) %collective-permute-start.16) | collective-permute-done | bytes 655392 | tf_op jit(solution)/shard_map/ppermute | solution.py:88
  51.0 0.0 collective-permute-start.11
  51.0 1.7 %collective-permute-done.10.refs_3_ = bf16[3,320,128]{2,1,0:T(8,128)(2,1)S(1)} collective-permute-done((bf16[3,320,128]{2,1,0:T(8,128)(2,1)S(1)}, bf16[3,320,128]{2,1,0:T(8,128)(2,1)S(1)}, u32[]{:S(2)}, u32[]{:S(2)}) %collective-permute-start.10) | collective-permute-done | bytes 245792 | tf_op jit(solution)/shard_map/ppermute | solution.py:88
  52.7 6.6 %collective-permute-start.14 = (bf16[3,320,128]{2,1,0:T(8,128)(2,1)S(1)}, bf16[3,320,128]{2,1,0:T(8,128)(2,1)S(1)}, u32[]{:S(2)}, u32[]{:S(2)}) collective-permute-start(bf16[3,320,128]{2,1,0:T(8,128)(2,1)S(1)} %collective-permute-done.10.refs_3_), channel_id=1, source_target_pairs={{0,1},{1,0},{2,3},{3,2},{4,5},{5,4},{6,7},{7,6},{8,9},{9,8},{10,11... | collective-permute-start | bytes 737288 | tf_op jit(solution)/shard_map/ppermute | solution.py:88
  59.3 0.0 collective-permute-done.9.refs_2_
  59.3 0.0 collective-permute-start.13
  59.3 0.0 collective-permute-done.8.refs_1_
  59.3 1.7 %collective-permute-start.12 = (bf16[3,320,128]{2,1,0:T(8,128)(2,1)S(1)}, bf16[3,320,128]{2,1,0:T(8,128)(2,1)S(1)}, u32[]{:S(2)}, u32[]{:S(2)}) collective-permute-start(bf16[3,320,128]{2,1,0:T(8,128)(2,1)S(1)} %collective-permute-done.8.refs_1_), channel_id=1, source_target_pairs={{0,1},{1,0},{2,3},{3,2},{4,5},{5,4},{6,7},{7,6},{8,9},{9,8},{10,11... | collective-permute-start | bytes 737288 | tf_op jit(solution)/shard_map/ppermute | solution.py:88
  61.1 0.0 collective-permute-done.15.refs_9_
  61.1 0.1 collective-permute-start.19
  61.1 0.0 collective-permute-done.11.refs_4_
  61.2 1.3 %collective-permute-start.18 = (bf16[3,320,128]{2,1,0:T(8,128)(2,1)S(1)}, bf16[3,320,128]{2,1,0:T(8,128)(2,1)S(1)}, u32[]{:S(2)}, u32[]{:S(2)}) collective-permute-start(bf16[3,320,128]{2,1,0:T(8,128)(2,1)S(1)} %broadcast_select_fusion.5.refs_11_), channel_id=1, source_target_pairs={{0,16},{1,17},{2,18},{3,19},{4,20},{5,21},{6,22},{7,23},{8,24},{9,... | collective-permute-start | bytes 737288 | tf_op jit(solution)/shard_map/ppermute | solution.py:88
  62.4 0.0 collective-permute-done.14.refs_7_
  62.4 1.4 %collective-permute-start.17 = (bf16[3,320,128]{2,1,0:T(8,128)(2,1)S(1)}, bf16[3,320,128]{2,1,0:T(8,128)(2,1)S(1)}, u32[]{:S(2)}, u32[]{:S(2)}) collective-permute-start(bf16[3,320,128]{2,1,0:T(8,128)(2,1)S(1)} %broadcast_select_fusion.5.refs_11_), channel_id=1, source_target_pairs={{0,2},{1,3},{2,0},{3,1},{4,6},{5,7},{6,4},{7,5},{8,10},{9,11},{10,... | collective-permute-start | bytes 737288 | tf_op jit(solution)/shard_map/ppermute | solution.py:88
  63.8 0.0 collective-permute-done.13.refs_6_
  63.8 0.0 collective-permute-done.12.refs_5_
  63.8 16.7 %residual_conv.3 = (bf16[8,8,320,128]{3,2,1,0:T(8,128)(2,1)S(1)}, bf16[8,1,320,128]{3,2,1,0:T(8,128)(2,1)S(1)}, bf16[8,1,320,128]{3,2,1,0:T(8,128)(2,1)S(1)}) custom-call(s32[2]{0:T(128)S(1)} %pad_add_fusion.ids, bf16[3,320,128]{2,1,0:T(8,128)(2,1)S(1)} %select_select_fusion.refs_0_, bf16[3,320,128]{2,1,0:T(8,128)(2,1)S(1)} %collective-permute-done.8.refs_1_, ...), custom_call_target="tpu_custom_call" | custom-call | flops 15099494400 | bytes 10485760 | tf_op jit(solution)/shard_map/residual_conv/pallas_call | solution.py:282
  80.5 0.9 collective-permute-start.25
  81.4 0.0 collective-permute-done.19
  81.4 0.0 collective-permute-done.18
  81.4 0.0 collective-permute-done.17
  81.4 0.1 broadcast_select_fusion.6
  81.5 0.1 collective-permute-start.23
  81.6 0.5 collective-permute-start.20
  82.0 0.1 collective-permute-start.21
  82.1 0.4 collective-permute-start.22
  82.6 0.9 collective-permute-done.23.refs_7_
  83.5 2.2 %collective-permute-start.24 = (bf16[8,1,320,128]{3,2,1,0:T(8,128)(2,1)S(1)}, bf16[8,1,320,128]{3,2,1,0:T(8,128)(2,1)S(1)}, u32[]{:S(2)}, u32[]{:S(2)}) collective-permute-start(bf16[8,1,320,128]{3,2,1,0:T(8,128)(2,1)S(1)} %get-tuple-element.24), channel_id=1, source_target_pairs={{0,0},{1,2},{2,1},{3,4},{4,3},{5,6},{6,5},{7,8},{8,7},{9,10},{10,9... | collective-permute-start | bytes 1966088 | tf_op jit(solution)/shard_map/ppermute | solution.py:88
  85.6 0.0 collective-permute-done.20.refs_4_
  85.6 0.0 collective-permute-done.21.refs_5_
  85.6 0.0 collective-permute-done.22.refs_6_
  85.7 0.0 collective-permute-done.25.refs_9_
  85.7 13.5 %residual_conv.4.refs_10_ = bf16[8,8,320,128]{3,2,1,0:T(8,128)(2,1)} custom-call(s32[2]{0:T(128)S(1)} %pad_add_fusion.ids, bf16[3,320,128]{2,1,0:T(8,128)(2,1)S(1)} %get-tuple-element.32.refs_0_, bf16[3,320,128]{2,1,0:T(8,128)(2,1)S(1)} %get-tuple-element.33.refs_1_, bf16[3,320,128]{2,1,0:T(8,128)(2,1)S(1)} %get-tuple-element.34.refs_2_, ...), custom_call_target="tpu_custom_call" | custom-call | flops 11324620800 | bytes 10485760 | tf_op jit(solution)/shard_map/residual_conv/pallas_call | solution.py:282
  99.1 0.8 collective-permute-done.24.refs_9_
  100.0 6.6 %residual_conv.5 = bf16[8,8,320,128]{3,2,1,0:T(8,128)(2,1)} custom-call(s32[2]{0:T(128)S(1)} %pad_add_fusion.ids, bf16[3,320,128]{2,1,0:T(8,128)(2,1)S(1)} %get-tuple-element.32.refs_0_, bf16[3,320,128]{2,1,0:T(8,128)(2,1)S(1)} %get-tuple-element.33.refs_1_, bf16[3,320,128]{2,1,0:T(8,128)(2,1)S(1)} %get-tuple-element.34.refs_2_, ...), custom_call_target="tpu_custom_call", output_to_operand_aliasing={{}: (11, {})} | custom-call | flops 3774873600 | bytes 10485760 | tf_op jit(solution)/shard_map/residual_conv/pallas_call | solution.py:282
  (6 shorter events, 0.1 us)
Async XLA Ops:
  0.1 0.7 copy-start.1
  0.7 9.8 %copy-start = (bf16[8,8,128,320]{2,3,1,0:T(8,128)(2,1)S(1)}, bf16[8,8,128,320]{2,3,1,0:T(8,128)(2,1)}, u32[]{:S(2)}) copy-start(bf16[8,8,128,320]{2,3,1,0:T(8,128)(2,1)} %param.5) | copy-start | bytes 15728644
  3.3 2.3 %collective-permute-start.1 = (bf16[2,3,320,128]{3,2,1,0:T(8,128)(2,1)S(1)}, bf16[2,3,320,128]{3,2,1,0:T(8,128)(2,1)S(1)}, u32[]{:S(2)}, u32[]{:S(2)}) collective-permute-start(bf16[2,3,320,128]{3,2,1,0:T(8,128)(2,1)S(1)} %get-tuple-element.18), channel_id=1, source_target_pairs={{0,1},{1,0},{2,3},{3,2},{4,5},{5,4},{6,7},{7,6},{8,9},{9,8},{10,11... | collective-permute-start | bytes 1474568 | tf_op jit(solution)/shard_map/ppermute | solution.py:88
  3.3 8.2 %collective-permute-start = (bf16[2,3,320,128]{3,2,1,0:T(8,128)(2,1)S(1)}, bf16[2,3,320,128]{3,2,1,0:T(8,128)(2,1)S(1)}, u32[]{:S(2)}, u32[]{:S(2)}) collective-permute-start(bf16[2,3,320,128]{3,2,1,0:T(8,128)(2,1)S(1)} %get-tuple-element.16), channel_id=1, source_target_pairs={{0,1},{1,0},{2,3},{3,2},{4,5},{5,4},{6,7},{7,6},{8,9},{9,8},{10,11... | collective-permute-start | bytes 1474568 | tf_op jit(solution)/shard_map/ppermute | solution.py:88
  5.7 8.2 %collective-permute-start.2 = (bf16[3,320,128]{2,1,0:T(8,128)(2,1)S(1)}, bf16[3,320,128]{2,1,0:T(8,128)(2,1)S(1)}, u32[]{:S(2)}, u32[]{:S(2)}) collective-permute-start(bf16[3,320,128]{2,1,0:T(8,128)(2,1)S(1)} %get-tuple-element.29), channel_id=1, source_target_pairs={{0,2},{1,3},{2,0},{3,1},{4,6},{5,7},{6,4},{7,5},{8,10},{9,11},{10,... | collective-permute-start | bytes 737288 | tf_op jit(solution)/shard_map/ppermute | solution.py:88
  8.0 6.7 %collective-permute-start.5 = (bf16[3,320,128]{2,1,0:T(8,128)(2,1)S(1)}, bf16[3,320,128]{2,1,0:T(8,128)(2,1)S(1)}, u32[]{:S(2)}, u32[]{:S(2)}) collective-permute-start(bf16[3,320,128]{2,1,0:T(8,128)(2,1)S(1)} %get-tuple-element.30._), channel_id=1, source_target_pairs={{0,4},{1,5},{2,6},{3,7},{4,0},{5,1},{6,2},{7,3},{8,12},{9,13},{10,... | collective-permute-start | bytes 737288 | tf_op jit(solution)/shard_map/ppermute | solution.py:88
  14.8 15.2 %collective-permute-start.6 = (bf16[3,320,128]{2,1,0:T(8,128)(2,1)S(1)}, bf16[3,320,128]{2,1,0:T(8,128)(2,1)S(1)}, u32[]{:S(2)}, u32[]{:S(2)}) collective-permute-start(bf16[3,320,128]{2,1,0:T(8,128)(2,1)S(1)} %get-tuple-element.27), channel_id=1, source_target_pairs={{0,8},{1,9},{2,10},{3,11},{4,12},{5,13},{6,14},{7,15},{8,0},{9,1},... | collective-permute-start | bytes 737288 | tf_op jit(solution)/shard_map/ppermute | solution.py:88
  18.5 11.4 %collective-permute-start.3 = (bf16[3,320,128]{2,1,0:T(8,128)(2,1)S(1)}, bf16[3,320,128]{2,1,0:T(8,128)(2,1)S(1)}, u32[]{:S(2)}, u32[]{:S(2)}) collective-permute-start(bf16[3,320,128]{2,1,0:T(8,128)(2,1)S(1)} %get-tuple-element.28), channel_id=1, source_target_pairs={{0,4},{1,5},{2,6},{3,7},{4,0},{5,1},{6,2},{7,3},{8,12},{9,13},{10,... | collective-permute-start | bytes 737288 | tf_op jit(solution)/shard_map/ppermute | solution.py:88
  30.0 7.0 %collective-permute-start.7 = (bf16[3,320,128]{2,1,0:T(8,128)(2,1)S(1)}, bf16[3,320,128]{2,1,0:T(8,128)(2,1)S(1)}, u32[]{:S(2)}, u32[]{:S(2)}) collective-permute-start(bf16[3,320,128]{2,1,0:T(8,128)(2,1)S(1)} %get-tuple-element.25), channel_id=1, source_target_pairs={{0,2},{1,3},{2,0},{3,1},{4,6},{5,7},{6,4},{7,5},{8,10},{9,11},{10,... | collective-permute-start | bytes 737288 | tf_op jit(solution)/shard_map/ppermute | solution.py:88
  31.4 12.5 %collective-permute-start.4 = (bf16[3,320,128]{2,1,0:T(8,128)(2,1)S(1)}, bf16[3,320,128]{2,1,0:T(8,128)(2,1)S(1)}, u32[]{:S(2)}, u32[]{:S(2)}) collective-permute-start(bf16[3,320,128]{2,1,0:T(8,128)(2,1)S(1)} %get-tuple-element.26), channel_id=1, source_target_pairs={{0,8},{1,9},{2,10},{3,11},{4,12},{5,13},{6,14},{7,15},{8,0},{9,1},... | collective-permute-start | bytes 737288 | tf_op jit(solution)/shard_map/ppermute | solution.py:88
  31.4 19.5 %collective-permute-start.16 = (bf16[8,1,320,128]{3,2,1,0:T(8,128)(2,1)S(1)}, bf16[8,1,320,128]{3,2,1,0:T(8,128)(2,1)S(1)}, u32[]{:S(2)}, u32[]{:S(2)}) collective-permute-start(bf16[8,1,320,128]{3,2,1,0:T(8,128)(2,1)S(1)} %get-tuple-element.21), channel_id=1, source_target_pairs={{0,0},{1,2},{2,1},{3,4},{4,3},{5,6},{6,5},{7,8},{8,7},{9,10},{10,9... | collective-permute-start | bytes 1966088 | tf_op jit(solution)/shard_map/ppermute | solution.py:88
  37.0 24.1 %collective-permute-start.15 = (bf16[8,1,320,128]{3,2,1,0:T(8,128)(2,1)S(1)}, bf16[8,1,320,128]{3,2,1,0:T(8,128)(2,1)S(1)}, u32[]{:S(2)}, u32[]{:S(2)}) collective-permute-start(bf16[8,1,320,128]{3,2,1,0:T(8,128)(2,1)S(1)} %get-tuple-element.19), channel_id=1, source_target_pairs={{0,1},{1,0},{2,3},{3,2},{4,5},{5,4},{6,7},{7,6},{8,9},{9,8},{10,11... | collective-permute-start | bytes 1966088 | tf_op jit(solution)/shard_map/ppermute | solution.py:88
  44.0 8.7 %collective-permute-start.10 = (bf16[3,320,128]{2,1,0:T(8,128)(2,1)S(1)}, bf16[3,320,128]{2,1,0:T(8,128)(2,1)S(1)}, u32[]{:S(2)}, u32[]{:S(2)}) collective-permute-start(bf16[3,320,128]{2,1,0:T(8,128)(2,1)S(1)} %select_select_fusion.refs_0_), channel_id=1, source_target_pairs={{0,20},{1,21},{2,22},{3,23},{4,16},{5,17},{6,18},{7,19},{8,28},{9,... | collective-permute-start | bytes 737288 | tf_op jit(solution)/shard_map/ppermute | solution.py:88
  44.6 14.7 %collective-permute-start.9 = (bf16[3,320,128]{2,1,0:T(8,128)(2,1)S(1)}, bf16[3,320,128]{2,1,0:T(8,128)(2,1)S(1)}, u32[]{:S(2)}, u32[]{:S(2)}) collective-permute-start(bf16[3,320,128]{2,1,0:T(8,128)(2,1)S(1)} %select_select_fusion.refs_0_), channel_id=1, source_target_pairs={{0,16},{1,17},{2,18},{3,19},{4,20},{5,21},{6,22},{7,23},{8,24},{9,... | collective-permute-start | bytes 737288 | tf_op jit(solution)/shard_map/ppermute | solution.py:88
  45.4 14.0 %collective-permute-start.8 = (bf16[3,320,128]{2,1,0:T(8,128)(2,1)S(1)}, bf16[3,320,128]{2,1,0:T(8,128)(2,1)S(1)}, u32[]{:S(2)}, u32[]{:S(2)}) collective-permute-start(bf16[3,320,128]{2,1,0:T(8,128)(2,1)S(1)} %select_select_fusion.refs_0_), channel_id=1, source_target_pairs={{0,4},{1,5},{2,6},{3,7},{4,0},{5,1},{6,2},{7,3},{8,12},{9,13},{10,... | collective-permute-start | bytes 737288 | tf_op jit(solution)/shard_map/ppermute | solution.py:88
  51.0 10.2 %collective-permute-start.11 = (bf16[3,320,128]{2,1,0:T(8,128)(2,1)S(1)}, bf16[3,320,128]{2,1,0:T(8,128)(2,1)S(1)}, u32[]{:S(2)}, u32[]{:S(2)}) collective-permute-start(bf16[3,320,128]{2,1,0:T(8,128)(2,1)S(1)} %select_select_fusion.refs_0_), channel_id=1, source_target_pairs={{0,1},{1,0},{2,3},{3,2},{4,5},{5,4},{6,7},{7,6},{8,9},{9,8},{10,11... | collective-permute-start | bytes 737288 | tf_op jit(solution)/shard_map/ppermute | solution.py:88
  52.7 9.7 %collective-permute-start.14 = (bf16[3,320,128]{2,1,0:T(8,128)(2,1)S(1)}, bf16[3,320,128]{2,1,0:T(8,128)(2,1)S(1)}, u32[]{:S(2)}, u32[]{:S(2)}) collective-permute-start(bf16[3,320,128]{2,1,0:T(8,128)(2,1)S(1)} %collective-permute-done.10.refs_3_), channel_id=1, source_target_pairs={{0,1},{1,0},{2,3},{3,2},{4,5},{5,4},{6,7},{7,6},{8,9},{9,8},{10,11... | collective-permute-start | bytes 737288 | tf_op jit(solution)/shard_map/ppermute | solution.py:88
  59.3 4.5 %collective-permute-start.13 = (bf16[3,320,128]{2,1,0:T(8,128)(2,1)S(1)}, bf16[3,320,128]{2,1,0:T(8,128)(2,1)S(1)}, u32[]{:S(2)}, u32[]{:S(2)}) collective-permute-start(bf16[3,320,128]{2,1,0:T(8,128)(2,1)S(1)} %collective-permute-done.9.refs_2_), channel_id=1, source_target_pairs={{0,1},{1,0},{2,3},{3,2},{4,5},{5,4},{6,7},{7,6},{8,9},{9,8},{10,11... | collective-permute-start | bytes 737288 | tf_op jit(solution)/shard_map/ppermute | solution.py:88
  59.3 4.5 %collective-permute-start.12 = (bf16[3,320,128]{2,1,0:T(8,128)(2,1)S(1)}, bf16[3,320,128]{2,1,0:T(8,128)(2,1)S(1)}, u32[]{:S(2)}, u32[]{:S(2)}) collective-permute-start(bf16[3,320,128]{2,1,0:T(8,128)(2,1)S(1)} %collective-permute-done.8.refs_1_), channel_id=1, source_target_pairs={{0,1},{1,0},{2,3},{3,2},{4,5},{5,4},{6,7},{7,6},{8,9},{9,8},{10,11... | collective-permute-start | bytes 737288 | tf_op jit(solution)/shard_map/ppermute | solution.py:88
  61.1 20.3 %collective-permute-start.19 = (bf16[3,320,128]{2,1,0:T(8,128)(2,1)S(1)}, bf16[3,320,128]{2,1,0:T(8,128)(2,1)S(1)}, u32[]{:S(2)}, u32[]{:S(2)}) collective-permute-start(bf16[3,320,128]{2,1,0:T(8,128)(2,1)S(1)} %broadcast_select_fusion.5.refs_11_), channel_id=1, source_target_pairs={{0,18},{1,19},{2,16},{3,17},{4,22},{5,23},{6,20},{7,21},{8,26},{9,... | collective-permute-start | bytes 737288 | tf_op jit(solution)/shard_map/ppermute | solution.py:88
  61.2 20.2 %collective-permute-start.18 = (bf16[3,320,128]{2,1,0:T(8,128)(2,1)S(1)}, bf16[3,320,128]{2,1,0:T(8,128)(2,1)S(1)}, u32[]{:S(2)}, u32[]{:S(2)}) collective-permute-start(bf16[3,320,128]{2,1,0:T(8,128)(2,1)S(1)} %broadcast_select_fusion.5.refs_11_), channel_id=1, source_target_pairs={{0,16},{1,17},{2,18},{3,19},{4,20},{5,21},{6,22},{7,23},{8,24},{9,... | collective-permute-start | bytes 737288 | tf_op jit(solution)/shard_map/ppermute | solution.py:88
  62.4 18.9 %collective-permute-start.17 = (bf16[3,320,128]{2,1,0:T(8,128)(2,1)S(1)}, bf16[3,320,128]{2,1,0:T(8,128)(2,1)S(1)}, u32[]{:S(2)}, u32[]{:S(2)}) collective-permute-start(bf16[3,320,128]{2,1,0:T(8,128)(2,1)S(1)} %broadcast_select_fusion.5.refs_11_), channel_id=1, source_target_pairs={{0,2},{1,3},{2,0},{3,1},{4,6},{5,7},{6,4},{7,5},{8,10},{9,11},{10,... | collective-permute-start | bytes 737288 | tf_op jit(solution)/shard_map/ppermute | solution.py:88
  80.5 5.2 %collective-permute-start.25 = (bf16[8,1,320,128]{3,2,1,0:T(8,128)(2,1)S(1)}, bf16[8,1,320,128]{3,2,1,0:T(8,128)(2,1)S(1)}, u32[]{:S(2)}, u32[]{:S(2)}) collective-permute-start(bf16[8,1,320,128]{3,2,1,0:T(8,128)(2,1)S(1)} %get-tuple-element.22), channel_id=1, source_target_pairs={{0,1},{1,0},{2,3},{3,2},{4,5},{5,4},{6,7},{7,6},{8,9},{9,8},{10,11... | collective-permute-start | bytes 1966088 | tf_op jit(solution)/shard_map/ppermute | solution.py:88
  81.5 2.0 %collective-permute-start.23 = (bf16[3,320,128]{2,1,0:T(8,128)(2,1)S(1)}, bf16[3,320,128]{2,1,0:T(8,128)(2,1)S(1)}, u32[]{:S(2)}, u32[]{:S(2)}) collective-permute-start(bf16[3,320,128]{2,1,0:T(8,128)(2,1)S(1)} %get-tuple-element.31.refs_3_), channel_id=1, source_target_pairs={{0,1},{1,0},{2,3},{3,2},{4,5},{5,4},{6,7},{7,6},{8,9},{9,8},{10,11... | collective-permute-start | bytes 737288 | tf_op jit(solution)/shard_map/ppermute | solution.py:88
  81.6 4.1 %collective-permute-start.20 = (bf16[3,320,128]{2,1,0:T(8,128)(2,1)S(1)}, bf16[3,320,128]{2,1,0:T(8,128)(2,1)S(1)}, u32[]{:S(2)}, u32[]{:S(2)}) collective-permute-start(bf16[3,320,128]{2,1,0:T(8,128)(2,1)S(1)} %get-tuple-element.32.refs_0_), channel_id=1, source_target_pairs={{0,1},{1,0},{2,3},{3,2},{4,5},{5,4},{6,7},{7,6},{8,9},{9,8},{10,11... | collective-permute-start | bytes 737288 | tf_op jit(solution)/shard_map/ppermute | solution.py:88
  82.0 3.6 %collective-permute-start.21 = (bf16[3,320,128]{2,1,0:T(8,128)(2,1)S(1)}, bf16[3,320,128]{2,1,0:T(8,128)(2,1)S(1)}, u32[]{:S(2)}, u32[]{:S(2)}) collective-permute-start(bf16[3,320,128]{2,1,0:T(8,128)(2,1)S(1)} %get-tuple-element.33.refs_1_), channel_id=1, source_target_pairs={{0,1},{1,0},{2,3},{3,2},{4,5},{5,4},{6,7},{7,6},{8,9},{9,8},{10,11... | collective-permute-start | bytes 737288 | tf_op jit(solution)/shard_map/ppermute | solution.py:88
  82.1 3.5 %collective-permute-start.22 = (bf16[3,320,128]{2,1,0:T(8,128)(2,1)S(1)}, bf16[3,320,128]{2,1,0:T(8,128)(2,1)S(1)}, u32[]{:S(2)}, u32[]{:S(2)}) collective-permute-start(bf16[3,320,128]{2,1,0:T(8,128)(2,1)S(1)} %get-tuple-element.34.refs_2_), channel_id=1, source_target_pairs={{0,1},{1,0},{2,3},{3,2},{4,5},{5,4},{6,7},{7,6},{8,9},{9,8},{10,11... | collective-permute-start | bytes 737288 | tf_op jit(solution)/shard_map/ppermute | solution.py:88
  83.5 16.5 %collective-permute-start.24 = (bf16[8,1,320,128]{3,2,1,0:T(8,128)(2,1)S(1)}, bf16[8,1,320,128]{3,2,1,0:T(8,128)(2,1)S(1)}, u32[]{:S(2)}, u32[]{:S(2)}) collective-permute-start(bf16[8,1,320,128]{3,2,1,0:T(8,128)(2,1)S(1)} %get-tuple-element.24), channel_id=1, source_target_pairs={{0,0},{1,2},{2,1},{3,4},{4,3},{5,6},{6,5},{7,8},{8,7},{9,10},{10,9... | collective-permute-start | bytes 1966088 | tf_op jit(solution)/shard_map/ppermute | solution.py:88
